TPU v7x, 128 devices: a whole 4x4x4 slice. The times are simulated.
128 devices in a mesh: dp: 16 (over y, x), tensor: 8 (over z, core).
Axes of the slice: x: 4, y: 4, z: 4, core: 2. Of those that a mesh axis runs over, the one named last changes fastest.
Arguments:
- old_master: float32 [128, 672, 128], P(('dp', 'tensor')), may hold values from -6 to 6
- old_avg: float32 [128, 672, 128], P(('dp', 'tensor')), may hold values from -1.8 to 1.8
- old_sq: float32 [128, 672, 128], P(('dp', 'tensor')), may hold values from 0.001 to 1
- grad: float32 [128, 672, 128], P(('dp', 'tensor')), may hold values from -6 to 6
- old_table: int32 [128, 3], replicated, may hold values from 0 to 10751, as said below
- new_table: int32 [128, 3], replicated, may hold values from 0 to 5375, as said below
- head_order: int32 [112], replicated, may hold values from 0 to 111, each once
Outputs:
- new_master: float32 [128, 672, 128], P(('dp', 'tensor'))
- new_avg: float32 [128, 672, 128], P(('dp', 'tensor'))
- new_sq: float32 [128, 672, 128], P(('dp', 'tensor'))
- params: bfloat16 [128, 43008], P(None, 'tensor')
Inputs may be any that keep to these rules, and one draw needn't show every extreme that they name: `old_table`: row k belongs to old rank k // 32; the fragments of one old rank follow one another in k without gaps and cover its 10752 units; every length is 1 to 672, in each old rank one length is exactly 672, and the last fragment of each old rank has length 1. `new_table`: row k = d * 8 + n belongs to new rank n; for one new rank the ranges follow one another in d without gaps and cover its 5376 units; range d lies within units d * 336 to (d + 3) * 336 - 1; every length is 1 to 672, in each new rank one length is exactly 672 and that range reaches unit (d + 2) * 336 or beyond, and the last range of each new rank has length 1.
All inputs are finite; a program needn't handle non-finite values.
Results may differ from a plain program's by a relative error of at most 0.0033.
Values may be sent and summed in bfloat16 or wider, within the bound.
No kernel may reach another device: no remote copies, remote signals or barrier semaphores. Data moves between devices by JAX's collectives and lax.ppermute only.
A program may use at most 128 MiB of HBM per device.

v0:
```python
import jax
import jax.numpy as jnp
from jax import lax
from jax.sharding import PartitionSpec as P

OLD_TP = 4
STEPS_DONE = 10


beta_first = 0.9
beta_second = 0.95
learn_rate = 0.1
decay_rate = 0.1
epsilon_add = 1e-08


def shifted(shard, axis, by):
    peers = lax.axis_size(axis)
    pairs = [(i, i + by) for i in range(peers) if 0 <= i + by < peers]
    return lax.ppermute(shard, axis, pairs)


def adam_update(master, moment, square, gradient):
    moment_new = beta_first * moment + (1.0 - beta_first) * gradient
    square_new = beta_second * square + (1.0 - beta_second) * gradient * gradient
    moment_hat = moment_new / (1.0 - beta_first**STEPS_DONE)
    square_hat = square_new / (1.0 - beta_second**STEPS_DONE)
    master_new = master - learn_rate * (
        moment_hat / (jnp.sqrt(square_hat) + epsilon_add) + decay_rate * master
    )
    return (master_new, moment_new, square_new)


def pick_units(source, wanted, begin_at, count_of):
    offset = wanted - begin_at
    inside = (offset >= 0) & (offset < count_of)
    safe_index = jnp.clip(offset, 0, source.shape[0] - 1)
    return jnp.where(inside[..., None], source[safe_index], jnp.zeros((), source.dtype))


def owner_slice(whole, begin_at, count_of, slot_size):
    padded = jnp.concatenate([whole, jnp.zeros((slot_size, whole.shape[1]), whole.dtype)], axis=0)
    window = lax.dynamic_slice_in_dim(padded, begin_at, slot_size, 0)
    inside = jnp.arange(slot_size, dtype=jnp.int32) < count_of
    return jnp.where(inside[:, None], window, jnp.zeros((), whole.dtype))


def on_device(old_master, old_avg, old_sq, grad, old_table, new_table, head_order):
    slot_size = old_master.shape[1]
    head_dim = old_master.shape[2]
    head_count = head_order.shape[0]
    dp_count = lax.axis_size("dp")
    tp_count = lax.axis_size("tensor")
    all_count = dp_count * tp_count
    dp_index = lax.axis_index("dp")
    tp_index = lax.axis_index("tensor")
    dev_index = dp_index * tp_count + tp_index
    unit_dev = slot_size // 2
    heads_old = head_count // OLD_TP
    heads_new = head_count // tp_count
    new_units = 3 * heads_new
    rows_dev = unit_dev // (3 * head_count)
    block_units = rows_dev * 3 * heads_old
    old_states = (old_master[0], old_avg[0], old_sq[0])
    frag_start = old_table[dev_index, 1]
    frag_length = old_table[dev_index, 2]
    within = jnp.arange(block_units, dtype=jnp.int32)
    target = jnp.arange(all_count, dtype=jnp.int32)[:, None] * block_units + within[None, :]
    sending = tuple((pick_units(single, target, frag_start, frag_length) for single in old_states))
    arrived = lax.all_to_all(sending, ("dp", "tensor"), split_axis=0, concat_axis=0, tiled=True)
    canonical = tuple(
        (
            single.reshape(OLD_TP, all_count // OLD_TP, block_units, head_dim).sum(axis=1)
            for single in arrived
        )
    )
    order_table = head_order.reshape(tp_count, heads_new)

    def regroup(single):
        weight = single.reshape(OLD_TP, rows_dev, heads_old, 3, head_dim).transpose(1, 0, 2, 3, 4)
        weight = weight.reshape(rows_dev, head_count, 3, head_dim)
        return weight[:, order_table].transpose(1, 0, 3, 2, 4)

    regrouped = tuple((regroup(single) for single in canonical))
    landed = lax.all_to_all(regrouped, "tensor", split_axis=0, concat_axis=0, tiled=True)
    blocks = tuple((single.reshape(unit_dev, head_dim) for single in landed))
    new_start = new_table[dev_index, 1]
    new_length = new_table[dev_index, 2]
    gradient = grad[0]
    stacked = jnp.stack(blocks, axis=0)
    nearby = [stacked]
    for distance in (1, 2):
        nearby.append(shifted(stacked, "dp", -distance))
    joined = jnp.concatenate(nearby, axis=1)
    local_start = new_start - dp_index * unit_dev
    mine = tuple(
        (owner_slice(joined[which], local_start, new_length, slot_size) for which in range(3))
    )
    master_new, moment_new, square_new = adam_update(mine[0], mine[1], mine[2], gradient)
    inside = (jnp.arange(slot_size, dtype=jnp.int32) < new_length)[:, None]
    master_new = jnp.where(inside, master_new, 0.0)
    moment_new = jnp.where(inside, moment_new, 0.0)
    square_new = jnp.where(inside, square_new, 0.0)
    pieces = lax.all_gather(master_new.astype(jnp.bfloat16), "dp", axis=0, tiled=True)
    starts_all = new_table.reshape(dp_count, tp_count, 3)[:, tp_index, 1]
    flat_place = jnp.arange(dp_count * unit_dev, dtype=jnp.int32)
    owner = jnp.sum((flat_place[:, None] >= starts_all[None, :]).astype(jnp.int32), axis=1) - 1
    source_index = owner * slot_size + flat_place - starts_all[owner]
    params_flat = pieces[source_index]
    params = params_flat.reshape(-1, new_units * head_dim)
    return (master_new[None], moment_new[None], square_new[None], params)


def solution(mesh):
    in_specs = (
        P(("dp", "tensor"), None, None),
        P(("dp", "tensor"), None, None),
        P(("dp", "tensor"), None, None),
        P(("dp", "tensor"), None, None),
        P(),
        P(),
        P(),
    )
    out_specs = (
        P(("dp", "tensor"), None, None),
        P(("dp", "tensor"), None, None),
        P(("dp", "tensor"), None, None),
        P(None, "tensor"),
    )
    return jax.shard_map(
        on_device, mesh=mesh, in_specs=in_specs, out_specs=out_specs, check_vma=False
    )
```

profile of v0, /device:TPU:0, one launch (start us, length us, event | category | flops | bytes accessed | tf_op | source)
XLA Modules:
  0.0 457.3 jit_solution(10279314720494581328)
XLA Ops:
  9.5 20.5 %gather_fusion = f32[10752,128]{1,0:T(8,128)} fusion(f32[672,128]{1,0:T(8,128)S(1)} %bitcast.81, s32[11264]{0:T(1024)S(1)} %pad_clamp_fusion), kind=kCustom, calls=%fused_computation | custom fusion | bytes 11053056 | tf_op jit(solution)/shard_map/gather | solution.py:38
  29.9 6.8 %reshape.187 = f32[128,84,128]{2,1,0:T(8,128)} reshape(f32[10752,128]{1,0:T(8,128)} %gather_fusion) | data formatting | bytes 11010048 | tf_op jit(solution)/shard_map/gather | solution.py:38
  38.1 20.5 %gather_fusion.2 = f32[10752,128]{1,0:T(8,128)} fusion(f32[672,128]{1,0:T(8,128)S(1)} %bitcast.82, s32[11264]{0:T(1024)S(1)} %pad_clamp_fusion), kind=kCustom, calls=%fused_computation.2 | custom fusion | bytes 11053056 | tf_op jit(solution)/shard_map/gather | solution.py:38
  58.6 6.7 %reshape.205 = f32[128,84,128]{2,1,0:T(8,128)} reshape(f32[10752,128]{1,0:T(8,128)} %gather_fusion.2) | data formatting | bytes 11010048 | tf_op jit(solution)/shard_map/gather | solution.py:38
  65.3 20.5 %gather_fusion.4 = f32[10752,128]{1,0:T(8,128)} fusion(f32[672,128]{1,0:T(8,128)S(1)} %bitcast.83, s32[11264]{0:T(1024)S(1)} %pad_clamp_fusion), kind=kCustom, calls=%fused_computation.4 | custom fusion | bytes 11053056 | tf_op jit(solution)/shard_map/gather | solution.py:38
  85.8 6.7 %reshape.223 = f32[128,84,128]{2,1,0:T(8,128)} reshape(f32[10752,128]{1,0:T(8,128)} %gather_fusion.4) | data formatting | bytes 11010048 | tf_op jit(solution)/shard_map/gather | solution.py:38
  92.5 10.2 %broadcast_select_fusion.2 = (f32[128,84,128]{2,1,0:T(8,128)}, f32[128,84,128]{2,1,0:T(8,128)S(1)}, f32[128,84,128]{2,1,0:T(8,128)S(1)}) fusion(f32[128,84,128]{2,1,0:T(8,128)} %reshape.187, pred[128,84]{1,0:T(8,128)(4,1)S(1)} %fusion.9, f32[128,84,128]{2,1,0:T(8,128)} %reshape.205, f32[128,84,128]{2,1,0:T(8,128)} %reshape.223), kind=kLoop, calls=%fused_computation.12 | loop fusion | flops 4128768 | bytes 33040896 | tf_op jit(solution)/shard_map/jit(_where)/select_n | solution.py:38
  102.6 80.8 %all_to_all.30 = f32[128,84,128]{2,1,0:T(8,128)} all-to-all(f32[128,84,128]{2,1,0:T(8,128)S(1)} %get-tuple-element.42), channel_id=1, replica_groups=mesh['dp'=16,'tensor'=8] {'dp','tensor'}, dimensions={0} | all-to-all | bytes 11010048 | tf_op jit(solution)/shard_map/all_to_all | solution.py:70
  183.5 74.5 %all_to_all.31 = f32[128,84,128]{2,1,0:T(8,128)} all-to-all(f32[128,84,128]{2,1,0:T(8,128)S(1)} %get-tuple-element.41), channel_id=1, replica_groups=mesh['dp'=16,'tensor'=8] {'dp','tensor'}, dimensions={0} | all-to-all | bytes 11010048 | tf_op jit(solution)/shard_map/all_to_all | solution.py:70
  258.0 5.9 %all-to-all-start = ((f32[128,84,128]{2,1,0:T(8,128)}), f32[128,84,128]{2,1,0:T(8,128)}, u32[]{:S(2)}, u32[]{:S(2)}) async-start(f32[128,84,128]{2,1,0:T(8,128)} %get-tuple-element.40), calls=%async_computation | async-start | bytes 11534336 | tf_op jit(solution)/shard_map/all_to_all | solution.py:70
  264.1 2.9 bitcast_reduce_fusion
  268.7 64.9 %all-to-all-done = f32[128,84,128]{2,1,0:T(8,128)} async-done(((f32[128,84,128]{2,1,0:T(8,128)}), f32[128,84,128]{2,1,0:T(8,128)}, u32[]{:S(2)}, u32[]{:S(2)}) %all-to-all-start) | async-done | bytes 5505056 | tf_op jit(solution)/shard_map/all_to_all | solution.py:70
  333.7 3.4 all-to-all-start.5
  337.1 2.9 bitcast_reduce_fusion.1
  343.7 3.4 all-to-all-start.3
  347.1 2.9 bitcast_reduce_fusion.2
  351.1 2.5 all-to-all-done.3
  353.6 9.0 %all_to_all.32 = f32[8,1,3,14,128]{4,1,3,2,0:T(1,128)S(1)} all-to-all(f32[8,1,3,14,128]{4,1,3,2,0:T(1,128)S(1)} %copy.40), channel_id=1, replica_groups=mesh['dp'=16,'tensor'=8] {'tensor'}, dimensions={0} | all-to-all | bytes 344064 | tf_op jit(solution)/shard_map/all_to_all | solution.py:85
  366.5 12.7 %collective-permute-done.1 = f32[3,336,128]{2,1,0:T(8,128)S(1)} collective-permute-done((f32[3,336,128]{2,1,0:T(8,128)S(1)}, f32[3,336,128]{2,1,0:T(8,128)S(1)}, u32[]{:S(2)}, u32[]{:S(2)}) %collective-permute-start.1) | collective-permute-done | bytes 516128 | tf_op jit(solution)/shard_map/ppermute | solution.py:20
  382.2 4.3 fusion.10
  387.1 5.5 %select_select_fusion = s32[5376]{0:T(1024)S(1)} fusion(pred[5376]{0:T(1024)(128)(4,1)S(1)} %get-tuple-element.12, pred[5376]{0:T(1024)(128)(4,1)S(1)} %get-tuple-element.11, pred[5376]{0:T(1024)(128)(4,1)S(1)} %get-tuple-element.10, pred[5376]{0:T(1024)(128)(4,1)S(1)} %get-tuple-element.9, pred[5376]{0:T(1024)(128)(4,1)S(1)} %get-tuple-element.8, ...), kind=kLoop, calls=%fused_computation.62 | loop fusion | flops 48384 | bytes 91428 | tf_op jit(solution)/shard_map/gather | solution.py:108
  392.8 44.4 %all-gather.2.cloned.1.call-done = bf16[10752,128]{1,0:T(8,128)(2,1)} async-done(((bf16[672,128]{1,0:T(8,128)(2,1)}), bf16[10752,128]{1,0:T(8,128)(2,1)}) %all-gather.2.cloned.1.call-update) | async-done | bytes 2752528 | tf_op jit(solution)/shard_map/all_gather | solution.py:104
  437.2 10.8 %gather_fusion.6 = bf16[5376,128]{1,0:T(8,128)(2,1)S(1)} fusion(bf16[10752,128]{1,0:T(8,128)(2,1)} %all-gather.2.cloned.1.call-done, s32[6144]{0:T(1024)S(1)} %pad_clamp_fusion.1), kind=kCustom, calls=%fused_computation.6 | custom fusion | bytes 2774016 | tf_op jit(solution)/shard_map/gather | solution.py:109
  448.0 2.4 reshape.185
  (55 shorter events, 17.0 us)
Async XLA Ops:
  7.2 2.3 copy-start
  29.9 8.2 %copy-start.2 = (f32[1,672,128]{2,1,0:T(8,128)S(1)}, f32[1,672,128]{2,1,0:T(8,128)}, u32[]{:S(2)}) copy-start(f32[1,672,128]{2,1,0:T(8,128)} %param.8) | copy-start | bytes 1032196
  58.6 6.7 %copy-start.3 = (f32[1,672,128]{2,1,0:T(8,128)S(1)}, f32[1,672,128]{2,1,0:T(8,128)}, u32[]{:S(2)}) copy-start(f32[1,672,128]{2,1,0:T(8,128)} %param.9) | copy-start | bytes 1032196
  258.0 6.0 %copy-start.6 = (s32[112]{0:T(128)S(1)}, s32[112]{0:T(128)}, u32[]{:S(2)}) copy-start(s32[112]{0:T(128)} %param.13) | copy-start | bytes 1348
  258.0 75.7 %all-to-all-start = ((f32[128,84,128]{2,1,0:T(8,128)}), f32[128,84,128]{2,1,0:T(8,128)}, u32[]{:S(2)}, u32[]{:S(2)}) async-start(f32[128,84,128]{2,1,0:T(8,128)} %get-tuple-element.40), calls=%async_computation | async-start | bytes 11534336 | tf_op jit(solution)/shard_map/all_to_all | solution.py:70
  333.7 10.0 %all-to-all-start.5 = ((f32[8,1,3,14,128]{4,1,3,2,0:T(1,128)}), f32[8,1,3,14,128]{4,1,3,2,0:T(1,128)S(1)}, u32[]{:S(2)}, u32[]{:S(2)}) async-start(f32[8,1,3,14,128]{4,1,3,2,0:T(1,128)} %copy.44), calls=%async_computation.5 | async-start | bytes 344064 | tf_op jit(solution)/shard_map/all_to_all | solution.py:85
  343.7 9.9 %all-to-all-start.3 = ((f32[8,1,3,14,128]{4,1,3,2,0:T(1,128)}), f32[8,1,3,14,128]{4,1,3,2,0:T(1,128)S(1)}, u32[]{:S(2)}, u32[]{:S(2)}) async-start(f32[8,1,3,14,128]{4,1,3,2,0:T(1,128)} %copy.42), calls=%async_computation.3 | async-start | bytes 344064 | tf_op jit(solution)/shard_map/all_to_all | solution.py:85
  347.1 90.1 %all-gather.2.cloned.1.call-start = ((), (), s32[]{:S(2)}) async-start(), calls=%async_computation.6 | async-start | bytes 2924544 | tf_op jit(solution)/shard_map/all_gather | solution.py:104
  350.0 29.4 %copy-start.4 = (f32[1,672,128]{2,1,0:T(8,128)S(1)}, f32[1,672,128]{2,1,0:T(8,128)}, u32[]{:S(2)}) copy-start(f32[1,672,128]{2,1,0:T(8,128)} %param.10) | copy-start | bytes 1032196
  350.9 30.1 %copy-start.5 = (s32[128,3]{0,1:T(4,128)S(1)}, s32[128,3]{0,1:T(4,128)}, u32[]{:S(2)}) copy-start(s32[128,3]{0,1:T(4,128)} %param.12) | copy-start | bytes 4612
  362.6 16.6 %collective-permute-start.1 = (f32[3,336,128]{2,1,0:T(8,128)S(1)}, f32[3,336,128]{2,1,0:T(8,128)S(1)}, u32[]{:S(2)}, u32[]{:S(2)}) collective-permute-start(f32[3,336,128]{2,1,0:T(8,128)S(1)} %pad_maximum_fusion.1), channel_id=1, source_target_pairs={{16,0},{24,8},{32,16},{40,24},{48,32},{56,40},{64,48},{72,56},{80,... | collective-permute-start | bytes 1548296 | tf_op jit(solution)/shard_map/ppermute | solution.py:20
  363.9 15.3 %collective-permute-start = (f32[3,336,128]{2,1,0:T(8,128)S(1)}, f32[3,336,128]{2,1,0:T(8,128)S(1)}, u32[]{:S(2)}, u32[]{:S(2)}) collective-permute-start(f32[3,336,128]{2,1,0:T(8,128)S(1)} %pad_maximum_fusion.1), channel_id=1, source_target_pairs={{8,0},{16,8},{24,16},{32,24},{40,32},{48,40},{56,48},{64,56},{72,6... | collective-permute-start | bytes 1548296 | tf_op jit(solution)/shard_map/ppermute | solution.py:20
  392.7 57.7 %copy-start.1 = (f32[1,672,128]{2,1,0:T(8,128)S(1)}, f32[1,672,128]{2,1,0:T(8,128)}, u32[]{:S(2)}) copy-start(f32[1,672,128]{2,1,0:T(8,128)} %param.7) | copy-start | bytes 1032196
Sparse Core Ops, SparseCore 0:
  381.1 56.0 all-gather.1
where the time goes:
time: 459 us; the launch traced here: 457 us
  blocking collectives  164 us (36%)
  waiting for transfers between devices  127 us (28%)
  local copies, waits for them, and re-layouts  102 us (22%)
  other arithmetic  34 us (7%)
  starting transfers between devices  15.4 us (3%)
  between operations  15 us (3%)
    all_to_all x2, blocking collectives, on_device(): lax.all_to_all(sending, ('dp', 'tensor'), split_axis=0, concat_axis=0, ti...  155 us
    gather x6, local copies, waits for them, and re-layouts, pick_units(): source[safe_index]  81.6 us
    all_to_all x1, waiting for transfers between devices, on_device(): lax.all_to_all(sending, ('dp', 'tensor'), split_axis=0, concat_axis=0, ti...  64.9 us
    all_gather x1, waiting for transfers between devices, on_device(): lax.all_gather(master_new.astype(jnp.bfloat16), 'dp', axis=0, tiled=True)  44.4 us
    ppermute x2, waiting for transfers between devices, shifted(): return lax.ppermute(shard, axis, pairs)  12.7 us
    gather x1, local copies, waits for them, and re-layouts, on_device(): params_flat = pieces[source_index]  10.8 us
    gather x3, other arithmetic, on_device(): source_index = owner * slot_size + flat_place - starts_all[owner]  10.4 us
    select_n x1, other arithmetic, pick_units(): jnp.where(inside[..., None], source[safe_index], jnp.zeros((), source.dty...  10.2 us
  transfers between devices with their start and end apart: 6, of which 5 were waited for; matrix products, arithmetic and copies ran while one was open for 6% of the time, Pallas kernels for 0%

commit v1 on v0

v1 whole, which is shorter than its diff:
```python
import functools
import jax
import jax.numpy as jnp
from jax import lax
from jax.experimental import pallas as pl
from jax.experimental.pallas import tpu as pltpu
from jax.sharding import Mesh, PartitionSpec as P

OLD_TP = 4
STEPS_DONE = 10
SLOT = 672
UNIT = 336
LANES = 128
ROW_OLD = 84
QUART = 21
QPAD = 24
ROW_NEW = 42
RPAD = 48

beta_first = 0.9
beta_second = 0.95
learn_rate = 0.1
decay_rate = 0.1
epsilon_add = 1e-08

SCALE_W = 2.0**13
SCALE_M = 2.0**15
SCALE_V = 2.0**15
SCALE_G = 2.0**13


def adam_update(master, moment, square, gradient):
    moment_new = beta_first * moment + (1.0 - beta_first) * gradient
    square_new = beta_second * square + (1.0 - beta_second) * gradient * gradient
    moment_hat = moment_new / (1.0 - beta_first**STEPS_DONE)
    square_hat = square_new / (1.0 - beta_second**STEPS_DONE)
    master_new = master - learn_rate * (
        moment_hat / (jnp.sqrt(square_hat) + epsilon_add) + decay_rate * master
    )
    return (master_new, moment_new, square_new)


def wrap(value):
    return jnp.where(value < 0, value + SLOT, value)


def pack_kernel(place, w_ref, m_ref, v_ref, g_ref, out_ref, gout_ref, scratch):
    for s, ref in enumerate((w_ref, m_ref, v_ref, g_ref)):
        scratch[s, pl.ds(0, SLOT), :] = ref[0]
        scratch[s, pl.ds(SLOT, RPAD), :] = ref[0, pl.ds(0, RPAD), :]
    scales = (SCALE_W, SCALE_M, SCALE_V)
    for hq in range(4):
        for t in range(8):
            offset = wrap(t * ROW_OLD + hq * QUART - place[0])
            for s in range(3):
                piece = scratch[s, pl.ds(offset, QPAD), :]
                out_ref[hq * 8 + t, :, pl.ds(s * LANES, LANES)] = piece * scales[s]
    for half in range(2):
        for t in range(8):
            offset = wrap(half * UNIT + t * ROW_NEW - place[1])
            gout_ref[half, t] = scratch[3, pl.ds(offset, RPAD), :] * SCALE_G


def owner_kernel(place, near_ref, mid_ref, g_ref, w_out, m_out, v_out, scratch):
    for half, ref in enumerate((near_ref, mid_ref)):
        for t in range(8):
            for s in range(3):
                piece = ref[t, pl.ds(0, ROW_NEW), pl.ds(s * LANES, LANES)]
                at = half * UNIT + t * ROW_NEW
                scratch[s, pl.ds(at, ROW_NEW), :] = piece
                scratch[s, pl.ds(at + SLOT, ROW_NEW), :] = piece
    step = 96
    for c in range(SLOT // step):
        at = place[1] + c * step
        w = scratch[0, pl.ds(at, step), :] * (1.0 / SCALE_W)
        m = scratch[1, pl.ds(at, step), :] * (1.0 / SCALE_M)
        v = scratch[2, pl.ds(at, step), :] * (1.0 / SCALE_V)
        rows = pl.ds(c * step, step)
        slot = lax.broadcasted_iota(jnp.int32, (step, LANES), 0) + c * step
        inside = slot < place[2]
        new = adam_update(w, m, v, g_ref[0, rows, :])
        for ref, value in zip((w_out, m_out, v_out), new):
            ref[0, rows, :] = jnp.where(inside, value, 0.0)


def one_hot_dot(chosen, source):
    picked = jnp.dot(
        chosen.astype(jnp.float32),
        source.astype(jnp.float32),
        precision=lax.Precision.HIGH,
        preferred_element_type=jnp.float32,
    )
    return picked.astype(jnp.float16)


def on_device(old_master, old_avg, old_sq, grad, old_table, new_table, head_order):
    y = lax.axis_index("y")
    x = lax.axis_index("x")
    t = lax.axis_index("tensor")
    dp = y * 4 + x
    dev = dp * 8 + t
    f16 = jnp.float16

    new_start = new_table[dev, 1]
    new_length = new_table[dev, 2]
    place = jnp.stack(
        [
            old_table[dev, 1] % SLOT,
            (new_start - dp * UNIT) % SLOT,
            new_length,
        ]
    ).astype(jnp.int32)

    vmem = pl.BlockSpec(memory_space=pltpu.VMEM)
    smem = pl.BlockSpec(memory_space=pltpu.SMEM)
    packed, grad_rows = pl.pallas_call(
        pack_kernel,
        out_shape=(
            jax.ShapeDtypeStruct((32, QPAD, 3 * LANES), jnp.float32),
            jax.ShapeDtypeStruct((2, 8, RPAD, LANES), jnp.float32),
        ),
        in_specs=[smem, vmem, vmem, vmem, vmem],
        out_specs=(vmem, vmem),
        scratch_shapes=[pltpu.VMEM((4, SLOT + RPAD, LANES), jnp.float32)],
        compiler_params=pltpu.CompilerParams(vmem_limit_bytes=24 * 1024 * 1024),
    )(place, old_master, old_avg, old_sq, grad)

    grad_send = grad_rows.astype(f16)
    up = lambda by: [(i, i + by) for i in range(16 - by)]
    down = lambda by: [(i + by, i) for i in range(16 - by)]
    grad_one = lax.ppermute(grad_send[1], ("y", "x"), up(1))
    grad_two = lax.ppermute(grad_send[0], ("y", "x"), up(2))

    first = lax.all_to_all(packed.astype(f16), ("x", "tensor"), 0, 0, tiled=True)
    ranks = lax.dynamic_slice_in_dim(old_table, y * 32, 32, 0)
    begin = jnp.broadcast_to(ranks[:, 1:2], (32, QPAD)).reshape(1, 32 * QPAD)
    end = begin + jnp.broadcast_to(ranks[:, 2:3], (32, QPAD)).reshape(1, 32 * QPAD)
    row_id = lax.broadcasted_iota(jnp.int32, (16 * QPAD, 32 * QPAD), 0)
    col_id = lax.broadcasted_iota(jnp.int32, (16 * QPAD, 32 * QPAD), 1)
    j = row_id % QPAD
    flat = ((row_id // QPAD) * 8 + t) * ROW_OLD + x * QUART + j
    chosen = (j == col_id % QPAD) & (j < QUART) & (flat >= begin) & (flat < end)
    rows = one_hot_dot(chosen, first.reshape(32 * QPAD, 3 * LANES))

    second = lax.all_to_all(
        rows.reshape(16, QPAD, 3 * LANES), ("y", "x"), 0, 0, tiled=True
    )
    order = head_order.reshape(8, 1, 14)
    comp = jnp.arange(3, dtype=jnp.int32).reshape(1, 3, 1)
    origin = (order // 7) * QPAD + (order % 7) * 3 + comp
    origin = jnp.pad(origin.reshape(8, ROW_NEW), ((0, 0), (0, RPAD - ROW_NEW)))
    origin = origin.reshape(8 * RPAD, 1)
    col_id = lax.broadcasted_iota(jnp.int32, (8 * RPAD, 16 * QPAD), 1)
    heads = one_hot_dot(origin == col_id, second.reshape(16 * QPAD, 3 * LANES))

    block = lax.all_to_all(heads.reshape(8, RPAD, 3 * LANES), "tensor", 0, 0, tiled=True)
    block_one = lax.ppermute(block, ("y", "x"), down(1))
    block_two = lax.ppermute(block, ("y", "x"), down(2))

    own = lax.broadcasted_iota(jnp.int32, (8, RPAD, 1), 0) * ROW_NEW
    own = own + lax.broadcasted_iota(jnp.int32, (8, RPAD, 1), 1) + dp * UNIT
    start_below = new_table[jnp.maximum(dp - 1, 0) * 8 + t, 1]
    gradient = jnp.where(
        own >= new_start,
        grad_send[0].astype(jnp.float32),
        jnp.where(
            own >= start_below, grad_one.astype(jnp.float32), grad_two.astype(jnp.float32)
        ),
    ) * (1.0 / SCALE_G)
    wide = block.astype(jnp.float32)
    master, _, _ = adam_update(
        wide[:, :, :LANES] * (1.0 / SCALE_W),
        wide[:, :, LANES : 2 * LANES] * (1.0 / SCALE_M),
        wide[:, :, 2 * LANES :] * (1.0 / SCALE_V),
        gradient,
    )
    mine = master[:, :ROW_NEW].astype(jnp.bfloat16).reshape(8, ROW_NEW * LANES)
    params = lax.all_to_all(
        jnp.broadcast_to(mine[None], (16, 8, ROW_NEW * LANES)), ("y", "x"), 0, 0, tiled=True
    ).reshape(128, ROW_NEW * LANES)

    near = jnp.where(own >= new_start, block, block_two).astype(jnp.float32)
    outs = pl.pallas_call(
        owner_kernel,
        out_shape=(jax.ShapeDtypeStruct((1, SLOT, LANES), jnp.float32),) * 3,
        in_specs=[smem, vmem, vmem, vmem],
        out_specs=(vmem, vmem, vmem),
        scratch_shapes=[pltpu.VMEM((3, 2 * SLOT, LANES), jnp.float32)],
        compiler_params=pltpu.CompilerParams(vmem_limit_bytes=24 * 1024 * 1024),
    )(place, near, block_one.astype(jnp.float32), grad)
    return (*outs, params)


def solution(mesh):
    fine = Mesh(mesh.devices.reshape(4, 4, 8), ("y", "x", "tensor"))
    parts = P(("y", "x", "tensor"), None, None)
    return jax.shard_map(
        on_device,
        mesh=fine,
        in_specs=(parts, parts, parts, parts, P(), P(), P()),
        out_specs=(parts, parts, parts, P(None, "tensor")),
        check_vma=False,
    )
```

time: 459 us -> 106 us (0.23)
  blocking collectives: 164 us -> 0 us
  local copies, waits for them, and re-layouts: 102 us -> 7.13 us
  waiting for transfers between devices: 127 us -> 52.2 us
  other arithmetic: 34 us -> 5 us
  starting transfers between devices: 15.4 us -> 30.2 us
  between operations: 15 us -> 4.16 us
    all_to_all x3 -> x0, blocking collectives: 164 us -> none  [the longest x2 155 us: on_device(): lax.all_to_all(sending, ('dp', 'tensor'), split_axis=0, concat_axis=0, ti...]
    gather x14 -> x0, local copies, waits for them, and re-layouts: 95.5 us -> none  [the longest x6 81.6 us: pick_units(): source[safe_index]]
    all_to_all x3 -> x4, waiting for transfers between devices: 69.4 us -> 22.2 us  [the longest x1 11 us: on_device(): lax.all_to_all(packed.astype(f16), ('x', 'tensor'), 0, 0, tiled=True)]
    all_gather x1 -> x0, waiting for transfers between devices: 44.4 us -> none  [on_device(): lax.all_gather(master_new.astype(jnp.bfloat16), 'dp', axis=0, tiled=True)]
    ppermute x2 -> x4, waiting for transfers between devices: 12.7 us -> 30 us  [the longest x1 20.9 us: on_device(): block_one = lax.ppermute(block, ('y', 'x'), down(1))]
    select_n x4 -> x0, other arithmetic: 11 us -> none  [the longest x1 10.2 us: pick_units(): jnp.where(inside[..., None], source[safe_index], jnp.zeros((), source.dty...]
    gather x6 -> x0, other arithmetic: 10.4 us -> none  [the longest x3 10.4 us: on_device(): source_index = owner * slot_size + flat_place - starts_all[owner]]
    all_to_all x3 -> x4, starting transfers between devices: 12.8 us -> 21.7 us  [the longest x1 8.25 us: on_device(): lax.all_to_all(packed.astype(f16), ('x', 'tensor'), 0, 0, tiled=True)]
  transfers between devices with their start and end apart: 6 -> 8, of which waited for: 5 -> 5; matrix products, arithmetic and copies ran while one was open for 6% -> 2% of each run, Pallas kernels for 0% -> 2%
where the time goes in v1:
time: 106 us; the launch traced here: 105 us
  waiting for transfers between devices  52.2 us (49%)
  starting transfers between devices  30.2 us (28%)
  local copies, waits for them, and re-layouts  7.13 us (7%)
  other arithmetic  5 us (5%)
  between operations  4.16 us (4%)
  matrix products  3.35 us (3%)
  Pallas kernels  2.72 us (3%)
    ppermute x1, waiting for transfers between devices, on_device(): block_one = lax.ppermute(block, ('y', 'x'), down(1))  20.9 us
    all_to_all x1, waiting for transfers between devices, on_device(): lax.all_to_all(packed.astype(f16), ('x', 'tensor'), 0, 0, tiled=True)  11 us
    all_to_all x1, waiting for transfers between devices, on_device(): lax.all_to_all(rows.reshape(16, QPAD, 3 * LANES), ('y', 'x'), 0, 0, tiled...  9.33 us
    ppermute x1, waiting for transfers between devices, on_device(): block_two = lax.ppermute(block, ('y', 'x'), down(2))  9.06 us
    all_to_all x1, starting transfers between devices, on_device(): lax.all_to_all(packed.astype(f16), ('x', 'tensor'), 0, 0, tiled=True)  8.25 us
    all_to_all x1, starting transfers between devices, on_device(): lax.all_to_all(rows.reshape(16, QPAD, 3 * LANES), ('y', 'x'), 0, 0, tiled...  5.77 us
    unnamed x16, local copies, waits for them, and re-layouts  5.03 us
    all_to_all x1, starting transfers between devices, on_device(): lax.all_to_all(jnp.broadcast_to(mine[None], (16, 8, ROW_NEW * LANES)), ('...  4.28 us
  transfers between devices with their start and end apart: 8, of which 5 were waited for; matrix products, arithmetic and copies ran while one was open for 2% of the time, Pallas kernels for 2%

profile of v1, /device:TPU:0, one launch (start us, length us, event | category | flops | bytes accessed | tf_op | source)
XLA Modules:
  0.0 104.7 jit_solution(15027630675855224549)
XLA Ops:
  0.6 1.4 %constant_dynamic-slice_fusion = (s32[1,1]{0,1:T(1,128)}, s32[1,1]{0,1:T(1,128)}, s32[1,1]{0,1:T(1,128)}, s32[1,1]{0,1:T(1,128)}) fusion(s32[128,3]{0,1:T(4,128)} %param.12, s32[]{:T(128)S(6)} %select_n.81, s32[]{:T(128)S(6)} %select_n.71, s32[128,3]{0,1:T(4,128)} %param.11), kind=kLoop, calls=%fused_computation.71 | loop fusion | flops 1 | bytes 40 | tf_op jit(solution)/shard_map/dynamic_slice | solution.py:162
  6.0 1.0 copy-done
  7.0 1.0 copy-done.2
  8.0 1.0 copy-done.3
  9.0 1.0 copy-done.4
  11.6 8.2 %all-to-all-start = ((f16[32,24,384]{2,1,0:T(8,128)(2,1)}), f16[32,24,384]{2,1,0:T(8,128)(2,1)S(1)}, u32[]{:S(2)}, u32[]{:S(2)}) async-start(f16[32,24,384]{2,1,0:T(8,128)(2,1)} %convert_element_type.35), calls=%async_computation | async-start | bytes 1179648 | tf_op jit(solution)/shard_map/all_to_all | solution.py:134
  20.6 11.0 %all-to-all-done = f16[32,24,384]{2,1,0:T(8,128)(2,1)S(1)} async-done(((f16[32,24,384]{2,1,0:T(8,128)(2,1)}), f16[32,24,384]{2,1,0:T(8,128)(2,1)S(1)}, u32[]{:S(2)}, u32[]{:S(2)}) %all-to-all-start) | async-done | bytes 589856 | tf_op jit(solution)/shard_map/all_to_all | solution.py:134
  31.7 2.1 %convolution_convert_fusion.1 = f16[384,384]{1,0:T(8,128)(2,1)} fusion(f16[768,384]{1,0:T(8,128)(2,1)S(1)} %bitcast.31, s32[768]{0:T(1024)S(1)} %add.178, s32[768]{0:T(1024)S(1)} %ge.36, s32[]{:T(128)S(6)} %mul.113, s32[]{:T(128)S(6)} %axis_index.38, s32[384]{0:T(512)S(1)} %get-tuple-element.33, s32[384]{0:T(512)S(1)} %get-tuple-element.36, ...), kind=kOutput, calls=%fused_computation.4 | convolution fusion | flops 231063552 | bytes 904712 | tf_op jit(solution)/shard_map/dot_general | solution.py:87
  33.8 5.8 %all-to-all-start.1 = ((f16[16,24,384]{2,1,0:T(8,128)(2,1)}), f16[16,24,384]{2,1,0:T(8,128)(2,1)S(1)}, u32[]{:S(2)}, u32[]{:S(2)}) async-start(f16[16,24,384]{2,1,0:T(8,128)(2,1)} %bitcast.8), calls=%async_computation.1 | async-start | bytes 589824 | tf_op jit(solution)/shard_map/all_to_all | solution.py:145
  39.8 9.3 %all-to-all-done.1 = f16[16,24,384]{2,1,0:T(8,128)(2,1)S(1)} async-done(((f16[16,24,384]{2,1,0:T(8,128)(2,1)}), f16[16,24,384]{2,1,0:T(8,128)(2,1)S(1)}, u32[]{:S(2)}, u32[]{:S(2)}) %all-to-all-start.1) | async-done | bytes 294944 | tf_op jit(solution)/shard_map/all_to_all | solution.py:145
  49.2 1.3 %convolution_convert_fusion = f16[384,384]{1,0:T(8,128)(2,1)} fusion(f16[384,384]{1,0:T(8,128)(2,1)S(1)} %bitcast.33, s32[384]{0:T(512)S(1)} %eq.21), kind=kOutput, calls=%fused_computation.3 | convolution fusion | flops 113541120 | bytes 591360 | tf_op jit(solution)/shard_map/dot_general | solution.py:87
  50.4 3.4 %all-to-all-start.2 = ((f16[8,48,384]{2,1,0:T(8,128)(2,1)}), f16[8,48,384]{2,1,0:T(8,128)(2,1)S(1)}, u32[]{:S(2)}, u32[]{:S(2)}) async-start(f16[8,48,384]{2,1,0:T(8,128)(2,1)} %bitcast.10), calls=%async_computation.2 | async-start | bytes 589824 | tf_op jit(solution)/shard_map/all_to_all | solution.py:156
  54.0 2.5 %collective-permute-start.2 = (f16[8,48,128]{2,1,0:T(8,128)(2,1)S(1)}, f16[8,48,128]{2,1,0:T(8,128)(2,1)S(1)}, u32[]{:S(2)}, u32[]{:S(2)}) collective-permute-start(f16[8,48,128]{2,1,0:T(8,128)(2,1)S(1)} %get-tuple-element.19), channel_id=1, source_target_pairs={{0,8},{8,16},{16,24},{24,32},{32,40},{40,48},{48,56},{56,64},{64,7... | collective-permute-start | bytes 294920 | tf_op jit(solution)/shard_map/ppermute | solution.py:131
  56.4 3.4 %collective-permute-start.3 = (f16[8,48,128]{2,1,0:T(8,128)(2,1)S(1)}, f16[8,48,128]{2,1,0:T(8,128)(2,1)S(1)}, u32[]{:S(2)}, u32[]{:S(2)}) collective-permute-start(f16[8,48,128]{2,1,0:T(8,128)(2,1)S(1)} %get-tuple-element.20), channel_id=1, source_target_pairs={{0,16},{8,24},{16,32},{24,40},{32,48},{40,56},{48,64},{56,72},{64,... | collective-permute-start | bytes 294920 | tf_op jit(solution)/shard_map/ppermute | solution.py:132
  59.8 1.8 %all-to-all-done.2 = f16[8,48,384]{2,1,0:T(8,128)(2,1)S(1)} async-done(((f16[8,48,384]{2,1,0:T(8,128)(2,1)}), f16[8,48,384]{2,1,0:T(8,128)(2,1)S(1)}, u32[]{:S(2)}, u32[]{:S(2)}) %all-to-all-start.2) | async-done | bytes 294944 | tf_op jit(solution)/shard_map/all_to_all | solution.py:156
  61.7 1.3 %collective-permute-start = (f16[8,48,384]{2,1,0:T(8,128)(2,1)S(1)}, f16[8,48,384]{2,1,0:T(8,128)(2,1)S(1)}, u32[]{:S(2)}, u32[]{:S(2)}) collective-permute-start(f16[8,48,384]{2,1,0:T(8,128)(2,1)S(1)} %all-to-all-done.2), channel_id=1, source_target_pairs={{16,0},{24,8},{32,16},{40,24},{48,32},{56,40},{64,48},{72,56},{80,... | collective-permute-start | bytes 884744 | tf_op jit(solution)/shard_map/ppermute | solution.py:158
  63.0 1.4 %fusion.41 = (pred[8,48]{1,0:T(8,128)(4,1)S(1)}, pred[8,48]{1,0:T(8,128)(4,1)S(1)}) fusion(s32[]{:T(128)} %bitcast.12, s32[]{:T(128)S(6)} %mul.102, s32[8]{0:T(128)S(1)} %iota_multiply_fusion, s32[]{:T(128)} %bitcast.2), kind=kLoop, calls=%fused_computation.57 | loop fusion | flops 1536 | bytes 812 | tf_op jit(solution)/shard_map/ge | solution.py:167
  64.3 9.1 %collective-permute-done = f16[8,48,384]{2,1,0:T(8,128)(2,1)S(1)} collective-permute-done((f16[8,48,384]{2,1,0:T(8,128)(2,1)S(1)}, f16[8,48,384]{2,1,0:T(8,128)(2,1)S(1)}, u32[]{:S(2)}, u32[]{:S(2)}) %collective-permute-start) | collective-permute-done | bytes 294944 | tf_op jit(solution)/shard_map/ppermute | solution.py:158
  73.9 1.2 %broadcast_in_dim.50 = bf16[16,8,5376]{2,1,0:T(8,128)(2,1)} broadcast(bf16[8,5376]{1,0:T(8,128)(2,1)S(1)} %bitcast.32), dimensions={1,2} | broadcast | bytes 1462272 | tf_op jit(solution)/shard_map/broadcast_in_dim | solution.py:179
  75.1 4.3 %all-to-all-start.3 = ((bf16[16,8,5376]{2,1,0:T(8,128)(2,1)}), bf16[16,8,5376]{2,1,0:T(8,128)(2,1)S(1)}, u32[]{:S(2)}, u32[]{:S(2)}) async-start(bf16[16,8,5376]{2,1,0:T(8,128)(2,1)} %broadcast_in_dim.50), calls=%async_computation.3 | async-start | bytes 2752512 | tf_op jit(solution)/shard_map/all_to_all | solution.py:178
  79.4 1.3 %collective-permute-start.1 = (f16[8,48,384]{2,1,0:T(8,128)(2,1)S(1)}, f16[8,48,384]{2,1,0:T(8,128)(2,1)S(1)}, u32[]{:S(2)}, u32[]{:S(2)}) collective-permute-start(f16[8,48,384]{2,1,0:T(8,128)(2,1)S(1)} %all-to-all-done.2), channel_id=1, source_target_pairs={{8,0},{16,8},{24,16},{32,24},{40,32},{48,40},{56,48},{64,56},{72,6... | collective-permute-start | bytes 884744 | tf_op jit(solution)/shard_map/ppermute | solution.py:157
  80.7 20.9 %collective-permute-done.1 = f16[8,48,384]{2,1,0:T(8,128)(2,1)S(1)} collective-permute-done((f16[8,48,384]{2,1,0:T(8,128)(2,1)S(1)}, f16[8,48,384]{2,1,0:T(8,128)(2,1)S(1)}, u32[]{:S(2)}, u32[]{:S(2)}) %collective-permute-start.1) | collective-permute-done | bytes 294944 | tf_op jit(solution)/shard_map/ppermute | solution.py:157
  101.7 2.0 %shard_map.103 = (f32[1,672,128]{2,1,0:T(8,128)}, f32[1,672,128]{2,1,0:T(8,128)}, f32[1,672,128]{2,1,0:T(8,128)}) custom-call(s32[3]{0:T(128)S(1)} %pad_add_fusion.place, f32[8,48,384]{2,1,0:T(8,128)S(1)} %get-tuple-element.18.near_ref, f32[8,48,384]{2,1,0:T(8,128)S(1)} %convert_element_type.39.mid_ref, f32[1,672,128]{2,1,0:T(8,128)S(1)} %copy-done.1), custom_call_target="tpu_custom_call" | custom-call | tf_op jit(solution)/shard_map/pallas_call | solution.py:183
  103.6 1.1 %copy.15 = bf16[128,5376]{1,0:T(8,128)(2,1)} copy(bf16[128,5376]{1,0:T(8,128)(2,1)S(1)} %bitcast.30) | data formatting | bytes 2752512
  (49 shorter events, 4.0 us)
Async XLA Ops:
  6.0 1.0 copy-start
  7.0 1.0 copy-start.2
  8.0 1.0 copy-start.3
  9.0 1.0 copy-start.4
  10.7 9.2 %copy-start.5 = (s32[128,3]{0,1:T(4,128)S(1)}, s32[128,3]{0,1:T(4,128)}, u32[]{:S(2)}) copy-start(s32[128,3]{0,1:T(4,128)} %param.11) | copy-start | bytes 4612
  10.7 9.3 %copy-start.6 = (s32[112]{0:T(128)S(1)}, s32[112]{0:T(128)}, u32[]{:S(2)}) copy-start(s32[112]{0:T(128)} %param.13) | copy-start | bytes 1348
  11.6 20.1 %all-to-all-start = ((f16[32,24,384]{2,1,0:T(8,128)(2,1)}), f16[32,24,384]{2,1,0:T(8,128)(2,1)S(1)}, u32[]{:S(2)}, u32[]{:S(2)}) async-start(f16[32,24,384]{2,1,0:T(8,128)(2,1)} %convert_element_type.35), calls=%async_computation | async-start | bytes 1179648 | tf_op jit(solution)/shard_map/all_to_all | solution.py:134
  33.8 15.4 %all-to-all-start.1 = ((f16[16,24,384]{2,1,0:T(8,128)(2,1)}), f16[16,24,384]{2,1,0:T(8,128)(2,1)S(1)}, u32[]{:S(2)}, u32[]{:S(2)}) async-start(f16[16,24,384]{2,1,0:T(8,128)(2,1)} %bitcast.8), calls=%async_computation.1 | async-start | bytes 589824 | tf_op jit(solution)/shard_map/all_to_all | solution.py:145
  50.4 11.2 %all-to-all-start.2 = ((f16[8,48,384]{2,1,0:T(8,128)(2,1)}), f16[8,48,384]{2,1,0:T(8,128)(2,1)S(1)}, u32[]{:S(2)}, u32[]{:S(2)}) async-start(f16[8,48,384]{2,1,0:T(8,128)(2,1)} %bitcast.10), calls=%async_computation.2 | async-start | bytes 589824 | tf_op jit(solution)/shard_map/all_to_all | solution.py:156
  54.0 19.6 %collective-permute-start.2 = (f16[8,48,128]{2,1,0:T(8,128)(2,1)S(1)}, f16[8,48,128]{2,1,0:T(8,128)(2,1)S(1)}, u32[]{:S(2)}, u32[]{:S(2)}) collective-permute-start(f16[8,48,128]{2,1,0:T(8,128)(2,1)S(1)} %get-tuple-element.19), channel_id=1, source_target_pairs={{0,8},{8,16},{16,24},{24,32},{32,40},{40,48},{48,56},{56,64},{64,7... | collective-permute-start | bytes 294920 | tf_op jit(solution)/shard_map/ppermute | solution.py:131
  56.4 17.1 %collective-permute-start.3 = (f16[8,48,128]{2,1,0:T(8,128)(2,1)S(1)}, f16[8,48,128]{2,1,0:T(8,128)(2,1)S(1)}, u32[]{:S(2)}, u32[]{:S(2)}) collective-permute-start(f16[8,48,128]{2,1,0:T(8,128)(2,1)S(1)} %get-tuple-element.20), channel_id=1, source_target_pairs={{0,16},{8,24},{16,32},{24,40},{32,48},{40,56},{48,64},{56,72},{64,... | collective-permute-start | bytes 294920 | tf_op jit(solution)/shard_map/ppermute | solution.py:132
  61.7 11.7 %collective-permute-start = (f16[8,48,384]{2,1,0:T(8,128)(2,1)S(1)}, f16[8,48,384]{2,1,0:T(8,128)(2,1)S(1)}, u32[]{:S(2)}, u32[]{:S(2)}) collective-permute-start(f16[8,48,384]{2,1,0:T(8,128)(2,1)S(1)} %all-to-all-done.2), channel_id=1, source_target_pairs={{16,0},{24,8},{32,16},{40,24},{48,32},{56,40},{64,48},{72,56},{80,... | collective-permute-start | bytes 884744 | tf_op jit(solution)/shard_map/ppermute | solution.py:158
  75.1 26.6 %copy-start.1 = (f32[1,672,128]{2,1,0:T(8,128)S(1)}, f32[1,672,128]{2,1,0:T(8,128)}, u32[]{:S(2)}) copy-start(f32[1,672,128]{2,1,0:T(8,128)} %g_ref.3) | copy-start | bytes 1032196
  75.1 28.5 %all-to-all-start.3 = ((bf16[16,8,5376]{2,1,0:T(8,128)(2,1)}), bf16[16,8,5376]{2,1,0:T(8,128)(2,1)S(1)}, u32[]{:S(2)}, u32[]{:S(2)}) async-start(bf16[16,8,5376]{2,1,0:T(8,128)(2,1)} %broadcast_in_dim.50), calls=%async_computation.3 | async-start | bytes 2752512 | tf_op jit(solution)/shard_map/all_to_all | solution.py:178
  79.4 22.2 %collective-permute-start.1 = (f16[8,48,384]{2,1,0:T(8,128)(2,1)S(1)}, f16[8,48,384]{2,1,0:T(8,128)(2,1)S(1)}, u32[]{:S(2)}, u32[]{:S(2)}) collective-permute-start(f16[8,48,384]{2,1,0:T(8,128)(2,1)S(1)} %all-to-all-done.2), channel_id=1, source_target_pairs={{8,0},{16,8},{24,16},{32,24},{40,32},{48,40},{56,48},{64,56},{72,6... | collective-permute-start | bytes 884744 | tf_op jit(solution)/shard_map/ppermute | solution.py:157

commit v2 on v1

v2 whole, which is shorter than its diff:
```python
import functools
import jax
import jax.numpy as jnp
from jax import lax
from jax.experimental import pallas as pl
from jax.experimental.pallas import tpu as pltpu
from jax.sharding import Mesh, PartitionSpec as P

OLD_TP = 4
STEPS_DONE = 10
SLOT = 672
UNIT = 336
LANES = 128
ROW_OLD = 84
QUART = 21
QPAD = 24
ROW_NEW = 42
RPAD = 48

beta_first = 0.9
beta_second = 0.95
learn_rate = 0.1
decay_rate = 0.1
epsilon_add = 1e-08

SCALE_W = 2.0**13
SCALE_M = 2.0**15
SCALE_V = 2.0**15
SCALE_G = 2.0**13


def adam_update(master, moment, square, gradient):
    moment_new = beta_first * moment + (1.0 - beta_first) * gradient
    square_new = beta_second * square + (1.0 - beta_second) * gradient * gradient
    moment_hat = moment_new / (1.0 - beta_first**STEPS_DONE)
    square_hat = square_new / (1.0 - beta_second**STEPS_DONE)
    master_new = master - learn_rate * (
        moment_hat / (jnp.sqrt(square_hat) + epsilon_add) + decay_rate * master
    )
    return (master_new, moment_new, square_new)


def wrap(value):
    return jnp.where(value < 0, value + SLOT, value)


def pack_kernel(
    old_hbm, new_hbm, w_ref, m_ref, v_ref, g_ref, out_ref, gout_ref, info_ref,
    scratch, old_ref, new_ref, sems,
):
    tables = [
        pltpu.make_async_copy(old_hbm, old_ref, sems.at[4]),
        pltpu.make_async_copy(new_hbm, new_ref, sems.at[5]),
    ]
    for copy in tables:
        copy.start()
    copies = [
        pltpu.make_async_copy(ref.at[0], scratch.at[s, pl.ds(0, SLOT)], sems.at[s])
        for s, ref in enumerate((g_ref, w_ref, m_ref, v_ref))
    ]
    for copy in copies:
        copy.start()
    for copy in tables:
        copy.wait()
    dp = lax.axis_index("y") * 4 + lax.axis_index("x")
    tp = lax.axis_index("tensor")
    old_start = lax.rem(old_ref[1, dp * 8 + tp], SLOT)
    new_start = new_ref[1, dp * 8 + tp]
    new_place = lax.rem(new_start - dp * UNIT, SLOT)
    above = lax.rem(dp + 1, 16)
    info_ref[0] = jnp.full((8, LANES), new_start, jnp.int32)
    info_ref[1] = jnp.full((8, LANES), new_ref[1, above * 8 + tp], jnp.int32)
    for s, copy in enumerate(copies):
        copy.wait()
        scratch[s, pl.ds(SLOT, RPAD), :] = scratch[s, pl.ds(0, RPAD), :]
        if s == 0:
            for half in range(2):
                for t in range(8):
                    offset = wrap(half * UNIT + t * ROW_NEW - new_place)
                    gout_ref[half, t] = scratch[0, pl.ds(offset, RPAD), :] * SCALE_G
            continue
        scale = (SCALE_W, SCALE_M, SCALE_V)[s - 1]
        for hq in range(4):
            for t in range(8):
                offset = wrap(t * ROW_OLD + hq * QUART - old_start)
                piece = scratch[s, pl.ds(offset, QPAD), :]
                out_ref[hq * 8 + t, :, pl.ds((s - 1) * LANES, LANES)] = piece * scale


def owner_kernel(new_ref, ends_ref, mid_ref, g_ref, w_out, m_out, v_out, scratch):
    dp = lax.axis_index("y") * 4 + lax.axis_index("x")
    tp = lax.axis_index("tensor")
    new_place = lax.rem(new_ref[1, dp * 8 + tp] - dp * UNIT, SLOT)
    length = new_ref[2, dp * 8 + tp]
    for half, ref in enumerate((ends_ref, mid_ref)):
        for t in range(8):
            for s in range(3):
                piece = ref[t, pl.ds(0, ROW_NEW), pl.ds(s * LANES, LANES)]
                at = half * UNIT + t * ROW_NEW
                scratch[s, pl.ds(at, ROW_NEW), :] = piece
                scratch[s, pl.ds(at + SLOT, ROW_NEW), :] = piece
    step = 96
    for c in range(SLOT // step):
        at = new_place + c * step
        w = scratch[0, pl.ds(at, step), :] * (1.0 / SCALE_W)
        m = scratch[1, pl.ds(at, step), :] * (1.0 / SCALE_M)
        v = scratch[2, pl.ds(at, step), :] * (1.0 / SCALE_V)
        rows = pl.ds(c * step, step)
        slot = lax.broadcasted_iota(jnp.int32, (step, LANES), 0) + c * step
        inside = slot < length
        new = adam_update(w, m, v, g_ref[0, rows, :])
        for ref, value in zip((w_out, m_out, v_out), new):
            ref[0, rows, :] = jnp.where(inside, value, 0.0)


def one_hot_dot(chosen, source):
    picked = jnp.dot(
        chosen.astype(jnp.float32),
        source.astype(jnp.float32),
        precision=lax.Precision.HIGH,
        preferred_element_type=jnp.float32,
    )
    return picked.astype(jnp.float16)


def on_device(old_master, old_avg, old_sq, grad, old_table, new_table, head_order):
    y = lax.axis_index("y")
    x = lax.axis_index("x")
    t = lax.axis_index("tensor")
    dp = y * 4 + x
    f16 = jnp.float16

    vmem = pl.BlockSpec(memory_space=pltpu.VMEM)
    smem = pl.BlockSpec(memory_space=pltpu.SMEM)
    hbm = pl.BlockSpec(memory_space=pltpu.HBM)
    packed, grad_rows, info = pl.pallas_call(
        pack_kernel,
        out_shape=(
            pltpu.VMEM((32, QPAD, 3 * LANES), jnp.float32),
            pltpu.VMEM((2, 8, RPAD, LANES), jnp.float32),
            pltpu.VMEM((2, 8, LANES), jnp.int32),
        ),
        in_specs=[hbm] * 6,
        out_specs=(vmem, vmem, vmem),
        scratch_shapes=[
            pltpu.VMEM((4, SLOT + RPAD, LANES), jnp.float32),
            pltpu.SMEM((3, 128), jnp.int32),
            pltpu.SMEM((3, 128), jnp.int32),
            pltpu.SemaphoreType.DMA((6,)),
        ],
    )(old_table.T, new_table.T, old_master, old_avg, old_sq, grad)

    up = [(i, (i + 1) % 16) for i in range(16)]
    down = [(i, (i - 1) % 16) for i in range(16)]

    first = lax.all_to_all(packed.astype(f16), ("x", "tensor"), 0, 0, tiled=True)

    grad_rows, first = lax.optimization_barrier((grad_rows, first))
    grad_send = grad_rows.astype(f16)
    grad_first = lax.ppermute(grad_send[0], ("y", "x"), down)
    grad_last = lax.ppermute(grad_send[0], ("y", "x"), up)

    ranks = lax.dynamic_slice_in_dim(old_table, y * 32, 32, 0)
    begin = jnp.broadcast_to(ranks[:, 1:2], (32, QPAD)).reshape(1, 32 * QPAD)
    end = begin + jnp.broadcast_to(ranks[:, 2:3], (32, QPAD)).reshape(1, 32 * QPAD)
    row_id = lax.broadcasted_iota(jnp.int32, (16 * QPAD, 32 * QPAD), 0)
    col_id = lax.broadcasted_iota(jnp.int32, (16 * QPAD, 32 * QPAD), 1)
    j = row_id % QPAD
    flat = (((row_id // QPAD + 1) % 16) * 8 + t) * ROW_OLD + x * QUART + j
    chosen = (j == col_id % QPAD) & (j < QUART) & (flat >= begin) & (flat < end)
    chosen = lax.optimization_barrier(chosen.astype(jnp.bfloat16))
    rows = one_hot_dot(chosen, first.reshape(32 * QPAD, 3 * LANES))

    second = lax.all_to_all(
        rows.reshape(16, QPAD, 3 * LANES), ("y", "x"), 0, 0, tiled=True
    )
    order = head_order.reshape(8, 1, 14)
    comp = jnp.arange(3, dtype=jnp.int32).reshape(1, 3, 1)
    origin = (order // 7) * QPAD + (order % 7) * 3 + comp
    origin = jnp.pad(origin.reshape(8, ROW_NEW), ((0, 0), (0, RPAD - ROW_NEW)))
    origin = origin.reshape(8 * RPAD, 1)
    col_id = lax.broadcasted_iota(jnp.int32, (8 * RPAD, 16 * QPAD), 1)
    moved = lax.optimization_barrier((origin == col_id).astype(jnp.bfloat16))
    heads = one_hot_dot(moved, second.reshape(16 * QPAD, 3 * LANES))

    block = lax.all_to_all(heads.reshape(8, RPAD, 3 * LANES), "tensor", 0, 0, tiled=True)

    above = (dp + 1) % 16
    own = lax.broadcasted_iota(jnp.int32, (8, RPAD, LANES), 0) * ROW_NEW
    own = own + lax.broadcasted_iota(jnp.int32, (8, RPAD, LANES), 1)
    gradient = jnp.where(
        own >= info[1, 0] - above * UNIT,
        grad_first.astype(jnp.float32),
        jnp.where(
            own >= info[0, 0] - above * UNIT,
            grad_send[1].astype(jnp.float32),
            grad_last.astype(jnp.float32),
        ),
    ) * (1.0 / SCALE_G)
    wide = block.astype(jnp.float32)
    master, _, _ = adam_update(
        wide[:, :, :LANES] * (1.0 / SCALE_W),
        wide[:, :, LANES : 2 * LANES] * (1.0 / SCALE_M),
        wide[:, :, 2 * LANES :] * (1.0 / SCALE_V),
        gradient,
    )
    mine = master[:, :ROW_NEW].astype(jnp.bfloat16).reshape(8, ROW_NEW * LANES)
    mine = jnp.broadcast_to(mine[None], (16, 8, ROW_NEW * LANES))
    mine, block = lax.optimization_barrier((mine, block))
    spread = lax.all_to_all(mine, ("y", "x"), 0, 0, tiled=True)
    params = jnp.concatenate([spread[15:], spread[:15]]).reshape(128, ROW_NEW * LANES)

    block_near = lax.ppermute(block, ("y", "x"), up)
    block_far = lax.ppermute(block, ("y", "x"), down)
    own = jnp.concatenate([own] * 3, axis=2)
    near = own >= jnp.concatenate([info[0, 0]] * 3) - dp * UNIT
    ends = jnp.where(near, block_near, block_far).astype(jnp.float32)
    outs = pl.pallas_call(
        owner_kernel,
        out_shape=(jax.ShapeDtypeStruct((1, SLOT, LANES), jnp.float32),) * 3,
        in_specs=[smem, vmem, vmem, vmem],
        out_specs=(vmem, vmem, vmem),
        scratch_shapes=[pltpu.VMEM((3, 2 * SLOT, LANES), jnp.float32)],
        compiler_params=pltpu.CompilerParams(vmem_limit_bytes=24 * 1024 * 1024),
    )(new_table.T, ends, block.astype(jnp.float32), grad)
    return (*outs, params)


def solution(mesh):
    fine = Mesh(mesh.devices.reshape(4, 4, 8), ("y", "x", "tensor"))
    parts = P(("y", "x", "tensor"), None, None)
    return jax.shard_map(
        on_device,
        mesh=fine,
        in_specs=(parts, parts, parts, parts, P(), P(), P()),
        out_specs=(parts, parts, parts, P(None, "tensor")),
        check_vma=False,
    )
```

time: 106 us -> 91.9 us (0.87)
  waiting for transfers between devices: 52.2 us -> 43.4 us
  local copies, waits for them, and re-layouts: 7.13 us -> 2.22 us
  starting transfers between devices: 30.2 us -> 34.6 us
  between operations: 4.16 us -> 0.94 us
  other arithmetic: 5 us -> 3.55 us
    ppermute x4, waiting for transfers between devices: 30 us -> 21.6 us  [the longest x1 17.4 us: on_device(): block_far = lax.ppermute(block, ('y', 'x'), down)]
    unnamed x16 -> x9, local copies, waits for them, and re-layouts: 5.03 us -> 0.05 us
    ppermute x4, starting transfers between devices: 8.45 us -> 10.7 us  [the longest x1 5.25 us: on_device(): block_far = lax.ppermute(block, ('y', 'x'), down)]
    all_to_all x1, starting transfers between devices: 4.28 us -> 6.44 us  [on_device(): spread = lax.all_to_all(mine, ('y', 'x'), 0, 0, tiled=True)]
    dynamic_slice x1 -> x0, other arithmetic: 1.4 us -> none  [on_device(): start_below = new_table[jnp.maximum(dp - 1, 0) * 8 + t, 1]]
    ge x1 -> x0, other arithmetic: 1.37 us -> none  [on_device(): own >= start_below]
    reshape x0 -> x1, other arithmetic: none -> 1.2 us  [on_device(): jnp.concatenate([spread[15:], spread[:15]]).reshape(128, ROW_NEW * LANES)]
  transfers between devices with their start and end apart: 8 -> 8, of which waited for: 5 -> 6; matrix products, arithmetic and copies ran while one was open for 2% -> 2% of each run, Pallas kernels for 2% -> 2%
where the time goes in v2:
time: 91.9 us; the launch traced here: 90.8 us
  waiting for transfers between devices  43.4 us (47%)
  starting transfers between devices  34.6 us (38%)
  other arithmetic  3.55 us (4%)
  Pallas kernels  3.37 us (4%)
  matrix products  2.77 us (3%)
  local copies, waits for them, and re-layouts  2.22 us (2%)
  between operations  0.94 us (1%)
    ppermute x1, waiting for transfers between devices, on_device(): block_far = lax.ppermute(block, ('y', 'x'), down)  17.4 us
    all_to_all x1, waiting for transfers between devices, on_device(): lax.all_to_all(packed.astype(f16), ('x', 'tensor'), 0, 0, tiled=True)  10.1 us
    all_to_all x1, waiting for transfers between devices, on_device(): lax.all_to_all(rows.reshape(16, QPAD, 3 * LANES), ('y', 'x'), 0, 0, tiled...  9.43 us
    all_to_all x1, starting transfers between devices, on_device(): lax.all_to_all(packed.astype(f16), ('x', 'tensor'), 0, 0, tiled=True)  8.25 us
    all_to_all x1, starting transfers between devices, on_device(): spread = lax.all_to_all(mine, ('y', 'x'), 0, 0, tiled=True)  6.44 us
    all_to_all x1, starting transfers between devices, on_device(): lax.all_to_all(rows.reshape(16, QPAD, 3 * LANES), ('y', 'x'), 0, 0, tiled...  5.77 us
    ppermute x1, starting transfers between devices, on_device(): block_far = lax.ppermute(block, ('y', 'x'), down)  5.25 us
    ppermute x1, starting transfers between devices, on_device(): grad_first = lax.ppermute(grad_send[0], ('y', 'x'), down)  4.78 us
  transfers between devices with their start and end apart: 8, of which 6 were waited for; matrix products, arithmetic and copies ran while one was open for 2% of the time, Pallas kernels for 2%

profile of v2, /device:TPU:0, one launch (start us, length us, event | category | flops | bytes accessed | tf_op | source)
XLA Modules:
  0.0 90.8 jit_solution(13696300107173358926)
XLA Ops:
  0.6 1.4 %shard_map.102 = (f32[32,24,384]{2,1,0:T(8,128)S(1)}, f32[2,8,48,128]{3,2,1,0:T(8,128)S(1)}, s32[2,8,128]{2,1,0:T(8,128)S(1)}) custom-call(s32[3,128]{1,0:T(4,128)} %bitcast.43, s32[3,128]{1,0:T(4,128)} %bitcast.38, f32[1,672,128]{2,1,0:T(8,128)} %w_ref.1, f32[1,672,128]{2,1,0:T(8,128)} %m_ref.1, f32[1,672,128]{2,1,0:T(8,128)} %v_ref.1, f32[1,672,128]{2,1,0:T(8,128)} %g_ref.3), custom_call_target="tpu_custom_call" | custom-call | tf_op jit(solution)/shard_map/pallas_call | solution.py:136
  2.0 0.9 convert_element_type.46
  2.9 8.2 %all-to-all-start = ((f16[32,24,384]{2,1,0:T(8,128)(2,1)}), f16[32,24,384]{2,1,0:T(8,128)(2,1)S(1)}, u32[]{:S(2)}, u32[]{:S(2)}) async-start(f16[32,24,384]{2,1,0:T(8,128)(2,1)} %convert_element_type.46), calls=%async_computation | async-start | bytes 1179648 | tf_op jit(solution)/shard_map/all_to_all | solution.py:156
  12.0 0.1 reshape.128
  12.3 0.7 fusion.8
  12.9 10.1 %all-to-all-done = f16[32,24,384]{2,1,0:T(8,128)(2,1)S(1)} async-done(((f16[32,24,384]{2,1,0:T(8,128)(2,1)}), f16[32,24,384]{2,1,0:T(8,128)(2,1)S(1)}, u32[]{:S(2)}, u32[]{:S(2)}) %all-to-all-start) | async-done | bytes 589856 | tf_op jit(solution)/shard_map/all_to_all | solution.py:156
  23.0 1.5 %convolution_convert_fusion.1 = f16[384,384]{1,0:T(8,128)(2,1)} fusion(bf16[384,768]{1,0:T(8,128)(2,1)S(1)} %fusion.8, f16[768,384]{1,0:T(8,128)(2,1)S(1)} %bitcast.40), kind=kOutput, calls=%fused_computation.8 | convolution fusion | flops 226639872 | bytes 1474560 | tf_op jit(solution)/shard_map/dot_general | solution.py:117
  24.5 5.8 %all-to-all-start.1 = ((f16[16,24,384]{2,1,0:T(8,128)(2,1)}), f16[16,24,384]{2,1,0:T(8,128)(2,1)S(1)}, u32[]{:S(2)}, u32[]{:S(2)}) async-start(f16[16,24,384]{2,1,0:T(8,128)(2,1)} %bitcast.6), calls=%async_computation.1 | async-start | bytes 589824 | tf_op jit(solution)/shard_map/all_to_all | solution.py:174
  30.3 0.1 fusion.10
  30.5 9.4 %all-to-all-done.1 = f16[16,24,384]{2,1,0:T(8,128)(2,1)S(1)} async-done(((f16[16,24,384]{2,1,0:T(8,128)(2,1)}), f16[16,24,384]{2,1,0:T(8,128)(2,1)S(1)}, u32[]{:S(2)}, u32[]{:S(2)}) %all-to-all-start.1) | async-done | bytes 294944 | tf_op jit(solution)/shard_map/all_to_all | solution.py:174
  39.9 1.3 %convolution_convert_fusion = f16[384,384]{1,0:T(8,128)(2,1)} fusion(bf16[384,384]{1,0:T(8,128)(2,1)S(1)} %fusion.10, f16[384,384]{1,0:T(8,128)(2,1)S(1)} %bitcast.41), kind=kOutput, calls=%fused_computation.7 | convolution fusion | flops 113393664 | bytes 884736 | tf_op jit(solution)/shard_map/dot_general | solution.py:117
  41.2 3.4 %all-to-all-start.2 = ((f16[8,48,384]{2,1,0:T(8,128)(2,1)}), f16[8,48,384]{2,1,0:T(8,128)(2,1)S(1)}, u32[]{:S(2)}, u32[]{:S(2)}) async-start(f16[8,48,384]{2,1,0:T(8,128)(2,1)} %bitcast.8), calls=%async_computation.2 | async-start | bytes 589824 | tf_op jit(solution)/shard_map/all_to_all | solution.py:186
  44.6 0.6 collective-permute-start.1
  45.3 4.8 %collective-permute-start = (f16[8,48,128]{2,1,0:T(8,128)(2,1)S(1)}, f16[8,48,128]{2,1,0:T(8,128)(2,1)S(1)}, u32[]{:S(2)}, u32[]{:S(2)}) collective-permute-start(f16[8,48,128]{2,1,0:T(8,128)(2,1)S(1)} %slice_bitcast_fusion.1), channel_id=1, source_target_pairs={{0,120},{8,0},{16,8},{24,16},{32,24},{40,32},{48,40},{56,48},{64,5... | collective-permute-start | bytes 294920 | tf_op jit(solution)/shard_map/ppermute | solution.py:160
  50.1 2.4 %all-to-all-done.2 = f16[8,48,384]{2,1,0:T(8,128)(2,1)S(1)} async-done(((f16[8,48,384]{2,1,0:T(8,128)(2,1)}), f16[8,48,384]{2,1,0:T(8,128)(2,1)S(1)}, u32[]{:S(2)}, u32[]{:S(2)}) %all-to-all-start.2) | async-done | bytes 294944 | tf_op jit(solution)/shard_map/all_to_all | solution.py:186
  52.5 0.7 collective-permute-done.1
  53.2 0.2 fusion.19
  53.5 1.2 %broadcast_in_dim.29 = bf16[16,8,5376]{2,1,0:T(8,128)(2,1)} broadcast(bf16[8,5376]{1,0:T(8,128)(2,1)S(1)} %bitcast.42), dimensions={1,2} | broadcast | bytes 1462272 | tf_op jit(solution)/shard_map/broadcast_in_dim | solution.py:208
  54.7 6.4 %all-to-all-start.3 = ((bf16[16,8,5376]{2,1,0:T(8,128)(2,1)}), bf16[16,8,5376]{2,1,0:T(8,128)(2,1)S(1)}, u32[]{:S(2)}, u32[]{:S(2)}) async-start(bf16[16,8,5376]{2,1,0:T(8,128)(2,1)} %broadcast_in_dim.29), calls=%async_computation.3 | async-start | bytes 2752512 | tf_op jit(solution)/shard_map/all_to_all | solution.py:210
  61.1 5.2 %collective-permute-start.3 = (f16[8,48,384]{2,1,0:T(8,128)(2,1)S(1)}, f16[8,48,384]{2,1,0:T(8,128)(2,1)S(1)}, u32[]{:S(2)}, u32[]{:S(2)}) collective-permute-start(f16[8,48,384]{2,1,0:T(8,128)(2,1)S(1)} %all-to-all-done.2), channel_id=1, source_target_pairs={{0,120},{8,0},{16,8},{24,16},{32,24},{40,32},{48,40},{56,48},{64,5... | collective-permute-start | bytes 884744 | tf_op jit(solution)/shard_map/ppermute | solution.py:214
  66.6 17.4 %collective-permute-done.3 = f16[8,48,384]{2,1,0:T(8,128)(2,1)S(1)} collective-permute-done((f16[8,48,384]{2,1,0:T(8,128)(2,1)S(1)}, f16[8,48,384]{2,1,0:T(8,128)(2,1)S(1)}, u32[]{:S(2)}, u32[]{:S(2)}) %collective-permute-start.3) | collective-permute-done | bytes 294944 | tf_op jit(solution)/shard_map/ppermute | solution.py:214
  84.0 3.4 %collective-permute-done.2 = f16[8,48,384]{2,1,0:T(8,128)(2,1)S(1)} collective-permute-done((f16[8,48,384]{2,1,0:T(8,128)(2,1)S(1)}, f16[8,48,384]{2,1,0:T(8,128)(2,1)S(1)}, u32[]{:S(2)}, u32[]{:S(2)}) %collective-permute-start.2) | collective-permute-done | bytes 294944 | tf_op jit(solution)/shard_map/ppermute | solution.py:213
  87.5 2.0 %shard_map.103 = (f32[1,672,128]{2,1,0:T(8,128)}, f32[1,672,128]{2,1,0:T(8,128)}, f32[1,672,128]{2,1,0:T(8,128)}) custom-call(s32[3,128]{1,0:T(4,128)S(1)} %bitcast.39, f32[8,48,384]{2,1,0:T(8,128)S(1)} %fusion.11.ends_ref, f32[8,48,384]{2,1,0:T(8,128)S(1)} %convert_element_type.56.mid_ref, f32[1,672,128]{2,1,0:T(8,128)S(1)} %copy-done), custom_call_target="tpu_custom_call" | custom-call | tf_op jit(solution)/shard_map/pallas_call | solution.py:218
  89.6 1.2 %maximum_bitcast_fusion = bf16[128,5376]{1,0:T(8,128)(2,1)} fusion(bf16[15,8,5376]{2,1,0:T(8,128)(2,1)S(1)} %slice.60, bf16[1,8,5376]{2,1,0:T(8,128)(2,1)S(1)} %slice.59), kind=kLoop, calls=%fused_computation.6 | loop fusion | flops 688128 | bytes 2752512 | tf_op jit(solution)/shard_map/reshape | solution.py:211
  (48 shorter events, 1.4 us)
Async XLA Ops:
  2.0 9.2 %copy-start.3 = (s32[112]{0:T(128)S(1)}, s32[112]{0:T(128)}, u32[]{:S(2)}) copy-start(s32[112]{0:T(128)} %param.13) | copy-start | bytes 1348
  2.0 9.3 %copy-start.2 = (s32[128,3]{0,1:T(4,128)S(1)}, s32[128,3]{0,1:T(4,128)}, u32[]{:S(2)}) copy-start(s32[128,3]{0,1:T(4,128)} %param.11) | copy-start | bytes 4612
  2.9 20.1 %all-to-all-start = ((f16[32,24,384]{2,1,0:T(8,128)(2,1)}), f16[32,24,384]{2,1,0:T(8,128)(2,1)S(1)}, u32[]{:S(2)}, u32[]{:S(2)}) async-start(f16[32,24,384]{2,1,0:T(8,128)(2,1)} %convert_element_type.46), calls=%async_computation | async-start | bytes 1179648 | tf_op jit(solution)/shard_map/all_to_all | solution.py:156
  24.5 15.4 %all-to-all-start.1 = ((f16[16,24,384]{2,1,0:T(8,128)(2,1)}), f16[16,24,384]{2,1,0:T(8,128)(2,1)S(1)}, u32[]{:S(2)}, u32[]{:S(2)}) async-start(f16[16,24,384]{2,1,0:T(8,128)(2,1)} %bitcast.6), calls=%async_computation.1 | async-start | bytes 589824 | tf_op jit(solution)/shard_map/all_to_all | solution.py:174
  41.2 11.2 %all-to-all-start.2 = ((f16[8,48,384]{2,1,0:T(8,128)(2,1)}), f16[8,48,384]{2,1,0:T(8,128)(2,1)S(1)}, u32[]{:S(2)}, u32[]{:S(2)}) async-start(f16[8,48,384]{2,1,0:T(8,128)(2,1)} %bitcast.8), calls=%async_computation.2 | async-start | bytes 589824 | tf_op jit(solution)/shard_map/all_to_all | solution.py:186
  44.6 8.5 %collective-permute-start.1 = (f16[8,48,128]{2,1,0:T(8,128)(2,1)S(1)}, f16[8,48,128]{2,1,0:T(8,128)(2,1)S(1)}, u32[]{:S(2)}, u32[]{:S(2)}) collective-permute-start(f16[8,48,128]{2,1,0:T(8,128)(2,1)S(1)} %slice_bitcast_fusion.1), channel_id=1, source_target_pairs={{0,8},{8,16},{16,24},{24,32},{32,40},{40,48},{48,56},{56,64},{64,7... | collective-permute-start | bytes 294920 | tf_op jit(solution)/shard_map/ppermute | solution.py:161
  45.3 7.9 %collective-permute-start = (f16[8,48,128]{2,1,0:T(8,128)(2,1)S(1)}, f16[8,48,128]{2,1,0:T(8,128)(2,1)S(1)}, u32[]{:S(2)}, u32[]{:S(2)}) collective-permute-start(f16[8,48,128]{2,1,0:T(8,128)(2,1)S(1)} %slice_bitcast_fusion.1), channel_id=1, source_target_pairs={{0,120},{8,0},{16,8},{24,16},{32,24},{40,32},{48,40},{56,48},{64,5... | collective-permute-start | bytes 294920 | tf_op jit(solution)/shard_map/ppermute | solution.py:160
  54.7 34.8 %all-to-all-start.3 = ((bf16[16,8,5376]{2,1,0:T(8,128)(2,1)}), bf16[16,8,5376]{2,1,0:T(8,128)(2,1)S(1)}, u32[]{:S(2)}, u32[]{:S(2)}) async-start(bf16[16,8,5376]{2,1,0:T(8,128)(2,1)} %broadcast_in_dim.29), calls=%async_computation.3 | async-start | bytes 2752512 | tf_op jit(solution)/shard_map/all_to_all | solution.py:210
  61.1 22.8 %collective-permute-start.3 = (f16[8,48,384]{2,1,0:T(8,128)(2,1)S(1)}, f16[8,48,384]{2,1,0:T(8,128)(2,1)S(1)}, u32[]{:S(2)}, u32[]{:S(2)}) collective-permute-start(f16[8,48,384]{2,1,0:T(8,128)(2,1)S(1)} %all-to-all-done.2), channel_id=1, source_target_pairs={{0,120},{8,0},{16,8},{24,16},{32,24},{40,32},{48,40},{56,48},{64,5... | collective-permute-start | bytes 884744 | tf_op jit(solution)/shard_map/ppermute | solution.py:214
  66.4 21.0 %collective-permute-start.2 = (f16[8,48,384]{2,1,0:T(8,128)(2,1)S(1)}, f16[8,48,384]{2,1,0:T(8,128)(2,1)S(1)}, u32[]{:S(2)}, u32[]{:S(2)}) collective-permute-start(f16[8,48,384]{2,1,0:T(8,128)(2,1)S(1)} %all-to-all-done.2), channel_id=1, source_target_pairs={{0,8},{8,16},{16,24},{24,32},{32,40},{40,48},{48,56},{56,64},{64,7... | collective-permute-start | bytes 884744 | tf_op jit(solution)/shard_map/ppermute | solution.py:213
  66.5 21.0 %copy-start = (f32[1,672,128]{2,1,0:T(8,128)S(1)}, f32[1,672,128]{2,1,0:T(8,128)}, u32[]{:S(2)}) copy-start(f32[1,672,128]{2,1,0:T(8,128)} %g_ref.3) | copy-start | bytes 1032196
  66.5 21.0 %copy-start.1 = (s32[128,3]{0,1:T(4,128)S(1)}, s32[128,3]{0,1:T(4,128)}, u32[]{:S(2)}) copy-start(s32[128,3]{0,1:T(4,128)} %param.12) | copy-start | bytes 4612

commit v3 on v2

--- a/solution.py
+++ b/solution.py
@@ -16,6 +16,9 @@
 QPAD = 24
 ROW_NEW = 42
 RPAD = 48
+PAIR = 88
+HALF = ROW_NEW * LANES // 2
+TURNS = (0, 1, 3, 2)
 
 beta_first = 0.9
 beta_second = 0.95
@@ -68,8 +71,8 @@
     new_start = new_ref[1, dp * 8 + tp]
     new_place = lax.rem(new_start - dp * UNIT, SLOT)
     above = lax.rem(dp + 1, 16)
-    info_ref[0] = jnp.full((8, LANES), new_start, jnp.int32)
-    info_ref[1] = jnp.full((8, LANES), new_ref[1, above * 8 + tp], jnp.int32)
+    info_ref[0] = jnp.full((8, LANES), new_ref[1, above * 8 + tp] - above * UNIT, jnp.int32)
+    info_ref[1] = jnp.full((8, LANES), new_start - above * UNIT, jnp.int32)
     for s, copy in enumerate(copies):
         copy.wait()
         scratch[s, pl.ds(SLOT, RPAD), :] = scratch[s, pl.ds(0, RPAD), :]
@@ -87,15 +90,15 @@
                 out_ref[hq * 8 + t, :, pl.ds((s - 1) * LANES, LANES)] = piece * scale
 
 
-def owner_kernel(new_ref, ends_ref, mid_ref, g_ref, w_out, m_out, v_out, scratch):
+def owner_kernel(new_ref, rows_ref, g_ref, w_out, m_out, v_out, scratch):
     dp = lax.axis_index("y") * 4 + lax.axis_index("x")
     tp = lax.axis_index("tensor")
     new_place = lax.rem(new_ref[1, dp * 8 + tp] - dp * UNIT, SLOT)
     length = new_ref[2, dp * 8 + tp]
-    for half, ref in enumerate((ends_ref, mid_ref)):
+    for half in range(2):
         for t in range(8):
             for s in range(3):
-                piece = ref[t, pl.ds(0, ROW_NEW), pl.ds(s * LANES, LANES)]
+                piece = rows_ref[t, pl.ds((1 - half) * ROW_NEW, ROW_NEW), pl.ds(s * LANES, LANES)]
                 at = half * UNIT + t * ROW_NEW
                 scratch[s, pl.ds(at, ROW_NEW), :] = piece
                 scratch[s, pl.ds(at + SLOT, ROW_NEW), :] = piece
@@ -111,6 +114,19 @@
         new = adam_update(w, m, v, g_ref[0, rows, :])
         for ref, value in zip((w_out, m_out, v_out), new):
             ref[0, rows, :] = jnp.where(inside, value, 0.0)
+
+
+def place_kernel(*refs):
+    pieces, out_ref = refs[:8], refs[8]
+    y, x = lax.axis_index("y"), lax.axis_index("x")
+    for half in range(2):
+        for k in range(4):
+            for l in range(4):
+                dy, dx = (k, l) if half == 0 else (l, k)
+                from_y = lax.rem(y + 4 - TURNS[dy], 4)
+                from_x = lax.rem(x + 4 - TURNS[dx], 4)
+                block = lax.rem(from_y * 4 + from_x + 1, 16)
+                out_ref[block, :, pl.ds(half * HALF, HALF)] = pieces[half * 4 + k][l]
 
 
 def one_hot_dot(chosen, source):
@@ -163,41 +179,56 @@
     ranks = lax.dynamic_slice_in_dim(old_table, y * 32, 32, 0)
     begin = jnp.broadcast_to(ranks[:, 1:2], (32, QPAD)).reshape(1, 32 * QPAD)
     end = begin + jnp.broadcast_to(ranks[:, 2:3], (32, QPAD)).reshape(1, 32 * QPAD)
-    row_id = lax.broadcasted_iota(jnp.int32, (16 * QPAD, 32 * QPAD), 0)
-    col_id = lax.broadcasted_iota(jnp.int32, (16 * QPAD, 32 * QPAD), 1)
-    j = row_id % QPAD
-    flat = (((row_id // QPAD + 1) % 16) * 8 + t) * ROW_OLD + x * QUART + j
-    chosen = (j == col_id % QPAD) & (j < QUART) & (flat >= begin) & (flat < end)
+    heads_here = y * 28 + x * 7 + jnp.arange(7, dtype=jnp.int32)
+    at_head = head_order[None, :] == heads_here[:, None]
+    position = jnp.sum(jnp.where(at_head, jnp.arange(112, dtype=jnp.int32)[None, :], 0), axis=1)
+    rank_new, j_new = position // 14, position % 14
+    starts = new_table[:, 1].reshape(16, 1, 8)
+    at_rank = rank_new[None, :, None] == jnp.arange(8, dtype=jnp.int32)[None, None, :]
+    edge = jnp.sum(jnp.where(at_rank, starts, 0), axis=2)
+    e = jnp.arange(16, dtype=jnp.int32)
+    edge = edge - e[:, None] * UNIT - t * ROW_NEW - j_new[None, :]
+    near = 14 * jnp.arange(3, dtype=jnp.int32)[None, None, :] >= edge[:, :, None]
+    near = jnp.pad(near.reshape(16, QUART), ((0, 0), (0, QPAD - QUART)))
+    block_end = jnp.where(near, e[:, None], (e[:, None] + 2) % 16)
+    block_own = jnp.broadcast_to((e[:, None] + 1) % 16, (16, QPAD))
+    source = jnp.stack([block_own, block_end], axis=1)
+    j = jnp.arange(QPAD, dtype=jnp.int32)[None, None, :]
+    flat = (source * 8 + t) * ROW_OLD + x * QUART + j
+    flat = jnp.where(j < QUART, flat, -1).reshape(32 * QPAD, 1)
+    row_id = lax.broadcasted_iota(jnp.int32, (32 * QPAD, 32 * QPAD), 0)
+    col_id = lax.broadcasted_iota(jnp.int32, (32 * QPAD, 32 * QPAD), 1)
+    chosen = (row_id % QPAD == col_id % QPAD) & (flat >= begin) & (flat < end)
     chosen = lax.optimization_barrier(chosen.astype(jnp.bfloat16))
     rows = one_hot_dot(chosen, first.reshape(32 * QPAD, 3 * LANES))
 
     second = lax.all_to_all(
-        rows.reshape(16, QPAD, 3 * LANES), ("y", "x"), 0, 0, tiled=True
-    )
-    order = head_order.reshape(8, 1, 14)
-    comp = jnp.arange(3, dtype=jnp.int32).reshape(1, 3, 1)
-    origin = (order // 7) * QPAD + (order % 7) * 3 + comp
-    origin = jnp.pad(origin.reshape(8, ROW_NEW), ((0, 0), (0, RPAD - ROW_NEW)))
-    origin = origin.reshape(8 * RPAD, 1)
-    col_id = lax.broadcasted_iota(jnp.int32, (8 * RPAD, 16 * QPAD), 1)
+        rows.reshape(16, 2 * QPAD, 3 * LANES), ("y", "x"), 0, 0, tiled=True
+    )
+    order = head_order.reshape(8, 1, 1, 14)
+    kind = jnp.arange(2, dtype=jnp.int32).reshape(1, 2, 1, 1)
+    comp = jnp.arange(3, dtype=jnp.int32).reshape(1, 1, 3, 1)
+    origin = ((order // 7) * 2 + kind) * QPAD + (order % 7) * 3 + comp
+    origin = jnp.pad(origin.reshape(8, 2 * ROW_NEW), ((0, 0), (0, PAIR - 2 * ROW_NEW)))
+    origin = origin.reshape(8 * PAIR, 1)
+    col_id = lax.broadcasted_iota(jnp.int32, (8 * PAIR, 32 * QPAD), 1)
     moved = lax.optimization_barrier((origin == col_id).astype(jnp.bfloat16))
-    heads = one_hot_dot(moved, second.reshape(16 * QPAD, 3 * LANES))
-
-    block = lax.all_to_all(heads.reshape(8, RPAD, 3 * LANES), "tensor", 0, 0, tiled=True)
-
-    above = (dp + 1) % 16
+    heads = one_hot_dot(moved, second.reshape(32 * QPAD, 3 * LANES))
+
+    block = lax.all_to_all(heads.reshape(8, PAIR, 3 * LANES), "tensor", 0, 0, tiled=True)
+
     own = lax.broadcasted_iota(jnp.int32, (8, RPAD, LANES), 0) * ROW_NEW
     own = own + lax.broadcasted_iota(jnp.int32, (8, RPAD, LANES), 1)
     gradient = jnp.where(
-        own >= info[1, 0] - above * UNIT,
+        own >= info[0, 0],
         grad_first.astype(jnp.float32),
         jnp.where(
-            own >= info[0, 0] - above * UNIT,
+            own >= info[1, 0],
             grad_send[1].astype(jnp.float32),
             grad_last.astype(jnp.float32),
         ),
     ) * (1.0 / SCALE_G)
-    wide = block.astype(jnp.float32)
+    wide = block[:, :RPAD].astype(jnp.float32)
     master, _, _ = adam_update(
         wide[:, :, :LANES] * (1.0 / SCALE_W),
         wide[:, :, LANES : 2 * LANES] * (1.0 / SCALE_M),
@@ -205,24 +236,32 @@
         gradient,
     )
     mine = master[:, :ROW_NEW].astype(jnp.bfloat16).reshape(8, ROW_NEW * LANES)
-    mine = jnp.broadcast_to(mine[None], (16, 8, ROW_NEW * LANES))
-    mine, block = lax.optimization_barrier((mine, block))
-    spread = lax.all_to_all(mine, ("y", "x"), 0, 0, tiled=True)
-    params = jnp.concatenate([spread[15:], spread[:15]]).reshape(128, ROW_NEW * LANES)
-
-    block_near = lax.ppermute(block, ("y", "x"), up)
-    block_far = lax.ppermute(block, ("y", "x"), down)
-    own = jnp.concatenate([own] * 3, axis=2)
-    near = own >= jnp.concatenate([info[0, 0]] * 3) - dp * UNIT
-    ends = jnp.where(near, block_near, block_far).astype(jnp.float32)
+
+    def turn(value, axis):
+        return [value] + [
+            lax.ppermute(value, axis, [(i, (i + by) % 4) for i in range(4)])
+            for by in TURNS[1:]
+        ]
+
+    by_x = jnp.stack(turn(mine[:, :HALF], "x"))
+    by_y = jnp.stack(turn(mine[:, HALF:], "y"))
+    pieces = turn(by_x, "y") + turn(by_y, "x")
+    params = pl.pallas_call(
+        place_kernel,
+        out_shape=jax.ShapeDtypeStruct((16, 8, ROW_NEW * LANES), jnp.bfloat16),
+        in_specs=[vmem] * 8,
+        out_specs=vmem,
+        compiler_params=pltpu.CompilerParams(vmem_limit_bytes=16 * 1024 * 1024),
+    )(*pieces).reshape(128, ROW_NEW * LANES)
+
     outs = pl.pallas_call(
         owner_kernel,
         out_shape=(jax.ShapeDtypeStruct((1, SLOT, LANES), jnp.float32),) * 3,
-        in_specs=[smem, vmem, vmem, vmem],
+        in_specs=[smem, vmem, vmem],
         out_specs=(vmem, vmem, vmem),
         scratch_shapes=[pltpu.VMEM((3, 2 * SLOT, LANES), jnp.float32)],
         compiler_params=pltpu.CompilerParams(vmem_limit_bytes=24 * 1024 * 1024),
-    )(new_table.T, ends, block.astype(jnp.float32), grad)
+    )(new_table.T, block.astype(jnp.float32), grad)
     return (*outs, params)
 
 

time: 91.9 us -> 88.2 us (0.960)
  waiting for transfers between devices: 43.4 us -> 40.1 us
  starting transfers between devices: 34.6 us -> 32.9 us
  matrix products: 2.77 us -> 4.32 us
  Pallas kernels: 3.37 us -> 4.6 us
    ppermute x2 -> x12, waiting for transfers between devices: 20.9 us -> 10.8 us  [turn(): lax.ppermute(value, axis, [(i, (i + by) % 4) for i in range(4)])]
    all_to_all x3 -> x2, waiting for transfers between devices: 11.8 us -> 20.5 us  [the longest x1 12.3 us: on_device(): lax.all_to_all(rows.reshape(16, 2 * QPAD, 3 * LANES), ('y', 'x'), 0, 0, t...]
    ppermute x2 -> x12, starting transfers between devices: 5.25 us -> 13.2 us  [turn(): lax.ppermute(value, axis, [(i, (i + by) % 4) for i in range(4)])]
    all_to_all x3 -> x2, starting transfers between devices: 15.6 us -> 9.3 us  [the longest x1 5.77 us: on_device(): lax.all_to_all(rows.reshape(16, 2 * QPAD, 3 * LANES), ('y', 'x'), 0, 0, t...]
    ppermute x1, starting transfers between devices: 4.78 us -> 1.27 us  [on_device(): grad_first = lax.ppermute(grad_send[0], ('y', 'x'), down)]
    dot_general x2, matrix products: 2.77 us -> 4.32 us  [one_hot_dot(): jnp.dot(chosen.astype(jnp.float32), source.astype(jnp.float32), precision...]
    all_to_all x1, waiting for transfers between devices: 10.1 us -> 8.82 us  [on_device(): lax.all_to_all(packed.astype(f16), ('x', 'tensor'), 0, 0, tiled=True)]
    pallas_call x0 -> x1, Pallas kernels: none -> 1.23 us  [on_device(): pl.pallas_call(place_kernel, out_shape=jax.ShapeDtypeStruct((16, 8, ROW_N...]
  transfers between devices with their start and end apart: 8 -> 17, of which waited for: 6 -> 6; matrix products, arithmetic and copies ran while one was open for 2% -> 4% of each run, Pallas kernels for 2% -> 2%
where the time goes in v3:
time: 88.2 us; the launch traced here: 87.7 us
  waiting for transfers between devices  40.1 us (45%)
  starting transfers between devices  32.9 us (37%)
  Pallas kernels  4.6 us (5%)
  matrix products  4.32 us (5%)
  other arithmetic  3.4 us (4%)
  local copies, waits for them, and re-layouts  1.43 us (2%)
  between operations  1.04 us (1%)
    ppermute x12, starting transfers between devices, turn(): lax.ppermute(value, axis, [(i, (i + by) % 4) for i in range(4)])  13.2 us
    all_to_all x1, waiting for transfers between devices, on_device(): lax.all_to_all(rows.reshape(16, 2 * QPAD, 3 * LANES), ('y', 'x'), 0, 0, t...  12.3 us
    ppermute x12, waiting for transfers between devices, turn(): lax.ppermute(value, axis, [(i, (i + by) % 4) for i in range(4)])  10.8 us
    all_to_all x1, waiting for transfers between devices, on_device(): lax.all_to_all(packed.astype(f16), ('x', 'tensor'), 0, 0, tiled=True)  8.82 us
    all_to_all x1, starting transfers between devices, on_device(): lax.all_to_all(packed.astype(f16), ('x', 'tensor'), 0, 0, tiled=True)  8.25 us
    all_to_all x1, waiting for transfers between devices, on_device(): lax.all_to_all(heads.reshape(8, PAIR, 3 * LANES), 'tensor', 0, 0, tiled=T...  8.23 us
    all_to_all x1, starting transfers between devices, on_device(): lax.all_to_all(rows.reshape(16, 2 * QPAD, 3 * LANES), ('y', 'x'), 0, 0, t...  5.77 us
    dot_general x2, matrix products, one_hot_dot(): jnp.dot(chosen.astype(jnp.float32), source.astype(jnp.float32), precision...  4.32 us
  transfers between devices with their start and end apart: 17, of which 6 were waited for; matrix products, arithmetic and copies ran while one was open for 4% of the time, Pallas kernels for 2%

profile of v3, /device:TPU:0, one launch (start us, length us, event | category | flops | bytes accessed | tf_op | source)
XLA Modules:
  0.0 87.7 jit_solution(13506214778912409852)
XLA Ops:
  0.6 1.4 %shard_map.102 = (f32[32,24,384]{2,1,0:T(8,128)S(1)}, f32[2,8,48,128]{3,2,1,0:T(8,128)S(1)}, s32[2,8,128]{2,1,0:T(8,128)S(1)}) custom-call(s32[3,128]{1,0:T(4,128)} %bitcast.61, s32[3,128]{1,0:T(4,128)} %bitcast.49, f32[1,672,128]{2,1,0:T(8,128)} %w_ref.1, f32[1,672,128]{2,1,0:T(8,128)} %m_ref.1, f32[1,672,128]{2,1,0:T(8,128)} %v_ref.1, f32[1,672,128]{2,1,0:T(8,128)} %g_ref.3), custom_call_target="tpu_custom_call" | custom-call | tf_op jit(solution)/shard_map/pallas_call | solution.py:152
  2.1 0.9 %convert_element_type.45 = f16[32,24,384]{2,1,0:T(8,128)(2,1)} convert(f32[32,24,384]{2,1,0:T(8,128)S(1)} %get-tuple-element.13) | non-fusion elementwise | flops 294912 | bytes 1769472 | tf_op jit(solution)/shard_map/convert_element_type | solution.py:172
  3.0 8.3 %all-to-all-start = ((f16[32,24,384]{2,1,0:T(8,128)(2,1)}), f16[32,24,384]{2,1,0:T(8,128)(2,1)S(1)}, u32[]{:S(2)}, u32[]{:S(2)}) async-start(f16[32,24,384]{2,1,0:T(8,128)(2,1)} %convert_element_type.45), calls=%async_computation | async-start | bytes 1179648 | tf_op jit(solution)/shard_map/all_to_all | solution.py:172
  12.9 1.0 %fusion.2 = bf16[768,768]{1,0:T(8,128)(2,1)S(1)} fusion(s32[768]{0:T(1024)S(1)} %add.243, s32[768]{0:T(1024)S(1)} %ge.62, s32[768]{0:T(1024)S(1)} %get-tuple-element.37, s32[768]{0:T(1024)S(1)} %get-tuple-element.38, s32[768]{0:T(1024)S(1)} %reshape.306, pred[768]{0:T(1024)(128)(4,1)S(1)} %fusion.27), kind=kLoop, calls=%fused_computation.3 | loop fusion | flops 4718592 | bytes 1195776 | tf_op jit(solution)/shard_map/convert_element_type | solution.py:202
  14.2 8.8 %all-to-all-done = f16[32,24,384]{2,1,0:T(8,128)(2,1)S(1)} async-done(((f16[32,24,384]{2,1,0:T(8,128)(2,1)}), f16[32,24,384]{2,1,0:T(8,128)(2,1)S(1)}, u32[]{:S(2)}, u32[]{:S(2)}) %all-to-all-start) | async-done | bytes 589856 | tf_op jit(solution)/shard_map/all_to_all | solution.py:172
  23.0 2.2 %convolution_convert_fusion = f16[768,384]{1,0:T(8,128)(2,1)} fusion(bf16[768,768]{1,0:T(8,128)(2,1)S(1)} %fusion.2, f16[768,384]{1,0:T(8,128)(2,1)S(1)} %bitcast.52), kind=kOutput, calls=%fused_computation.6 | convolution fusion | flops 453279744 | bytes 2359296 | tf_op jit(solution)/shard_map/dot_general | solution.py:133
  25.2 5.8 %all-to-all-start.1 = ((f16[16,48,384]{2,1,0:T(8,128)(2,1)}), f16[16,48,384]{2,1,0:T(8,128)(2,1)S(1)}, u32[]{:S(2)}, u32[]{:S(2)}) async-start(f16[16,48,384]{2,1,0:T(8,128)(2,1)} %bitcast.6), calls=%async_computation.1 | async-start | bytes 1179648 | tf_op jit(solution)/shard_map/all_to_all | solution.py:205
  31.6 12.3 %all-to-all-done.1 = f16[16,48,384]{2,1,0:T(8,128)(2,1)S(1)} async-done(((f16[16,48,384]{2,1,0:T(8,128)(2,1)}), f16[16,48,384]{2,1,0:T(8,128)(2,1)S(1)}, u32[]{:S(2)}, u32[]{:S(2)}) %all-to-all-start.1) | async-done | bytes 589856 | tf_op jit(solution)/shard_map/all_to_all | solution.py:205
  43.8 2.1 %convolution_convert_fusion.1 = f16[704,384]{1,0:T(8,128)(2,1)} fusion(bf16[704,768]{1,0:T(8,128)(2,1)S(1)} %fusion.3, f16[768,384]{1,0:T(8,128)(2,1)S(1)} %bitcast.53), kind=kOutput, calls=%fused_computation.7 | convolution fusion | flops 415506432 | bytes 2211840 | tf_op jit(solution)/shard_map/dot_general | solution.py:133
  46.0 3.5 %all-to-all-start.2 = ((f16[8,88,384]{2,1,0:T(8,128)(2,1)}), f16[8,88,384]{2,1,0:T(8,128)(2,1)S(1)}, u32[]{:S(2)}, u32[]{:S(2)}) async-start(f16[8,88,384]{2,1,0:T(8,128)(2,1)} %bitcast.8), calls=%async_computation.2 | async-start | bytes 1081344 | tf_op jit(solution)/shard_map/all_to_all | solution.py:218
  49.6 1.3 %collective-permute-start = (f16[8,48,128]{2,1,0:T(8,128)(2,1)S(1)}, f16[8,48,128]{2,1,0:T(8,128)(2,1)S(1)}, u32[]{:S(2)}, u32[]{:S(2)}) collective-permute-start(f16[8,48,128]{2,1,0:T(8,128)(2,1)S(1)} %slice_bitcast_fusion.1), channel_id=1, source_target_pairs={{0,120},{8,0},{16,8},{24,16},{32,24},{40,32},{48,40},{56,48},{64,5... | collective-permute-start | bytes 294920 | tf_op jit(solution)/shard_map/ppermute | solution.py:176
  50.9 0.9 collective-permute-start.1
  51.7 8.2 %all-to-all-done.2 = f16[8,88,384]{2,1,0:T(8,128)(2,1)S(1)} async-done(((f16[8,88,384]{2,1,0:T(8,128)(2,1)}), f16[8,88,384]{2,1,0:T(8,128)(2,1)S(1)}, u32[]{:S(2)}, u32[]{:S(2)}) %all-to-all-start.2) | async-done | bytes 540704 | tf_op jit(solution)/shard_map/all_to_all | solution.py:218
  60.5 3.2 %collective-permute-start.9 = (bf16[8,2688]{1,0:T(8,128)(2,1)S(1)}, bf16[8,2688]{1,0:T(8,128)(2,1)S(1)}, u32[]{:S(2)}, u32[]{:S(2)}) collective-permute-start(bf16[8,2688]{1,0:T(8,128)(2,1)S(1)} %get-tuple-element.25), channel_id=1, source_target_pairs={{0,96},{32,0},{64,32},{96,64},{1,97},{33,1},{65,33},{97,65},{2,98}... | collective-permute-start | bytes 129032 | tf_op jit(solution)/shard_map/ppermute | solution.py:242
  64.3 2.7 %collective-permute-start.3 = (bf16[8,2688]{1,0:T(8,128)(2,1)S(1)}, bf16[8,2688]{1,0:T(8,128)(2,1)S(1)}, u32[]{:S(2)}, u32[]{:S(2)}) collective-permute-start(bf16[8,2688]{1,0:T(8,128)(2,1)S(1)} %get-tuple-element.26), channel_id=1, source_target_pairs={{0,24},{8,0},{16,8},{24,16},{1,25},{9,1},{17,9},{25,17},{2,26},{10... | collective-permute-start | bytes 129032 | tf_op jit(solution)/shard_map/ppermute | solution.py:242
  66.9 2.3 %collective-permute-done.10 = bf16[8,2688]{1,0:T(8,128)(2,1)S(1)} collective-permute-done((bf16[8,2688]{1,0:T(8,128)(2,1)S(1)}, bf16[8,2688]{1,0:T(8,128)(2,1)S(1)}, u32[]{:S(2)}, u32[]{:S(2)}) %collective-permute-start.10) | collective-permute-done | bytes 43040 | tf_op jit(solution)/shard_map/ppermute | solution.py:242
  69.3 0.6 collective-permute-start.11
  69.9 2.7 %collective-permute-start.12 = (bf16[4,8,2688]{2,1,0:T(8,128)(2,1)S(1)}, bf16[4,8,2688]{2,1,0:T(8,128)(2,1)S(1)}, u32[]{:S(2)}, u32[]{:S(2)}) collective-permute-start(bf16[4,8,2688]{2,1,0:T(8,128)(2,1)S(1)} %pad_maximum_fusion.1.refs_4_), channel_id=1, source_target_pairs={{0,24},{8,0},{16,8},{24,16},{1,25},{9,1},{17,9},{25,17},{2,26},{10... | collective-permute-start | bytes 516104 | tf_op jit(solution)/shard_map/ppermute | solution.py:242
  72.7 0.9 %collective-permute-start.5 = (bf16[4,8,2688]{2,1,0:T(8,128)(2,1)S(1)}, bf16[4,8,2688]{2,1,0:T(8,128)(2,1)S(1)}, u32[]{:S(2)}, u32[]{:S(2)}) collective-permute-start(bf16[4,8,2688]{2,1,0:T(8,128)(2,1)S(1)} %pad_maximum_fusion.refs_0_), channel_id=1, source_target_pairs={{0,32},{32,64},{64,96},{96,0},{1,33},{33,65},{65,97},{97,1},{2,34}... | collective-permute-start | bytes 516104 | tf_op jit(solution)/shard_map/ppermute | solution.py:242
  73.6 2.4 %collective-permute-start.6 = (bf16[4,8,2688]{2,1,0:T(8,128)(2,1)S(1)}, bf16[4,8,2688]{2,1,0:T(8,128)(2,1)S(1)}, u32[]{:S(2)}, u32[]{:S(2)}) collective-permute-start(bf16[4,8,2688]{2,1,0:T(8,128)(2,1)S(1)} %pad_maximum_fusion.refs_0_), channel_id=1, source_target_pairs={{0,96},{32,0},{64,32},{96,64},{1,97},{33,1},{65,33},{97,65},{2,98}... | collective-permute-start | bytes 516104 | tf_op jit(solution)/shard_map/ppermute | solution.py:242
  76.0 3.6 %collective-permute-done.11.refs_5_ = bf16[4,8,2688]{2,1,0:T(8,128)(2,1)S(1)} collective-permute-done((bf16[4,8,2688]{2,1,0:T(8,128)(2,1)S(1)}, bf16[4,8,2688]{2,1,0:T(8,128)(2,1)S(1)}, u32[]{:S(2)}, u32[]{:S(2)}) %collective-permute-start.11) | collective-permute-done | bytes 172064 | tf_op jit(solution)/shard_map/ppermute | solution.py:242
  79.7 2.0 %shard_map.103 = (f32[1,672,128]{2,1,0:T(8,128)}, f32[1,672,128]{2,1,0:T(8,128)}, f32[1,672,128]{2,1,0:T(8,128)}) custom-call(s32[3,128]{1,0:T(4,128)S(1)} %bitcast.50, f32[8,88,384]{2,1,0:T(8,128)S(1)} %convert_element_type.48.rows_ref, f32[1,672,128]{2,1,0:T(8,128)S(1)} %copy-done), custom_call_target="tpu_custom_call" | custom-call | tf_op jit(solution)/shard_map/pallas_call | solution.py:257
  81.7 4.8 %collective-permute-done.7.refs_3_ = bf16[4,8,2688]{2,1,0:T(8,128)(2,1)S(1)} collective-permute-done((bf16[4,8,2688]{2,1,0:T(8,128)(2,1)S(1)}, bf16[4,8,2688]{2,1,0:T(8,128)(2,1)S(1)}, u32[]{:S(2)}, u32[]{:S(2)}) %collective-permute-start.7) | collective-permute-done | bytes 172064 | tf_op jit(solution)/shard_map/ppermute | solution.py:242
  86.5 1.2 %shard_map.104 = bf16[16,8,5376]{2,1,0:T(8,128)(2,1)} custom-call(bf16[4,8,2688]{2,1,0:T(8,128)(2,1)S(1)} %pad_maximum_fusion.refs_0_, bf16[4,8,2688]{2,1,0:T(8,128)(2,1)S(1)} %collective-permute-done.5.refs_1_, bf16[4,8,2688]{2,1,0:T(8,128)(2,1)S(1)} %collective-permute-done.6.refs_2_, bf16[4,8,2688]{2,1,0:T(8,128)(2,1)S(1)} %collective-permute-done.7.refs_3_, ...), custom_call_target="tpu_custom_call" | custom-call | tf_op jit(solution)/shard_map/pallas_call | solution.py:249
  (85 shorter events, 3.6 us)
Async XLA Ops:
  2.0 9.2 %copy-start.1 = (s32[128,3]{0,1:T(4,128)S(1)}, s32[128,3]{0,1:T(4,128)}, u32[]{:S(2)}) copy-start(s32[128,3]{0,1:T(4,128)} %param.12) | copy-start | bytes 4612
  2.0 9.3 %copy-start.2 = (s32[128,3]{0,1:T(4,128)S(1)}, s32[128,3]{0,1:T(4,128)}, u32[]{:S(2)}) copy-start(s32[128,3]{0,1:T(4,128)} %param.11) | copy-start | bytes 4612
  2.0 9.7 %copy-start.3 = (s32[112]{0:T(128)S(1)}, s32[112]{0:T(128)}, u32[]{:S(2)}) copy-start(s32[112]{0:T(128)} %param.13) | copy-start | bytes 1348
  3.0 20.1 %all-to-all-start = ((f16[32,24,384]{2,1,0:T(8,128)(2,1)}), f16[32,24,384]{2,1,0:T(8,128)(2,1)S(1)}, u32[]{:S(2)}, u32[]{:S(2)}) async-start(f16[32,24,384]{2,1,0:T(8,128)(2,1)} %convert_element_type.45), calls=%async_computation | async-start | bytes 1179648 | tf_op jit(solution)/shard_map/all_to_all | solution.py:172
  25.2 18.6 %all-to-all-start.1 = ((f16[16,48,384]{2,1,0:T(8,128)(2,1)}), f16[16,48,384]{2,1,0:T(8,128)(2,1)S(1)}, u32[]{:S(2)}, u32[]{:S(2)}) async-start(f16[16,48,384]{2,1,0:T(8,128)(2,1)} %bitcast.6), calls=%async_computation.1 | async-start | bytes 1179648 | tf_op jit(solution)/shard_map/all_to_all | solution.py:205
  46.0 14.0 %all-to-all-start.2 = ((f16[8,88,384]{2,1,0:T(8,128)(2,1)}), f16[8,88,384]{2,1,0:T(8,128)(2,1)S(1)}, u32[]{:S(2)}, u32[]{:S(2)}) async-start(f16[8,88,384]{2,1,0:T(8,128)(2,1)} %bitcast.8), calls=%async_computation.2 | async-start | bytes 1081344 | tf_op jit(solution)/shard_map/all_to_all | solution.py:218
  49.6 10.4 %collective-permute-start = (f16[8,48,128]{2,1,0:T(8,128)(2,1)S(1)}, f16[8,48,128]{2,1,0:T(8,128)(2,1)S(1)}, u32[]{:S(2)}, u32[]{:S(2)}) collective-permute-start(f16[8,48,128]{2,1,0:T(8,128)(2,1)S(1)} %slice_bitcast_fusion.1), channel_id=1, source_target_pairs={{0,120},{8,0},{16,8},{24,16},{32,24},{40,32},{48,40},{56,48},{64,5... | collective-permute-start | bytes 294920 | tf_op jit(solution)/shard_map/ppermute | solution.py:176
  50.9 9.1 %collective-permute-start.1 = (f16[8,48,128]{2,1,0:T(8,128)(2,1)S(1)}, f16[8,48,128]{2,1,0:T(8,128)(2,1)S(1)}, u32[]{:S(2)}, u32[]{:S(2)}) collective-permute-start(f16[8,48,128]{2,1,0:T(8,128)(2,1)S(1)} %slice_bitcast_fusion.1), channel_id=1, source_target_pairs={{0,8},{8,16},{16,24},{24,32},{32,40},{40,48},{48,56},{56,64},{64,7... | collective-permute-start | bytes 294920 | tf_op jit(solution)/shard_map/ppermute | solution.py:177
  60.4 19.3 %copy-start = (f32[1,672,128]{2,1,0:T(8,128)S(1)}, f32[1,672,128]{2,1,0:T(8,128)}, u32[]{:S(2)}) copy-start(f32[1,672,128]{2,1,0:T(8,128)} %g_ref.3) | copy-start | bytes 1032196
  60.4 6.5 %collective-permute-start.8 = (bf16[8,2688]{1,0:T(8,128)(2,1)S(1)}, bf16[8,2688]{1,0:T(8,128)(2,1)S(1)}, u32[]{:S(2)}, u32[]{:S(2)}) collective-permute-start(bf16[8,2688]{1,0:T(8,128)(2,1)S(1)} %get-tuple-element.25), channel_id=1, source_target_pairs={{0,32},{32,64},{64,96},{96,0},{1,33},{33,65},{65,97},{97,1},{2,34}... | collective-permute-start | bytes 129032 | tf_op jit(solution)/shard_map/ppermute | solution.py:242
  60.5 6.5 %collective-permute-start.9 = (bf16[8,2688]{1,0:T(8,128)(2,1)S(1)}, bf16[8,2688]{1,0:T(8,128)(2,1)S(1)}, u32[]{:S(2)}, u32[]{:S(2)}) collective-permute-start(bf16[8,2688]{1,0:T(8,128)(2,1)S(1)} %get-tuple-element.25), channel_id=1, source_target_pairs={{0,96},{32,0},{64,32},{96,64},{1,97},{33,1},{65,33},{97,65},{2,98}... | collective-permute-start | bytes 129032 | tf_op jit(solution)/shard_map/ppermute | solution.py:242
  63.7 5.5 %collective-permute-start.10 = (bf16[8,2688]{1,0:T(8,128)(2,1)S(1)}, bf16[8,2688]{1,0:T(8,128)(2,1)S(1)}, u32[]{:S(2)}, u32[]{:S(2)}) collective-permute-start(bf16[8,2688]{1,0:T(8,128)(2,1)S(1)} %get-tuple-element.25), channel_id=1, source_target_pairs={{0,64},{32,96},{64,0},{96,32},{1,65},{33,97},{65,1},{97,33},{2,66}... | collective-permute-start | bytes 129032 | tf_op jit(solution)/shard_map/ppermute | solution.py:242
  63.7 8.9 %collective-permute-start.2 = (bf16[8,2688]{1,0:T(8,128)(2,1)S(1)}, bf16[8,2688]{1,0:T(8,128)(2,1)S(1)}, u32[]{:S(2)}, u32[]{:S(2)}) collective-permute-start(bf16[8,2688]{1,0:T(8,128)(2,1)S(1)} %get-tuple-element.26), channel_id=1, source_target_pairs={{0,8},{8,16},{16,24},{24,0},{1,9},{9,17},{17,25},{25,1},{2,10},{10... | collective-permute-start | bytes 129032 | tf_op jit(solution)/shard_map/ppermute | solution.py:242
  64.3 8.3 %collective-permute-start.3 = (bf16[8,2688]{1,0:T(8,128)(2,1)S(1)}, bf16[8,2688]{1,0:T(8,128)(2,1)S(1)}, u32[]{:S(2)}, u32[]{:S(2)}) collective-permute-start(bf16[8,2688]{1,0:T(8,128)(2,1)S(1)} %get-tuple-element.26), channel_id=1, source_target_pairs={{0,24},{8,0},{16,8},{24,16},{1,25},{9,1},{17,9},{25,17},{2,26},{10... | collective-permute-start | bytes 129032 | tf_op jit(solution)/shard_map/ppermute | solution.py:242
  66.9 5.7 %collective-permute-start.4 = (bf16[8,2688]{1,0:T(8,128)(2,1)S(1)}, bf16[8,2688]{1,0:T(8,128)(2,1)S(1)}, u32[]{:S(2)}, u32[]{:S(2)}) collective-permute-start(bf16[8,2688]{1,0:T(8,128)(2,1)S(1)} %get-tuple-element.26), channel_id=1, source_target_pairs={{0,16},{8,24},{16,0},{24,8},{1,17},{9,25},{17,1},{25,9},{2,18},{10... | collective-permute-start | bytes 129032 | tf_op jit(solution)/shard_map/ppermute | solution.py:242
  69.3 10.4 %collective-permute-start.11 = (bf16[4,8,2688]{2,1,0:T(8,128)(2,1)S(1)}, bf16[4,8,2688]{2,1,0:T(8,128)(2,1)S(1)}, u32[]{:S(2)}, u32[]{:S(2)}) collective-permute-start(bf16[4,8,2688]{2,1,0:T(8,128)(2,1)S(1)} %pad_maximum_fusion.1.refs_4_), channel_id=1, source_target_pairs={{0,8},{8,16},{16,24},{24,0},{1,9},{9,17},{17,25},{25,1},{2,10},{10... | collective-permute-start | bytes 516104 | tf_op jit(solution)/shard_map/ppermute | solution.py:242
  69.9 11.8 %collective-permute-start.12 = (bf16[4,8,2688]{2,1,0:T(8,128)(2,1)S(1)}, bf16[4,8,2688]{2,1,0:T(8,128)(2,1)S(1)}, u32[]{:S(2)}, u32[]{:S(2)}) collective-permute-start(bf16[4,8,2688]{2,1,0:T(8,128)(2,1)S(1)} %pad_maximum_fusion.1.refs_4_), channel_id=1, source_target_pairs={{0,24},{8,0},{16,8},{24,16},{1,25},{9,1},{17,9},{25,17},{2,26},{10... | collective-permute-start | bytes 516104 | tf_op jit(solution)/shard_map/ppermute | solution.py:242
  72.6 9.1 %collective-permute-start.13 = (bf16[4,8,2688]{2,1,0:T(8,128)(2,1)S(1)}, bf16[4,8,2688]{2,1,0:T(8,128)(2,1)S(1)}, u32[]{:S(2)}, u32[]{:S(2)}) collective-permute-start(bf16[4,8,2688]{2,1,0:T(8,128)(2,1)S(1)} %pad_maximum_fusion.1.refs_4_), channel_id=1, source_target_pairs={{0,16},{8,24},{16,0},{24,8},{1,17},{9,25},{17,1},{25,9},{2,18},{10... | collective-permute-start | bytes 516104 | tf_op jit(solution)/shard_map/ppermute | solution.py:242
  72.7 9.0 %collective-permute-start.5 = (bf16[4,8,2688]{2,1,0:T(8,128)(2,1)S(1)}, bf16[4,8,2688]{2,1,0:T(8,128)(2,1)S(1)}, u32[]{:S(2)}, u32[]{:S(2)}) collective-permute-start(bf16[4,8,2688]{2,1,0:T(8,128)(2,1)S(1)} %pad_maximum_fusion.refs_0_), channel_id=1, source_target_pairs={{0,32},{32,64},{64,96},{96,0},{1,33},{33,65},{65,97},{97,1},{2,34}... | collective-permute-start | bytes 516104 | tf_op jit(solution)/shard_map/ppermute | solution.py:242
  73.6 8.1 %collective-permute-start.6 = (bf16[4,8,2688]{2,1,0:T(8,128)(2,1)S(1)}, bf16[4,8,2688]{2,1,0:T(8,128)(2,1)S(1)}, u32[]{:S(2)}, u32[]{:S(2)}) collective-permute-start(bf16[4,8,2688]{2,1,0:T(8,128)(2,1)S(1)} %pad_maximum_fusion.refs_0_), channel_id=1, source_target_pairs={{0,96},{32,0},{64,32},{96,64},{1,97},{33,1},{65,33},{97,65},{2,98}... | collective-permute-start | bytes 516104 | tf_op jit(solution)/shard_map/ppermute | solution.py:242
  79.6 6.9 %collective-permute-start.7 = (bf16[4,8,2688]{2,1,0:T(8,128)(2,1)S(1)}, bf16[4,8,2688]{2,1,0:T(8,128)(2,1)S(1)}, u32[]{:S(2)}, u32[]{:S(2)}) collective-permute-start(bf16[4,8,2688]{2,1,0:T(8,128)(2,1)S(1)} %pad_maximum_fusion.refs_0_), channel_id=1, source_target_pairs={{0,64},{32,96},{64,0},{96,32},{1,65},{33,97},{65,1},{97,33},{2,66}... | collective-permute-start | bytes 516104 | tf_op jit(solution)/shard_map/ppermute | solution.py:242

commit v4 on v3

--- a/solution.py
+++ b/solution.py
@@ -18,7 +18,7 @@
 RPAD = 48
 PAIR = 88
 HALF = ROW_NEW * LANES // 2
-TURNS = (0, 1, 3, 2)
+TURNS = (0, 2, 1, 3)
 
 beta_first = 0.9
 beta_second = 0.95

time: 88.2 us -> 84.1 us (0.954)
  waiting for transfers between devices: 40.1 us -> 32.9 us
  starting transfers between devices: 32.9 us -> 36 us
    ppermute x12, waiting for transfers between devices: 10.8 us -> 3.56 us  [turn(): lax.ppermute(value, axis, [(i, (i + by) % 4) for i in range(4)])]
    ppermute x12, starting transfers between devices: 13.2 us -> 16.3 us  [turn(): lax.ppermute(value, axis, [(i, (i + by) % 4) for i in range(4)])]
  transfers between devices with their start and end apart: 17 -> 17, of which waited for: 6 -> 7; matrix products, arithmetic and copies ran while one was open for 4% -> 4% of each run, Pallas kernels for 2% -> 2%
where the time goes in v4:
time: 84.1 us; the launch traced here: 83.7 us
  starting transfers between devices  36 us (43%)
  waiting for transfers between devices  32.9 us (39%)
  Pallas kernels  4.6 us (5%)
  matrix products  4.32 us (5%)
  other arithmetic  3.4 us (4%)
  local copies, waits for them, and re-layouts  1.43 us (2%)
  between operations  1.02 us (1%)
    ppermute x12, starting transfers between devices, turn(): lax.ppermute(value, axis, [(i, (i + by) % 4) for i in range(4)])  16.3 us
    all_to_all x1, waiting for transfers between devices, on_device(): lax.all_to_all(rows.reshape(16, 2 * QPAD, 3 * LANES), ('y', 'x'), 0, 0, t...  12.3 us
    all_to_all x1, waiting for transfers between devices, on_device(): lax.all_to_all(packed.astype(f16), ('x', 'tensor'), 0, 0, tiled=True)  8.82 us
    all_to_all x1, starting transfers between devices, on_device(): lax.all_to_all(packed.astype(f16), ('x', 'tensor'), 0, 0, tiled=True)  8.25 us
    all_to_all x1, waiting for transfers between devices, on_device(): lax.all_to_all(heads.reshape(8, PAIR, 3 * LANES), 'tensor', 0, 0, tiled=T...  8.23 us
    all_to_all x1, starting transfers between devices, on_device(): lax.all_to_all(rows.reshape(16, 2 * QPAD, 3 * LANES), ('y', 'x'), 0, 0, t...  5.77 us
    dot_general x2, matrix products, one_hot_dot(): jnp.dot(chosen.astype(jnp.float32), source.astype(jnp.float32), precision...  4.32 us
    ppermute x12, waiting for transfers between devices, turn(): lax.ppermute(value, axis, [(i, (i + by) % 4) for i in range(4)])  3.56 us
  transfers between devices with their start and end apart: 17, of which 7 were waited for; matrix products, arithmetic and copies ran while one was open for 4% of the time, Pallas kernels for 2%

profile of v4, /device:TPU:0, one launch (start us, length us, event | category | flops | bytes accessed | tf_op | source)
XLA Modules:
  0.0 83.7 jit_solution(6280534284573447043)
XLA Ops:
  0.6 1.4 %shard_map.102 = (f32[32,24,384]{2,1,0:T(8,128)S(1)}, f32[2,8,48,128]{3,2,1,0:T(8,128)S(1)}, s32[2,8,128]{2,1,0:T(8,128)S(1)}) custom-call(s32[3,128]{1,0:T(4,128)} %bitcast.61, s32[3,128]{1,0:T(4,128)} %bitcast.49, f32[1,672,128]{2,1,0:T(8,128)} %w_ref.1, f32[1,672,128]{2,1,0:T(8,128)} %m_ref.1, f32[1,672,128]{2,1,0:T(8,128)} %v_ref.1, f32[1,672,128]{2,1,0:T(8,128)} %g_ref.3), custom_call_target="tpu_custom_call" | custom-call | tf_op jit(solution)/shard_map/pallas_call | solution.py:152
  2.1 0.9 %convert_element_type.45 = f16[32,24,384]{2,1,0:T(8,128)(2,1)} convert(f32[32,24,384]{2,1,0:T(8,128)S(1)} %get-tuple-element.13) | non-fusion elementwise | flops 294912 | bytes 1769472 | tf_op jit(solution)/shard_map/convert_element_type | solution.py:172
  3.0 8.2 %all-to-all-start = ((f16[32,24,384]{2,1,0:T(8,128)(2,1)}), f16[32,24,384]{2,1,0:T(8,128)(2,1)S(1)}, u32[]{:S(2)}, u32[]{:S(2)}) async-start(f16[32,24,384]{2,1,0:T(8,128)(2,1)} %convert_element_type.45), calls=%async_computation | async-start | bytes 1179648 | tf_op jit(solution)/shard_map/all_to_all | solution.py:172
  12.9 1.0 %fusion.2 = bf16[768,768]{1,0:T(8,128)(2,1)S(1)} fusion(s32[768]{0:T(1024)S(1)} %add.243, s32[768]{0:T(1024)S(1)} %ge.62, s32[768]{0:T(1024)S(1)} %get-tuple-element.37, s32[768]{0:T(1024)S(1)} %get-tuple-element.38, s32[768]{0:T(1024)S(1)} %reshape.306, pred[768]{0:T(1024)(128)(4,1)S(1)} %fusion.27), kind=kLoop, calls=%fused_computation.3 | loop fusion | flops 4718592 | bytes 1195776 | tf_op jit(solution)/shard_map/convert_element_type | solution.py:202
  14.2 8.8 %all-to-all-done = f16[32,24,384]{2,1,0:T(8,128)(2,1)S(1)} async-done(((f16[32,24,384]{2,1,0:T(8,128)(2,1)}), f16[32,24,384]{2,1,0:T(8,128)(2,1)S(1)}, u32[]{:S(2)}, u32[]{:S(2)}) %all-to-all-start) | async-done | bytes 589856 | tf_op jit(solution)/shard_map/all_to_all | solution.py:172
  23.0 2.2 %convolution_convert_fusion = f16[768,384]{1,0:T(8,128)(2,1)} fusion(bf16[768,768]{1,0:T(8,128)(2,1)S(1)} %fusion.2, f16[768,384]{1,0:T(8,128)(2,1)S(1)} %bitcast.52), kind=kOutput, calls=%fused_computation.6 | convolution fusion | flops 453279744 | bytes 2359296 | tf_op jit(solution)/shard_map/dot_general | solution.py:133
  25.2 5.8 %all-to-all-start.1 = ((f16[16,48,384]{2,1,0:T(8,128)(2,1)}), f16[16,48,384]{2,1,0:T(8,128)(2,1)S(1)}, u32[]{:S(2)}, u32[]{:S(2)}) async-start(f16[16,48,384]{2,1,0:T(8,128)(2,1)} %bitcast.6), calls=%async_computation.1 | async-start | bytes 1179648 | tf_op jit(solution)/shard_map/all_to_all | solution.py:205
  31.6 12.3 %all-to-all-done.1 = f16[16,48,384]{2,1,0:T(8,128)(2,1)S(1)} async-done(((f16[16,48,384]{2,1,0:T(8,128)(2,1)}), f16[16,48,384]{2,1,0:T(8,128)(2,1)S(1)}, u32[]{:S(2)}, u32[]{:S(2)}) %all-to-all-start.1) | async-done | bytes 589856 | tf_op jit(solution)/shard_map/all_to_all | solution.py:205
  43.8 2.1 %convolution_convert_fusion.1 = f16[704,384]{1,0:T(8,128)(2,1)} fusion(bf16[704,768]{1,0:T(8,128)(2,1)S(1)} %fusion.3, f16[768,384]{1,0:T(8,128)(2,1)S(1)} %bitcast.53), kind=kOutput, calls=%fused_computation.7 | convolution fusion | flops 415506432 | bytes 2211840 | tf_op jit(solution)/shard_map/dot_general | solution.py:133
  46.0 3.5 %all-to-all-start.2 = ((f16[8,88,384]{2,1,0:T(8,128)(2,1)}), f16[8,88,384]{2,1,0:T(8,128)(2,1)S(1)}, u32[]{:S(2)}, u32[]{:S(2)}) async-start(f16[8,88,384]{2,1,0:T(8,128)(2,1)} %bitcast.8), calls=%async_computation.2 | async-start | bytes 1081344 | tf_op jit(solution)/shard_map/all_to_all | solution.py:218
  49.6 1.3 %collective-permute-start = (f16[8,48,128]{2,1,0:T(8,128)(2,1)S(1)}, f16[8,48,128]{2,1,0:T(8,128)(2,1)S(1)}, u32[]{:S(2)}, u32[]{:S(2)}) collective-permute-start(f16[8,48,128]{2,1,0:T(8,128)(2,1)S(1)} %slice_bitcast_fusion.1), channel_id=1, source_target_pairs={{0,120},{8,0},{16,8},{24,16},{32,24},{40,32},{48,40},{56,48},{64,5... | collective-permute-start | bytes 294920 | tf_op jit(solution)/shard_map/ppermute | solution.py:176
  51.7 8.2 %all-to-all-done.2 = f16[8,88,384]{2,1,0:T(8,128)(2,1)S(1)} async-done(((f16[8,88,384]{2,1,0:T(8,128)(2,1)}), f16[8,88,384]{2,1,0:T(8,128)(2,1)S(1)}, u32[]{:S(2)}, u32[]{:S(2)}) %all-to-all-start.2) | async-done | bytes 540704 | tf_op jit(solution)/shard_map/all_to_all | solution.py:218
  60.4 0.9 %collective-permute-start.8 = (bf16[8,2688]{1,0:T(8,128)(2,1)S(1)}, bf16[8,2688]{1,0:T(8,128)(2,1)S(1)}, u32[]{:S(2)}, u32[]{:S(2)}) collective-permute-start(bf16[8,2688]{1,0:T(8,128)(2,1)S(1)} %get-tuple-element.25), channel_id=1, source_target_pairs={{0,64},{32,96},{64,0},{96,32},{1,65},{33,97},{65,1},{97,33},{2,66}... | collective-permute-start | bytes 129032 | tf_op jit(solution)/shard_map/ppermute | solution.py:242
  62.2 2.4 %collective-permute-start.10 = (bf16[8,2688]{1,0:T(8,128)(2,1)S(1)}, bf16[8,2688]{1,0:T(8,128)(2,1)S(1)}, u32[]{:S(2)}, u32[]{:S(2)}) collective-permute-start(bf16[8,2688]{1,0:T(8,128)(2,1)S(1)} %get-tuple-element.25), channel_id=1, source_target_pairs={{0,96},{32,0},{64,32},{96,64},{1,97},{33,1},{65,33},{97,65},{2,98}... | collective-permute-start | bytes 129032 | tf_op jit(solution)/shard_map/ppermute | solution.py:242
  64.6 1.4 %collective-permute-start.2 = (bf16[8,2688]{1,0:T(8,128)(2,1)S(1)}, bf16[8,2688]{1,0:T(8,128)(2,1)S(1)}, u32[]{:S(2)}, u32[]{:S(2)}) collective-permute-start(bf16[8,2688]{1,0:T(8,128)(2,1)S(1)} %get-tuple-element.26), channel_id=1, source_target_pairs={{0,16},{8,24},{16,0},{24,8},{1,17},{9,25},{17,1},{25,9},{2,18},{10... | collective-permute-start | bytes 129032 | tf_op jit(solution)/shard_map/ppermute | solution.py:242
  66.6 2.6 %collective-permute-start.4 = (bf16[8,2688]{1,0:T(8,128)(2,1)S(1)}, bf16[8,2688]{1,0:T(8,128)(2,1)S(1)}, u32[]{:S(2)}, u32[]{:S(2)}) collective-permute-start(bf16[8,2688]{1,0:T(8,128)(2,1)S(1)} %get-tuple-element.26), channel_id=1, source_target_pairs={{0,24},{8,0},{16,8},{24,16},{1,25},{9,1},{17,9},{25,17},{2,26},{10... | collective-permute-start | bytes 129032 | tf_op jit(solution)/shard_map/ppermute | solution.py:242
  69.3 1.0 %collective-permute-start.11 = (bf16[4,8,2688]{2,1,0:T(8,128)(2,1)S(1)}, bf16[4,8,2688]{2,1,0:T(8,128)(2,1)S(1)}, u32[]{:S(2)}, u32[]{:S(2)}) collective-permute-start(bf16[4,8,2688]{2,1,0:T(8,128)(2,1)S(1)} %pad_maximum_fusion.1.refs_4_), channel_id=1, source_target_pairs={{0,16},{8,24},{16,0},{24,8},{1,17},{9,25},{17,1},{25,9},{2,18},{10... | collective-permute-start | bytes 516104 | tf_op jit(solution)/shard_map/ppermute | solution.py:242
  70.8 2.7 %collective-permute-start.13 = (bf16[4,8,2688]{2,1,0:T(8,128)(2,1)S(1)}, bf16[4,8,2688]{2,1,0:T(8,128)(2,1)S(1)}, u32[]{:S(2)}, u32[]{:S(2)}) collective-permute-start(bf16[4,8,2688]{2,1,0:T(8,128)(2,1)S(1)} %pad_maximum_fusion.1.refs_4_), channel_id=1, source_target_pairs={{0,24},{8,0},{16,8},{24,16},{1,25},{9,1},{17,9},{25,17},{2,26},{10... | collective-permute-start | bytes 516104 | tf_op jit(solution)/shard_map/ppermute | solution.py:242
  73.5 1.5 %collective-permute-start.5 = (bf16[4,8,2688]{2,1,0:T(8,128)(2,1)S(1)}, bf16[4,8,2688]{2,1,0:T(8,128)(2,1)S(1)}, u32[]{:S(2)}, u32[]{:S(2)}) collective-permute-start(bf16[4,8,2688]{2,1,0:T(8,128)(2,1)S(1)} %pad_maximum_fusion.refs_0_), channel_id=1, source_target_pairs={{0,64},{32,96},{64,0},{96,32},{1,65},{33,97},{65,1},{97,33},{2,66}... | collective-permute-start | bytes 516104 | tf_op jit(solution)/shard_map/ppermute | solution.py:242
  75.6 1.5 %collective-permute-done.11.refs_5_ = bf16[4,8,2688]{2,1,0:T(8,128)(2,1)S(1)} collective-permute-done((bf16[4,8,2688]{2,1,0:T(8,128)(2,1)S(1)}, bf16[4,8,2688]{2,1,0:T(8,128)(2,1)S(1)}, u32[]{:S(2)}, u32[]{:S(2)}) %collective-permute-start.11) | collective-permute-done | bytes 172064 | tf_op jit(solution)/shard_map/ppermute | solution.py:242
  77.0 1.3 %collective-permute-start.7 = (bf16[4,8,2688]{2,1,0:T(8,128)(2,1)S(1)}, bf16[4,8,2688]{2,1,0:T(8,128)(2,1)S(1)}, u32[]{:S(2)}, u32[]{:S(2)}) collective-permute-start(bf16[4,8,2688]{2,1,0:T(8,128)(2,1)S(1)} %pad_maximum_fusion.refs_0_), channel_id=1, source_target_pairs={{0,96},{32,0},{64,32},{96,64},{1,97},{33,1},{65,33},{97,65},{2,98}... | collective-permute-start | bytes 516104 | tf_op jit(solution)/shard_map/ppermute | solution.py:242
  78.4 2.0 %shard_map.103 = (f32[1,672,128]{2,1,0:T(8,128)}, f32[1,672,128]{2,1,0:T(8,128)}, f32[1,672,128]{2,1,0:T(8,128)}) custom-call(s32[3,128]{1,0:T(4,128)S(1)} %bitcast.50, f32[8,88,384]{2,1,0:T(8,128)S(1)} %convert_element_type.48.rows_ref, f32[1,672,128]{2,1,0:T(8,128)S(1)} %copy-done), custom_call_target="tpu_custom_call" | custom-call | tf_op jit(solution)/shard_map/pallas_call | solution.py:257
  80.6 1.8 %collective-permute-done.6.refs_2_ = bf16[4,8,2688]{2,1,0:T(8,128)(2,1)S(1)} collective-permute-done((bf16[4,8,2688]{2,1,0:T(8,128)(2,1)S(1)}, bf16[4,8,2688]{2,1,0:T(8,128)(2,1)S(1)}, u32[]{:S(2)}, u32[]{:S(2)}) %collective-permute-start.6) | collective-permute-done | bytes 172064 | tf_op jit(solution)/shard_map/ppermute | solution.py:242
  82.4 1.2 %shard_map.104 = bf16[16,8,5376]{2,1,0:T(8,128)(2,1)} custom-call(bf16[4,8,2688]{2,1,0:T(8,128)(2,1)S(1)} %pad_maximum_fusion.refs_0_, bf16[4,8,2688]{2,1,0:T(8,128)(2,1)S(1)} %collective-permute-done.5.refs_1_, bf16[4,8,2688]{2,1,0:T(8,128)(2,1)S(1)} %collective-permute-done.6.refs_2_, bf16[4,8,2688]{2,1,0:T(8,128)(2,1)S(1)} %collective-permute-done.7.refs_3_, ...), custom_call_target="tpu_custom_call" | custom-call | tf_op jit(solution)/shard_map/pallas_call | solution.py:249
  (85 shorter events, 6.6 us)
Async XLA Ops:
  2.0 9.2 %copy-start.1 = (s32[128,3]{0,1:T(4,128)S(1)}, s32[128,3]{0,1:T(4,128)}, u32[]{:S(2)}) copy-start(s32[128,3]{0,1:T(4,128)} %param.12) | copy-start | bytes 4612
  2.0 9.3 %copy-start.2 = (s32[128,3]{0,1:T(4,128)S(1)}, s32[128,3]{0,1:T(4,128)}, u32[]{:S(2)}) copy-start(s32[128,3]{0,1:T(4,128)} %param.11) | copy-start | bytes 4612
  2.0 9.7 %copy-start.3 = (s32[112]{0:T(128)S(1)}, s32[112]{0:T(128)}, u32[]{:S(2)}) copy-start(s32[112]{0:T(128)} %param.13) | copy-start | bytes 1348
  3.0 20.1 %all-to-all-start = ((f16[32,24,384]{2,1,0:T(8,128)(2,1)}), f16[32,24,384]{2,1,0:T(8,128)(2,1)S(1)}, u32[]{:S(2)}, u32[]{:S(2)}) async-start(f16[32,24,384]{2,1,0:T(8,128)(2,1)} %convert_element_type.45), calls=%async_computation | async-start | bytes 1179648 | tf_op jit(solution)/shard_map/all_to_all | solution.py:172
  25.2 18.6 %all-to-all-start.1 = ((f16[16,48,384]{2,1,0:T(8,128)(2,1)}), f16[16,48,384]{2,1,0:T(8,128)(2,1)S(1)}, u32[]{:S(2)}, u32[]{:S(2)}) async-start(f16[16,48,384]{2,1,0:T(8,128)(2,1)} %bitcast.6), calls=%async_computation.1 | async-start | bytes 1179648 | tf_op jit(solution)/shard_map/all_to_all | solution.py:205
  46.0 14.0 %all-to-all-start.2 = ((f16[8,88,384]{2,1,0:T(8,128)(2,1)}), f16[8,88,384]{2,1,0:T(8,128)(2,1)S(1)}, u32[]{:S(2)}, u32[]{:S(2)}) async-start(f16[8,88,384]{2,1,0:T(8,128)(2,1)} %bitcast.8), calls=%async_computation.2 | async-start | bytes 1081344 | tf_op jit(solution)/shard_map/all_to_all | solution.py:218
  49.6 10.4 %collective-permute-start = (f16[8,48,128]{2,1,0:T(8,128)(2,1)S(1)}, f16[8,48,128]{2,1,0:T(8,128)(2,1)S(1)}, u32[]{:S(2)}, u32[]{:S(2)}) collective-permute-start(f16[8,48,128]{2,1,0:T(8,128)(2,1)S(1)} %slice_bitcast_fusion.1), channel_id=1, source_target_pairs={{0,120},{8,0},{16,8},{24,16},{32,24},{40,32},{48,40},{56,48},{64,5... | collective-permute-start | bytes 294920 | tf_op jit(solution)/shard_map/ppermute | solution.py:176
  50.9 9.1 %collective-permute-start.1 = (f16[8,48,128]{2,1,0:T(8,128)(2,1)S(1)}, f16[8,48,128]{2,1,0:T(8,128)(2,1)S(1)}, u32[]{:S(2)}, u32[]{:S(2)}) collective-permute-start(f16[8,48,128]{2,1,0:T(8,128)(2,1)S(1)} %slice_bitcast_fusion.1), channel_id=1, source_target_pairs={{0,8},{8,16},{16,24},{24,32},{32,40},{40,48},{48,56},{56,64},{64,7... | collective-permute-start | bytes 294920 | tf_op jit(solution)/shard_map/ppermute | solution.py:177
  60.4 18.0 %copy-start = (f32[1,672,128]{2,1,0:T(8,128)S(1)}, f32[1,672,128]{2,1,0:T(8,128)}, u32[]{:S(2)}) copy-start(f32[1,672,128]{2,1,0:T(8,128)} %g_ref.3) | copy-start | bytes 1032196
  60.4 6.2 %collective-permute-start.8 = (bf16[8,2688]{1,0:T(8,128)(2,1)S(1)}, bf16[8,2688]{1,0:T(8,128)(2,1)S(1)}, u32[]{:S(2)}, u32[]{:S(2)}) collective-permute-start(bf16[8,2688]{1,0:T(8,128)(2,1)S(1)} %get-tuple-element.25), channel_id=1, source_target_pairs={{0,64},{32,96},{64,0},{96,32},{1,65},{33,97},{65,1},{97,33},{2,66}... | collective-permute-start | bytes 129032 | tf_op jit(solution)/shard_map/ppermute | solution.py:242
  61.3 7.9 %collective-permute-start.9 = (bf16[8,2688]{1,0:T(8,128)(2,1)S(1)}, bf16[8,2688]{1,0:T(8,128)(2,1)S(1)}, u32[]{:S(2)}, u32[]{:S(2)}) collective-permute-start(bf16[8,2688]{1,0:T(8,128)(2,1)S(1)} %get-tuple-element.25), channel_id=1, source_target_pairs={{0,32},{32,64},{64,96},{96,0},{1,33},{33,65},{65,97},{97,1},{2,34}... | collective-permute-start | bytes 129032 | tf_op jit(solution)/shard_map/ppermute | solution.py:242
  62.2 7.0 %collective-permute-start.10 = (bf16[8,2688]{1,0:T(8,128)(2,1)S(1)}, bf16[8,2688]{1,0:T(8,128)(2,1)S(1)}, u32[]{:S(2)}, u32[]{:S(2)}) collective-permute-start(bf16[8,2688]{1,0:T(8,128)(2,1)S(1)} %get-tuple-element.25), channel_id=1, source_target_pairs={{0,96},{32,0},{64,32},{96,64},{1,97},{33,1},{65,33},{97,65},{2,98}... | collective-permute-start | bytes 129032 | tf_op jit(solution)/shard_map/ppermute | solution.py:242
  64.6 6.3 %collective-permute-start.2 = (bf16[8,2688]{1,0:T(8,128)(2,1)S(1)}, bf16[8,2688]{1,0:T(8,128)(2,1)S(1)}, u32[]{:S(2)}, u32[]{:S(2)}) collective-permute-start(bf16[8,2688]{1,0:T(8,128)(2,1)S(1)} %get-tuple-element.26), channel_id=1, source_target_pairs={{0,16},{8,24},{16,0},{24,8},{1,17},{9,25},{17,1},{25,9},{2,18},{10... | collective-permute-start | bytes 129032 | tf_op jit(solution)/shard_map/ppermute | solution.py:242
  66.0 7.5 %collective-permute-start.3 = (bf16[8,2688]{1,0:T(8,128)(2,1)S(1)}, bf16[8,2688]{1,0:T(8,128)(2,1)S(1)}, u32[]{:S(2)}, u32[]{:S(2)}) collective-permute-start(bf16[8,2688]{1,0:T(8,128)(2,1)S(1)} %get-tuple-element.26), channel_id=1, source_target_pairs={{0,8},{8,16},{16,24},{24,0},{1,9},{9,17},{17,25},{25,1},{2,10},{10... | collective-permute-start | bytes 129032 | tf_op jit(solution)/shard_map/ppermute | solution.py:242
  66.6 6.9 %collective-permute-start.4 = (bf16[8,2688]{1,0:T(8,128)(2,1)S(1)}, bf16[8,2688]{1,0:T(8,128)(2,1)S(1)}, u32[]{:S(2)}, u32[]{:S(2)}) collective-permute-start(bf16[8,2688]{1,0:T(8,128)(2,1)S(1)} %get-tuple-element.26), channel_id=1, source_target_pairs={{0,24},{8,0},{16,8},{24,16},{1,25},{9,1},{17,9},{25,17},{2,26},{10... | collective-permute-start | bytes 129032 | tf_op jit(solution)/shard_map/ppermute | solution.py:242
  69.3 7.8 %collective-permute-start.11 = (bf16[4,8,2688]{2,1,0:T(8,128)(2,1)S(1)}, bf16[4,8,2688]{2,1,0:T(8,128)(2,1)S(1)}, u32[]{:S(2)}, u32[]{:S(2)}) collective-permute-start(bf16[4,8,2688]{2,1,0:T(8,128)(2,1)S(1)} %pad_maximum_fusion.1.refs_4_), channel_id=1, source_target_pairs={{0,16},{8,24},{16,0},{24,8},{1,17},{9,25},{17,1},{25,9},{2,18},{10... | collective-permute-start | bytes 516104 | tf_op jit(solution)/shard_map/ppermute | solution.py:242
  70.2 10.1 %collective-permute-start.12 = (bf16[4,8,2688]{2,1,0:T(8,128)(2,1)S(1)}, bf16[4,8,2688]{2,1,0:T(8,128)(2,1)S(1)}, u32[]{:S(2)}, u32[]{:S(2)}) collective-permute-start(bf16[4,8,2688]{2,1,0:T(8,128)(2,1)S(1)} %pad_maximum_fusion.1.refs_4_), channel_id=1, source_target_pairs={{0,8},{8,16},{16,24},{24,0},{1,9},{9,17},{17,25},{25,1},{2,10},{10... | collective-permute-start | bytes 516104 | tf_op jit(solution)/shard_map/ppermute | solution.py:242
  70.8 9.6 %collective-permute-start.13 = (bf16[4,8,2688]{2,1,0:T(8,128)(2,1)S(1)}, bf16[4,8,2688]{2,1,0:T(8,128)(2,1)S(1)}, u32[]{:S(2)}, u32[]{:S(2)}) collective-permute-start(bf16[4,8,2688]{2,1,0:T(8,128)(2,1)S(1)} %pad_maximum_fusion.1.refs_4_), channel_id=1, source_target_pairs={{0,24},{8,0},{16,8},{24,16},{1,25},{9,1},{17,9},{25,17},{2,26},{10... | collective-permute-start | bytes 516104 | tf_op jit(solution)/shard_map/ppermute | solution.py:242
  73.5 7.1 %collective-permute-start.5 = (bf16[4,8,2688]{2,1,0:T(8,128)(2,1)S(1)}, bf16[4,8,2688]{2,1,0:T(8,128)(2,1)S(1)}, u32[]{:S(2)}, u32[]{:S(2)}) collective-permute-start(bf16[4,8,2688]{2,1,0:T(8,128)(2,1)S(1)} %pad_maximum_fusion.refs_0_), channel_id=1, source_target_pairs={{0,64},{32,96},{64,0},{96,32},{1,65},{33,97},{65,1},{97,33},{2,66}... | collective-permute-start | bytes 516104 | tf_op jit(solution)/shard_map/ppermute | solution.py:242
  75.1 7.3 %collective-permute-start.6 = (bf16[4,8,2688]{2,1,0:T(8,128)(2,1)S(1)}, bf16[4,8,2688]{2,1,0:T(8,128)(2,1)S(1)}, u32[]{:S(2)}, u32[]{:S(2)}) collective-permute-start(bf16[4,8,2688]{2,1,0:T(8,128)(2,1)S(1)} %pad_maximum_fusion.refs_0_), channel_id=1, source_target_pairs={{0,32},{32,64},{64,96},{96,0},{1,33},{33,65},{65,97},{97,1},{2,34}... | collective-permute-start | bytes 516104 | tf_op jit(solution)/shard_map/ppermute | solution.py:242
  77.0 5.4 %collective-permute-start.7 = (bf16[4,8,2688]{2,1,0:T(8,128)(2,1)S(1)}, bf16[4,8,2688]{2,1,0:T(8,128)(2,1)S(1)}, u32[]{:S(2)}, u32[]{:S(2)}) collective-permute-start(bf16[4,8,2688]{2,1,0:T(8,128)(2,1)S(1)} %pad_maximum_fusion.refs_0_), channel_id=1, source_target_pairs={{0,96},{32,0},{64,32},{96,64},{1,97},{33,1},{65,33},{97,65},{2,98}... | collective-permute-start | bytes 516104 | tf_op jit(solution)/shard_map/ppermute | solution.py:242

commit v5 on v4

--- a/solution.py
+++ b/solution.py
@@ -17,7 +17,6 @@
 ROW_NEW = 42
 RPAD = 48
 PAIR = 88
-HALF = ROW_NEW * LANES // 2
 TURNS = (0, 2, 1, 3)
 
 beta_first = 0.9
@@ -66,7 +65,7 @@
     for copy in tables:
         copy.wait()
     dp = lax.axis_index("y") * 4 + lax.axis_index("x")
-    tp = lax.axis_index("tensor")
+    tp = lax.axis_index("z") * 2 + lax.axis_index("c")
     old_start = lax.rem(old_ref[1, dp * 8 + tp], SLOT)
     new_start = new_ref[1, dp * 8 + tp]
     new_place = lax.rem(new_start - dp * UNIT, SLOT)
@@ -92,7 +91,7 @@
 
 def owner_kernel(new_ref, rows_ref, g_ref, w_out, m_out, v_out, scratch):
     dp = lax.axis_index("y") * 4 + lax.axis_index("x")
-    tp = lax.axis_index("tensor")
+    tp = lax.axis_index("z") * 2 + lax.axis_index("c")
     new_place = lax.rem(new_ref[1, dp * 8 + tp] - dp * UNIT, SLOT)
     length = new_ref[2, dp * 8 + tp]
     for half in range(2):
@@ -117,16 +116,15 @@
 
 
 def place_kernel(*refs):
-    pieces, out_ref = refs[:8], refs[8]
+    held, out_ref = refs[:4], refs[4]
     y, x = lax.axis_index("y"), lax.axis_index("x")
-    for half in range(2):
-        for k in range(4):
-            for l in range(4):
-                dy, dx = (k, l) if half == 0 else (l, k)
-                from_y = lax.rem(y + 4 - TURNS[dy], 4)
-                from_x = lax.rem(x + 4 - TURNS[dx], 4)
-                block = lax.rem(from_y * 4 + from_x + 1, 16)
-                out_ref[block, :, pl.ds(half * HALF, HALF)] = pieces[half * 4 + k][l]
+    x_first = lax.axis_index("c") == 0
+    for k in range(4):
+        for l in range(4):
+            dy = jnp.where(x_first, TURNS[k], TURNS[l])
+            dx = jnp.where(x_first, TURNS[l], TURNS[k])
+            block = lax.rem(lax.rem(y + 4 - dy, 4) * 4 + lax.rem(x + 4 - dx, 4) + 1, 16)
+            out_ref[block] = held[k][l]
 
 
 def one_hot_dot(chosen, source):
@@ -142,7 +140,8 @@
 def on_device(old_master, old_avg, old_sq, grad, old_table, new_table, head_order):
     y = lax.axis_index("y")
     x = lax.axis_index("x")
-    t = lax.axis_index("tensor")
+    core = lax.axis_index("c")
+    t = lax.axis_index("z") * 2 + core
     dp = y * 4 + x
     f16 = jnp.float16
 
@@ -169,7 +168,7 @@
     up = [(i, (i + 1) % 16) for i in range(16)]
     down = [(i, (i - 1) % 16) for i in range(16)]
 
-    first = lax.all_to_all(packed.astype(f16), ("x", "tensor"), 0, 0, tiled=True)
+    first = lax.all_to_all(packed.astype(f16), ("x", "z", "c"), 0, 0, tiled=True)
 
     grad_rows, first = lax.optimization_barrier((grad_rows, first))
     grad_send = grad_rows.astype(f16)
@@ -215,7 +214,7 @@
     moved = lax.optimization_barrier((origin == col_id).astype(jnp.bfloat16))
     heads = one_hot_dot(moved, second.reshape(32 * QPAD, 3 * LANES))
 
-    block = lax.all_to_all(heads.reshape(8, PAIR, 3 * LANES), "tensor", 0, 0, tiled=True)
+    block = lax.all_to_all(heads.reshape(8, PAIR, 3 * LANES), ("z", "c"), 0, 0, tiled=True)
 
     own = lax.broadcasted_iota(jnp.int32, (8, RPAD, LANES), 0) * ROW_NEW
     own = own + lax.broadcasted_iota(jnp.int32, (8, RPAD, LANES), 1)
@@ -237,22 +236,34 @@
     )
     mine = master[:, :ROW_NEW].astype(jnp.bfloat16).reshape(8, ROW_NEW * LANES)
 
-    def turn(value, axis):
+    def linear(i_y, i_x, i_z, i_c):
+        return ((i_y * 4 + i_x) * 4 + i_z) * 2 + i_c
+
+    def moves(by, first):
+        pairs = []
+        for i_y in range(4):
+            for i_x in range(4):
+                for i_z in range(4):
+                    for i_c in range(2):
+                        along_x = (i_c == 0) == first
+                        to_y = i_y if along_x else (i_y + by) % 4
+                        to_x = (i_x + by) % 4 if along_x else i_x
+                        pairs.append((linear(i_y, i_x, i_z, i_c), linear(to_y, to_x, i_z, i_c)))
+        return pairs
+
+    def turn(value, first):
         return [value] + [
-            lax.ppermute(value, axis, [(i, (i + by) % 4) for i in range(4)])
-            for by in TURNS[1:]
+            lax.ppermute(value, ("y", "x", "z", "c"), moves(by, first)) for by in TURNS[1:]
         ]
 
-    by_x = jnp.stack(turn(mine[:, :HALF], "x"))
-    by_y = jnp.stack(turn(mine[:, HALF:], "y"))
-    pieces = turn(by_x, "y") + turn(by_y, "x")
+    held = turn(jnp.stack(turn(mine, True)), False)
     params = pl.pallas_call(
         place_kernel,
         out_shape=jax.ShapeDtypeStruct((16, 8, ROW_NEW * LANES), jnp.bfloat16),
-        in_specs=[vmem] * 8,
+        in_specs=[vmem] * 4,
         out_specs=vmem,
         compiler_params=pltpu.CompilerParams(vmem_limit_bytes=16 * 1024 * 1024),
-    )(*pieces).reshape(128, ROW_NEW * LANES)
+    )(*held).reshape(128, ROW_NEW * LANES)
 
     outs = pl.pallas_call(
         owner_kernel,
@@ -266,12 +277,12 @@
 
 
 def solution(mesh):
-    fine = Mesh(mesh.devices.reshape(4, 4, 8), ("y", "x", "tensor"))
-    parts = P(("y", "x", "tensor"), None, None)
+    fine = Mesh(mesh.devices.reshape(4, 4, 4, 2), ("y", "x", "z", "c"))
+    parts = P(("y", "x", "z", "c"), None, None)
     return jax.shard_map(
         on_device,
         mesh=fine,
         in_specs=(parts, parts, parts, parts, P(), P(), P()),
-        out_specs=(parts, parts, parts, P(None, "tensor")),
+        out_specs=(parts, parts, parts, P(None, ("z", "c"))),
         check_vma=False,
     )

time: 84.1 us -> 82.7 us (0.983); the launches traced: 83.7 us -> 81.2 us
  starting transfers between devices: 36 us -> 28.2 us
  waiting for transfers between devices: 32.9 us -> 38.2 us
    ppermute x12 -> x6, starting transfers between devices: 16.3 us -> 8.5 us  [turn(): lax.ppermute(value, ('y', 'x', 'z', 'c'), moves(by, first))]
    ppermute x12 -> x6, waiting for transfers between devices: 3.56 us -> 8.87 us  [turn(): lax.ppermute(value, ('y', 'x', 'z', 'c'), moves(by, first))]
  transfers between devices with their start and end apart: 17 -> 11, of which waited for: 7 -> 7; matrix products, arithmetic and copies ran while one was open for 4% -> 4% of each run, Pallas kernels for 2% -> 2%
where the time goes in v5:
time: 82.7 us; the launch traced here: 81.2 us
  waiting for transfers between devices  38.2 us (46%)
  starting transfers between devices  28.2 us (34%)
  Pallas kernels  4.67 us (6%)
  matrix products  4.32 us (5%)
  other arithmetic  3.38 us (4%)
  local copies, waits for them, and re-layouts  1.47 us (2%)
  between operations  1 us (1%)
    all_to_all x1, waiting for transfers between devices, on_device(): lax.all_to_all(rows.reshape(16, 2 * QPAD, 3 * LANES), ('y', 'x'), 0, 0, t...  12.3 us
    ppermute x6, waiting for transfers between devices, turn(): lax.ppermute(value, ('y', 'x', 'z', 'c'), moves(by, first))  8.87 us
    all_to_all x1, waiting for transfers between devices, on_device(): lax.all_to_all(packed.astype(f16), ('x', 'z', 'c'), 0, 0, tiled=True)  8.82 us
    ppermute x6, starting transfers between devices, turn(): lax.ppermute(value, ('y', 'x', 'z', 'c'), moves(by, first))  8.5 us
    all_to_all x1, starting transfers between devices, on_device(): lax.all_to_all(packed.astype(f16), ('x', 'z', 'c'), 0, 0, tiled=True)  8.25 us
    all_to_all x1, waiting for transfers between devices, on_device(): lax.all_to_all(heads.reshape(8, PAIR, 3 * LANES), ('z', 'c'), 0, 0, tiled...  8.23 us
    all_to_all x1, starting transfers between devices, on_device(): lax.all_to_all(rows.reshape(16, 2 * QPAD, 3 * LANES), ('y', 'x'), 0, 0, t...  5.77 us
    dot_general x2, matrix products, one_hot_dot(): jnp.dot(chosen.astype(jnp.float32), source.astype(jnp.float32), precision...  4.32 us
  transfers between devices with their start and end apart: 11, of which 7 were waited for; matrix products, arithmetic and copies ran while one was open for 4% of the time, Pallas kernels for 2%

profile of v5, /device:TPU:0, one launch (start us, length us, event | category | flops | bytes accessed | tf_op | source)
XLA Modules:
  0.0 81.2 jit_solution(14836661593244270676)
XLA Ops:
  0.6 1.4 %shard_map.102 = (f32[32,24,384]{2,1,0:T(8,128)S(1)}, f32[2,8,48,128]{3,2,1,0:T(8,128)S(1)}, s32[2,8,128]{2,1,0:T(8,128)S(1)}) custom-call(s32[3,128]{1,0:T(4,128)} %bitcast.53, s32[3,128]{1,0:T(4,128)} %bitcast.41, f32[1,672,128]{2,1,0:T(8,128)} %w_ref.1, f32[1,672,128]{2,1,0:T(8,128)} %m_ref.1, f32[1,672,128]{2,1,0:T(8,128)} %v_ref.1, f32[1,672,128]{2,1,0:T(8,128)} %g_ref.3), custom_call_target="tpu_custom_call" | custom-call | tf_op jit(solution)/shard_map/pallas_call | solution.py:151
  2.1 0.9 %convert_element_type.45 = f16[32,24,384]{2,1,0:T(8,128)(2,1)} convert(f32[32,24,384]{2,1,0:T(8,128)S(1)} %get-tuple-element.13) | non-fusion elementwise | flops 294912 | bytes 1769472 | tf_op jit(solution)/shard_map/convert_element_type | solution.py:171
  3.0 8.2 %all-to-all-start = ((f16[32,24,384]{2,1,0:T(8,128)(2,1)}), f16[32,24,384]{2,1,0:T(8,128)(2,1)S(1)}, u32[]{:S(2)}, u32[]{:S(2)}) async-start(f16[32,24,384]{2,1,0:T(8,128)(2,1)} %convert_element_type.45), calls=%async_computation | async-start | bytes 1179648 | tf_op jit(solution)/shard_map/all_to_all | solution.py:171
  12.9 1.0 %fusion.2 = bf16[768,768]{1,0:T(8,128)(2,1)S(1)} fusion(s32[768]{0:T(1024)S(1)} %add.247, s32[768]{0:T(1024)S(1)} %ge.62, s32[768]{0:T(1024)S(1)} %get-tuple-element.33, s32[768]{0:T(1024)S(1)} %get-tuple-element.34, s32[768]{0:T(1024)S(1)} %reshape.306, pred[768]{0:T(1024)(128)(4,1)S(1)} %fusion.26), kind=kLoop, calls=%fused_computation.3 | loop fusion | flops 4718592 | bytes 1195776 | tf_op jit(solution)/shard_map/convert_element_type | solution.py:201
  14.2 8.8 %all-to-all-done = f16[32,24,384]{2,1,0:T(8,128)(2,1)S(1)} async-done(((f16[32,24,384]{2,1,0:T(8,128)(2,1)}), f16[32,24,384]{2,1,0:T(8,128)(2,1)S(1)}, u32[]{:S(2)}, u32[]{:S(2)}) %all-to-all-start) | async-done | bytes 589856 | tf_op jit(solution)/shard_map/all_to_all | solution.py:171
  23.0 2.2 %convolution_convert_fusion = f16[768,384]{1,0:T(8,128)(2,1)} fusion(bf16[768,768]{1,0:T(8,128)(2,1)S(1)} %fusion.2, f16[768,384]{1,0:T(8,128)(2,1)S(1)} %bitcast.45), kind=kOutput, calls=%fused_computation.6 | convolution fusion | flops 453279744 | bytes 2359296 | tf_op jit(solution)/shard_map/dot_general | solution.py:131
  25.2 5.8 %all-to-all-start.1 = ((f16[16,48,384]{2,1,0:T(8,128)(2,1)}), f16[16,48,384]{2,1,0:T(8,128)(2,1)S(1)}, u32[]{:S(2)}, u32[]{:S(2)}) async-start(f16[16,48,384]{2,1,0:T(8,128)(2,1)} %bitcast.6), calls=%async_computation.1 | async-start | bytes 1179648 | tf_op jit(solution)/shard_map/all_to_all | solution.py:204
  31.6 12.3 %all-to-all-done.1 = f16[16,48,384]{2,1,0:T(8,128)(2,1)S(1)} async-done(((f16[16,48,384]{2,1,0:T(8,128)(2,1)}), f16[16,48,384]{2,1,0:T(8,128)(2,1)S(1)}, u32[]{:S(2)}, u32[]{:S(2)}) %all-to-all-start.1) | async-done | bytes 589856 | tf_op jit(solution)/shard_map/all_to_all | solution.py:204
  43.8 2.1 %convolution_convert_fusion.1 = f16[704,384]{1,0:T(8,128)(2,1)} fusion(bf16[704,768]{1,0:T(8,128)(2,1)S(1)} %fusion.3, f16[768,384]{1,0:T(8,128)(2,1)S(1)} %bitcast.46), kind=kOutput, calls=%fused_computation.7 | convolution fusion | flops 415506432 | bytes 2211840 | tf_op jit(solution)/shard_map/dot_general | solution.py:131
  46.0 3.5 %all-to-all-start.2 = ((f16[8,88,384]{2,1,0:T(8,128)(2,1)}), f16[8,88,384]{2,1,0:T(8,128)(2,1)S(1)}, u32[]{:S(2)}, u32[]{:S(2)}) async-start(f16[8,88,384]{2,1,0:T(8,128)(2,1)} %bitcast.8), calls=%async_computation.2 | async-start | bytes 1081344 | tf_op jit(solution)/shard_map/all_to_all | solution.py:217
  49.6 1.3 %collective-permute-start = (f16[8,48,128]{2,1,0:T(8,128)(2,1)S(1)}, f16[8,48,128]{2,1,0:T(8,128)(2,1)S(1)}, u32[]{:S(2)}, u32[]{:S(2)}) collective-permute-start(f16[8,48,128]{2,1,0:T(8,128)(2,1)S(1)} %slice_bitcast_fusion.1), channel_id=1, source_target_pairs={{0,120},{8,0},{16,8},{24,16},{32,24},{40,32},{48,40},{56,48},{64,5... | collective-permute-start | bytes 294920 | tf_op jit(solution)/shard_map/ppermute | solution.py:175
  50.9 0.9 %collective-permute-start.1 = (f16[8,48,128]{2,1,0:T(8,128)(2,1)S(1)}, f16[8,48,128]{2,1,0:T(8,128)(2,1)S(1)}, u32[]{:S(2)}, u32[]{:S(2)}) collective-permute-start(f16[8,48,128]{2,1,0:T(8,128)(2,1)S(1)} %slice_bitcast_fusion.1), channel_id=1, source_target_pairs={{0,8},{8,16},{16,24},{24,32},{32,40},{40,48},{48,56},{56,64},{64,7... | collective-permute-start | bytes 294920 | tf_op jit(solution)/shard_map/ppermute | solution.py:176
  51.7 8.2 %all-to-all-done.2 = f16[8,88,384]{2,1,0:T(8,128)(2,1)S(1)} async-done(((f16[8,88,384]{2,1,0:T(8,128)(2,1)}), f16[8,88,384]{2,1,0:T(8,128)(2,1)S(1)}, u32[]{:S(2)}, u32[]{:S(2)}) %all-to-all-start.2) | async-done | bytes 540704 | tf_op jit(solution)/shard_map/all_to_all | solution.py:217
  60.4 0.9 %collective-permute-start.2 = (bf16[8,5376]{1,0:T(8,128)(2,1)S(1)}, bf16[8,5376]{1,0:T(8,128)(2,1)S(1)}, u32[]{:S(2)}, u32[]{:S(2)}) collective-permute-start(bf16[8,5376]{1,0:T(8,128)(2,1)S(1)} %bitcast.47), channel_id=1, source_target_pairs={{0,16},{1,65},{2,18},{3,67},{4,20},{5,69},{6,22},{7,71},{8,24},{9,... | collective-permute-start | bytes 258056 | tf_op jit(solution)/shard_map/ppermute | solution.py:256
  61.8 2.7 %collective-permute-start.4 = (bf16[8,5376]{1,0:T(8,128)(2,1)S(1)}, bf16[8,5376]{1,0:T(8,128)(2,1)S(1)}, u32[]{:S(2)}, u32[]{:S(2)}) collective-permute-start(bf16[8,5376]{1,0:T(8,128)(2,1)S(1)} %bitcast.49), channel_id=1, source_target_pairs={{0,24},{1,97},{2,26},{3,99},{4,28},{5,101},{6,30},{7,103},{8,0},{9... | collective-permute-start | bytes 258056 | tf_op jit(solution)/shard_map/ppermute | solution.py:256
  64.5 1.9 %collective-permute-done.2 = bf16[8,5376]{1,0:T(8,128)(2,1)S(1)} collective-permute-done((bf16[8,5376]{1,0:T(8,128)(2,1)S(1)}, bf16[8,5376]{1,0:T(8,128)(2,1)S(1)}, u32[]{:S(2)}, u32[]{:S(2)}) %collective-permute-start.2) | collective-permute-done | bytes 86048 | tf_op jit(solution)/shard_map/ppermute | solution.py:256
  66.5 0.9 %collective-permute-done.3 = bf16[8,5376]{1,0:T(8,128)(2,1)S(1)} collective-permute-done((bf16[8,5376]{1,0:T(8,128)(2,1)S(1)}, bf16[8,5376]{1,0:T(8,128)(2,1)S(1)}, u32[]{:S(2)}, u32[]{:S(2)}) %collective-permute-start.3) | collective-permute-done | bytes 86048 | tf_op jit(solution)/shard_map/ppermute | solution.py:256
  67.4 1.1 %collective-permute-start.5 = (bf16[4,8,5376]{2,1,0:T(8,128)(2,1)S(1)}, bf16[4,8,5376]{2,1,0:T(8,128)(2,1)S(1)}, u32[]{:S(2)}, u32[]{:S(2)}) collective-permute-start(bf16[4,8,5376]{2,1,0:T(8,128)(2,1)S(1)} %pad_maximum_fusion.refs_0_), channel_id=1, source_target_pairs={{0,64},{1,17},{2,66},{3,19},{4,68},{5,21},{6,70},{7,23},{8,72},{9,... | collective-permute-start | bytes 1032200 | tf_op jit(solution)/shard_map/ppermute | solution.py:256
  68.5 0.7 collective-permute-start.6
  69.2 2.6 %collective-permute-start.7 = (bf16[4,8,5376]{2,1,0:T(8,128)(2,1)S(1)}, bf16[4,8,5376]{2,1,0:T(8,128)(2,1)S(1)}, u32[]{:S(2)}, u32[]{:S(2)}) collective-permute-start(bf16[4,8,5376]{2,1,0:T(8,128)(2,1)S(1)} %pad_maximum_fusion.refs_0_), channel_id=1, source_target_pairs={{0,96},{1,25},{2,98},{3,27},{4,100},{5,29},{6,102},{7,31},{8,104},... | collective-permute-start | bytes 1032200 | tf_op jit(solution)/shard_map/ppermute | solution.py:256
  71.9 2.0 %shard_map.103 = (f32[1,672,128]{2,1,0:T(8,128)}, f32[1,672,128]{2,1,0:T(8,128)}, f32[1,672,128]{2,1,0:T(8,128)}) custom-call(s32[3,128]{1,0:T(4,128)S(1)} %bitcast.42, f32[8,88,384]{2,1,0:T(8,128)S(1)} %convert_element_type.48.rows_ref, f32[1,672,128]{2,1,0:T(8,128)S(1)} %copy-done), custom_call_target="tpu_custom_call" | custom-call | tf_op jit(solution)/shard_map/pallas_call | solution.py:268
  73.8 2.5 %collective-permute-done.5.refs_1_ = bf16[4,8,5376]{2,1,0:T(8,128)(2,1)S(1)} collective-permute-done((bf16[4,8,5376]{2,1,0:T(8,128)(2,1)S(1)}, bf16[4,8,5376]{2,1,0:T(8,128)(2,1)S(1)}, u32[]{:S(2)}, u32[]{:S(2)}) %collective-permute-start.5) | collective-permute-done | bytes 344096 | tf_op jit(solution)/shard_map/ppermute | solution.py:256
  76.3 3.6 %collective-permute-done.6.refs_2_ = bf16[4,8,5376]{2,1,0:T(8,128)(2,1)S(1)} collective-permute-done((bf16[4,8,5376]{2,1,0:T(8,128)(2,1)S(1)}, bf16[4,8,5376]{2,1,0:T(8,128)(2,1)S(1)}, u32[]{:S(2)}, u32[]{:S(2)}) %collective-permute-start.6) | collective-permute-done | bytes 344096 | tf_op jit(solution)/shard_map/ppermute | solution.py:256
  79.9 1.3 %shard_map.104 = bf16[16,8,5376]{2,1,0:T(8,128)(2,1)} custom-call(bf16[4,8,5376]{2,1,0:T(8,128)(2,1)S(1)} %pad_maximum_fusion.refs_0_, bf16[4,8,5376]{2,1,0:T(8,128)(2,1)S(1)} %collective-permute-done.5.refs_1_, bf16[4,8,5376]{2,1,0:T(8,128)(2,1)S(1)} %collective-permute-done.6.refs_2_, bf16[4,8,5376]{2,1,0:T(8,128)(2,1)S(1)} %collective-permute-done.7.refs_3_), custom_call_target="tpu_custom_call" | custom-call | tf_op jit(solution)/shard_map/pallas_call | solution.py:260
  (72 shorter events, 3.5 us)
Async XLA Ops:
  2.0 9.2 %copy-start.1 = (s32[128,3]{0,1:T(4,128)S(1)}, s32[128,3]{0,1:T(4,128)}, u32[]{:S(2)}) copy-start(s32[128,3]{0,1:T(4,128)} %param.12) | copy-start | bytes 4612
  2.0 9.3 %copy-start.2 = (s32[128,3]{0,1:T(4,128)S(1)}, s32[128,3]{0,1:T(4,128)}, u32[]{:S(2)}) copy-start(s32[128,3]{0,1:T(4,128)} %param.11) | copy-start | bytes 4612
  2.0 9.7 %copy-start.3 = (s32[112]{0:T(128)S(1)}, s32[112]{0:T(128)}, u32[]{:S(2)}) copy-start(s32[112]{0:T(128)} %param.13) | copy-start | bytes 1348
  3.0 20.1 %all-to-all-start = ((f16[32,24,384]{2,1,0:T(8,128)(2,1)}), f16[32,24,384]{2,1,0:T(8,128)(2,1)S(1)}, u32[]{:S(2)}, u32[]{:S(2)}) async-start(f16[32,24,384]{2,1,0:T(8,128)(2,1)} %convert_element_type.45), calls=%async_computation | async-start | bytes 1179648 | tf_op jit(solution)/shard_map/all_to_all | solution.py:171
  25.2 18.6 %all-to-all-start.1 = ((f16[16,48,384]{2,1,0:T(8,128)(2,1)}), f16[16,48,384]{2,1,0:T(8,128)(2,1)S(1)}, u32[]{:S(2)}, u32[]{:S(2)}) async-start(f16[16,48,384]{2,1,0:T(8,128)(2,1)} %bitcast.6), calls=%async_computation.1 | async-start | bytes 1179648 | tf_op jit(solution)/shard_map/all_to_all | solution.py:204
  46.0 14.0 %all-to-all-start.2 = ((f16[8,88,384]{2,1,0:T(8,128)(2,1)}), f16[8,88,384]{2,1,0:T(8,128)(2,1)S(1)}, u32[]{:S(2)}, u32[]{:S(2)}) async-start(f16[8,88,384]{2,1,0:T(8,128)(2,1)} %bitcast.8), calls=%async_computation.2 | async-start | bytes 1081344 | tf_op jit(solution)/shard_map/all_to_all | solution.py:217
  49.6 10.4 %collective-permute-start = (f16[8,48,128]{2,1,0:T(8,128)(2,1)S(1)}, f16[8,48,128]{2,1,0:T(8,128)(2,1)S(1)}, u32[]{:S(2)}, u32[]{:S(2)}) collective-permute-start(f16[8,48,128]{2,1,0:T(8,128)(2,1)S(1)} %slice_bitcast_fusion.1), channel_id=1, source_target_pairs={{0,120},{8,0},{16,8},{24,16},{32,24},{40,32},{48,40},{56,48},{64,5... | collective-permute-start | bytes 294920 | tf_op jit(solution)/shard_map/ppermute | solution.py:175
  50.9 9.1 %collective-permute-start.1 = (f16[8,48,128]{2,1,0:T(8,128)(2,1)S(1)}, f16[8,48,128]{2,1,0:T(8,128)(2,1)S(1)}, u32[]{:S(2)}, u32[]{:S(2)}) collective-permute-start(f16[8,48,128]{2,1,0:T(8,128)(2,1)S(1)} %slice_bitcast_fusion.1), channel_id=1, source_target_pairs={{0,8},{8,16},{16,24},{24,32},{32,40},{40,48},{48,56},{56,64},{64,7... | collective-permute-start | bytes 294920 | tf_op jit(solution)/shard_map/ppermute | solution.py:176
  60.4 6.1 %collective-permute-start.2 = (bf16[8,5376]{1,0:T(8,128)(2,1)S(1)}, bf16[8,5376]{1,0:T(8,128)(2,1)S(1)}, u32[]{:S(2)}, u32[]{:S(2)}) collective-permute-start(bf16[8,5376]{1,0:T(8,128)(2,1)S(1)} %bitcast.47), channel_id=1, source_target_pairs={{0,16},{1,65},{2,18},{3,67},{4,20},{5,69},{6,22},{7,71},{8,24},{9,... | collective-permute-start | bytes 258056 | tf_op jit(solution)/shard_map/ppermute | solution.py:256
  61.2 6.1 %collective-permute-start.3 = (bf16[8,5376]{1,0:T(8,128)(2,1)S(1)}, bf16[8,5376]{1,0:T(8,128)(2,1)S(1)}, u32[]{:S(2)}, u32[]{:S(2)}) collective-permute-start(bf16[8,5376]{1,0:T(8,128)(2,1)S(1)} %bitcast.48), channel_id=1, source_target_pairs={{0,8},{1,33},{2,10},{3,35},{4,12},{5,37},{6,14},{7,39},{8,16},{9,4... | collective-permute-start | bytes 258056 | tf_op jit(solution)/shard_map/ppermute | solution.py:256
  61.8 5.5 %collective-permute-start.4 = (bf16[8,5376]{1,0:T(8,128)(2,1)S(1)}, bf16[8,5376]{1,0:T(8,128)(2,1)S(1)}, u32[]{:S(2)}, u32[]{:S(2)}) collective-permute-start(bf16[8,5376]{1,0:T(8,128)(2,1)S(1)} %bitcast.49), channel_id=1, source_target_pairs={{0,24},{1,97},{2,26},{3,99},{4,28},{5,101},{6,30},{7,103},{8,0},{9... | collective-permute-start | bytes 258056 | tf_op jit(solution)/shard_map/ppermute | solution.py:256
  64.5 7.3 %copy-start = (f32[1,672,128]{2,1,0:T(8,128)S(1)}, f32[1,672,128]{2,1,0:T(8,128)}, u32[]{:S(2)}) copy-start(f32[1,672,128]{2,1,0:T(8,128)} %g_ref.3) | copy-start | bytes 1032196
  67.4 8.9 %collective-permute-start.5 = (bf16[4,8,5376]{2,1,0:T(8,128)(2,1)S(1)}, bf16[4,8,5376]{2,1,0:T(8,128)(2,1)S(1)}, u32[]{:S(2)}, u32[]{:S(2)}) collective-permute-start(bf16[4,8,5376]{2,1,0:T(8,128)(2,1)S(1)} %pad_maximum_fusion.refs_0_), channel_id=1, source_target_pairs={{0,64},{1,17},{2,66},{3,19},{4,68},{5,21},{6,70},{7,23},{8,72},{9,... | collective-permute-start | bytes 1032200 | tf_op jit(solution)/shard_map/ppermute | solution.py:256
  68.5 11.4 %collective-permute-start.6 = (bf16[4,8,5376]{2,1,0:T(8,128)(2,1)S(1)}, bf16[4,8,5376]{2,1,0:T(8,128)(2,1)S(1)}, u32[]{:S(2)}, u32[]{:S(2)}) collective-permute-start(bf16[4,8,5376]{2,1,0:T(8,128)(2,1)S(1)} %pad_maximum_fusion.refs_0_), channel_id=1, source_target_pairs={{0,32},{1,9},{2,34},{3,11},{4,36},{5,13},{6,38},{7,15},{8,40},{9,1... | collective-permute-start | bytes 1032200 | tf_op jit(solution)/shard_map/ppermute | solution.py:256
  69.2 10.7 %collective-permute-start.7 = (bf16[4,8,5376]{2,1,0:T(8,128)(2,1)S(1)}, bf16[4,8,5376]{2,1,0:T(8,128)(2,1)S(1)}, u32[]{:S(2)}, u32[]{:S(2)}) collective-permute-start(bf16[4,8,5376]{2,1,0:T(8,128)(2,1)S(1)} %pad_maximum_fusion.refs_0_), channel_id=1, source_target_pairs={{0,96},{1,25},{2,98},{3,27},{4,100},{5,29},{6,102},{7,31},{8,104},... | collective-permute-start | bytes 1032200 | tf_op jit(solution)/shard_map/ppermute | solution.py:256

commit v6 on v5

--- a/solution.py
+++ b/solution.py
@@ -204,6 +204,7 @@
     second = lax.all_to_all(
         rows.reshape(16, 2 * QPAD, 3 * LANES), ("y", "x"), 0, 0, tiled=True
     )
+    second, grad_first = lax.optimization_barrier((second, grad_first))
     order = head_order.reshape(8, 1, 1, 14)
     kind = jnp.arange(2, dtype=jnp.int32).reshape(1, 2, 1, 1)
     comp = jnp.arange(3, dtype=jnp.int32).reshape(1, 1, 3, 1)

time: 82.7 us -> 82 us (level)
  waiting for transfers between devices: 38.2 us -> 31.3 us
  starting transfers between devices: 28.2 us -> 35 us
    all_to_all x1, waiting for transfers between devices: 12.3 us -> 1.51 us  [on_device(): lax.all_to_all(rows.reshape(16, 2 * QPAD, 3 * LANES), ('y', 'x'), 0, 0, t...]
    ppermute x1, waiting for transfers between devices: 0.01 us -> 5.59 us  [on_device(): grad_first = lax.ppermute(grad_send[0], ('y', 'x'), down)]
    ppermute x1, starting transfers between devices: 1.27 us -> 5.32 us  [on_device(): grad_first = lax.ppermute(grad_send[0], ('y', 'x'), down)]
    ppermute x6, starting transfers between devices: 8.5 us -> 10.7 us  [turn(): lax.ppermute(value, ('y', 'x', 'z', 'c'), moves(by, first))]
    ppermute x6, waiting for transfers between devices: 8.87 us -> 6.66 us  [turn(): lax.ppermute(value, ('y', 'x', 'z', 'c'), moves(by, first))]
  transfers between devices with their start and end apart: 11 -> 11, of which waited for: 7 -> 8; matrix products, arithmetic and copies ran while one was open for 4% -> 4% of each run, Pallas kernels for 2% -> 2%
where the time goes in v6:
time: 82 us; the launch traced here: 81.2 us
  starting transfers between devices  35 us (43%)
  waiting for transfers between devices  31.3 us (38%)
  Pallas kernels  4.67 us (6%)
  matrix products  4.32 us (5%)
  other arithmetic  3.37 us (4%)
  local copies, waits for them, and re-layouts  1.46 us (2%)
  between operations  1.01 us (1%)
    ppermute x6, starting transfers between devices, turn(): lax.ppermute(value, ('y', 'x', 'z', 'c'), moves(by, first))  10.7 us
    all_to_all x1, waiting for transfers between devices, on_device(): lax.all_to_all(heads.reshape(8, PAIR, 3 * LANES), ('z', 'c'), 0, 0, tiled...  8.97 us
    all_to_all x1, waiting for transfers between devices, on_device(): lax.all_to_all(packed.astype(f16), ('x', 'z', 'c'), 0, 0, tiled=True)  8.61 us
    all_to_all x1, starting transfers between devices, on_device(): lax.all_to_all(packed.astype(f16), ('x', 'z', 'c'), 0, 0, tiled=True)  8.25 us
    ppermute x6, waiting for transfers between devices, turn(): lax.ppermute(value, ('y', 'x', 'z', 'c'), moves(by, first))  6.66 us
    all_to_all x1, starting transfers between devices, on_device(): lax.all_to_all(rows.reshape(16, 2 * QPAD, 3 * LANES), ('y', 'x'), 0, 0, t...  5.77 us
    ppermute x1, waiting for transfers between devices, on_device(): grad_first = lax.ppermute(grad_send[0], ('y', 'x'), down)  5.59 us
    ppermute x1, starting transfers between devices, on_device(): grad_first = lax.ppermute(grad_send[0], ('y', 'x'), down)  5.32 us
  transfers between devices with their start and end apart: 11, of which 8 were waited for; matrix products, arithmetic and copies ran while one was open for 4% of the time, Pallas kernels for 2%

profile of v6, /device:TPU:0, one launch (start us, length us, event | category | flops | bytes accessed | tf_op | source)
XLA Modules:
  0.0 81.2 jit_solution(3259403813970978847)
XLA Ops:
  0.6 1.4 %shard_map.102 = (f32[32,24,384]{2,1,0:T(8,128)S(1)}, f32[2,8,48,128]{3,2,1,0:T(8,128)S(1)}, s32[2,8,128]{2,1,0:T(8,128)S(1)}) custom-call(s32[3,128]{1,0:T(4,128)} %bitcast.53, s32[3,128]{1,0:T(4,128)} %bitcast.41, f32[1,672,128]{2,1,0:T(8,128)} %w_ref.1, f32[1,672,128]{2,1,0:T(8,128)} %m_ref.1, f32[1,672,128]{2,1,0:T(8,128)} %v_ref.1, f32[1,672,128]{2,1,0:T(8,128)} %g_ref.3), custom_call_target="tpu_custom_call" | custom-call | tf_op jit(solution)/shard_map/pallas_call | solution.py:151
  2.1 0.9 %convert_element_type.45 = f16[32,24,384]{2,1,0:T(8,128)(2,1)} convert(f32[32,24,384]{2,1,0:T(8,128)S(1)} %get-tuple-element.15) | non-fusion elementwise | flops 294912 | bytes 1769472 | tf_op jit(solution)/shard_map/convert_element_type | solution.py:171
  3.0 8.2 %all-to-all-start = ((f16[32,24,384]{2,1,0:T(8,128)(2,1)}), f16[32,24,384]{2,1,0:T(8,128)(2,1)S(1)}, u32[]{:S(2)}, u32[]{:S(2)}) async-start(f16[32,24,384]{2,1,0:T(8,128)(2,1)} %convert_element_type.45), calls=%async_computation | async-start | bytes 1179648 | tf_op jit(solution)/shard_map/all_to_all | solution.py:171
  12.9 1.0 %fusion.2 = bf16[768,768]{1,0:T(8,128)(2,1)S(1)} fusion(s32[768]{0:T(1024)S(1)} %add.247, s32[768]{0:T(1024)S(1)} %ge.62, s32[768]{0:T(1024)S(1)} %get-tuple-element.37, s32[768]{0:T(1024)S(1)} %get-tuple-element.38, s32[768]{0:T(1024)S(1)} %reshape.306, pred[768]{0:T(1024)(128)(4,1)S(1)} %fusion.26), kind=kLoop, calls=%fused_computation.3 | loop fusion | flops 4718592 | bytes 1195776 | tf_op jit(solution)/shard_map/convert_element_type | solution.py:201
  14.4 8.6 %all-to-all-done = f16[32,24,384]{2,1,0:T(8,128)(2,1)S(1)} async-done(((f16[32,24,384]{2,1,0:T(8,128)(2,1)}), f16[32,24,384]{2,1,0:T(8,128)(2,1)S(1)}, u32[]{:S(2)}, u32[]{:S(2)}) %all-to-all-start) | async-done | bytes 589856 | tf_op jit(solution)/shard_map/all_to_all | solution.py:171
  23.0 2.2 %convolution_convert_fusion = f16[768,384]{1,0:T(8,128)(2,1)} fusion(bf16[768,768]{1,0:T(8,128)(2,1)S(1)} %fusion.2, f16[768,384]{1,0:T(8,128)(2,1)S(1)} %bitcast.45), kind=kOutput, calls=%fused_computation.6 | convolution fusion | flops 453279744 | bytes 2359296 | tf_op jit(solution)/shard_map/dot_general | solution.py:131
  25.2 5.8 %all-to-all-start.1 = ((f16[16,48,384]{2,1,0:T(8,128)(2,1)}), f16[16,48,384]{2,1,0:T(8,128)(2,1)S(1)}, u32[]{:S(2)}, u32[]{:S(2)}) async-start(f16[16,48,384]{2,1,0:T(8,128)(2,1)} %bitcast.6), calls=%async_computation.1 | async-start | bytes 1179648 | tf_op jit(solution)/shard_map/all_to_all | solution.py:204
  31.2 5.3 %collective-permute-start = (f16[8,48,128]{2,1,0:T(8,128)(2,1)S(1)}, f16[8,48,128]{2,1,0:T(8,128)(2,1)S(1)}, u32[]{:S(2)}, u32[]{:S(2)}) collective-permute-start(f16[8,48,128]{2,1,0:T(8,128)(2,1)S(1)} %slice_bitcast_fusion.1), channel_id=1, source_target_pairs={{0,120},{8,0},{16,8},{24,16},{32,24},{40,32},{48,40},{56,48},{64,5... | collective-permute-start | bytes 294920 | tf_op jit(solution)/shard_map/ppermute | solution.py:175
  36.7 5.6 %collective-permute-done = f16[8,48,128]{2,1,0:T(8,128)(2,1)S(1)} collective-permute-done((f16[8,48,128]{2,1,0:T(8,128)(2,1)S(1)}, f16[8,48,128]{2,1,0:T(8,128)(2,1)S(1)}, u32[]{:S(2)}, u32[]{:S(2)}) %collective-permute-start) | collective-permute-done | bytes 98336 | tf_op jit(solution)/shard_map/ppermute | solution.py:175
  42.3 1.5 %all-to-all-done.1 = f16[16,48,384]{2,1,0:T(8,128)(2,1)S(1)} async-done(((f16[16,48,384]{2,1,0:T(8,128)(2,1)}), f16[16,48,384]{2,1,0:T(8,128)(2,1)S(1)}, u32[]{:S(2)}, u32[]{:S(2)}) %all-to-all-start.1) | async-done | bytes 589856 | tf_op jit(solution)/shard_map/all_to_all | solution.py:204
  43.8 2.1 %convolution_convert_fusion.1 = f16[704,384]{1,0:T(8,128)(2,1)} fusion(bf16[704,768]{1,0:T(8,128)(2,1)S(1)} %fusion.3, f16[768,384]{1,0:T(8,128)(2,1)S(1)} %bitcast.46), kind=kOutput, calls=%fused_computation.7 | convolution fusion | flops 415506432 | bytes 2211840 | tf_op jit(solution)/shard_map/dot_general | solution.py:131
  46.0 3.5 %all-to-all-start.2 = ((f16[8,88,384]{2,1,0:T(8,128)(2,1)}), f16[8,88,384]{2,1,0:T(8,128)(2,1)S(1)}, u32[]{:S(2)}, u32[]{:S(2)}) async-start(f16[8,88,384]{2,1,0:T(8,128)(2,1)} %bitcast.9), calls=%async_computation.2 | async-start | bytes 1081344 | tf_op jit(solution)/shard_map/all_to_all | solution.py:218
  49.5 1.4 %collective-permute-start.1 = (f16[8,48,128]{2,1,0:T(8,128)(2,1)S(1)}, f16[8,48,128]{2,1,0:T(8,128)(2,1)S(1)}, u32[]{:S(2)}, u32[]{:S(2)}) collective-permute-start(f16[8,48,128]{2,1,0:T(8,128)(2,1)S(1)} %slice_bitcast_fusion.1), channel_id=1, source_target_pairs={{0,8},{8,16},{16,24},{24,32},{32,40},{40,48},{48,56},{56,64},{64,7... | collective-permute-start | bytes 294920 | tf_op jit(solution)/shard_map/ppermute | solution.py:176
  51.0 9.0 %all-to-all-done.2 = f16[8,88,384]{2,1,0:T(8,128)(2,1)S(1)} async-done(((f16[8,88,384]{2,1,0:T(8,128)(2,1)}), f16[8,88,384]{2,1,0:T(8,128)(2,1)S(1)}, u32[]{:S(2)}, u32[]{:S(2)}) %all-to-all-start.2) | async-done | bytes 540704 | tf_op jit(solution)/shard_map/all_to_all | solution.py:218
  60.3 1.2 %collective-permute-start.2 = (bf16[8,5376]{1,0:T(8,128)(2,1)S(1)}, bf16[8,5376]{1,0:T(8,128)(2,1)S(1)}, u32[]{:S(2)}, u32[]{:S(2)}) collective-permute-start(bf16[8,5376]{1,0:T(8,128)(2,1)S(1)} %bitcast.47), channel_id=1, source_target_pairs={{0,16},{1,65},{2,18},{3,67},{4,20},{5,69},{6,22},{7,71},{8,24},{9,... | collective-permute-start | bytes 258056 | tf_op jit(solution)/shard_map/ppermute | solution.py:257
  61.6 1.1 %collective-permute-start.3 = (bf16[8,5376]{1,0:T(8,128)(2,1)S(1)}, bf16[8,5376]{1,0:T(8,128)(2,1)S(1)}, u32[]{:S(2)}, u32[]{:S(2)}) collective-permute-start(bf16[8,5376]{1,0:T(8,128)(2,1)S(1)} %bitcast.48), channel_id=1, source_target_pairs={{0,8},{1,33},{2,10},{3,35},{4,12},{5,37},{6,14},{7,39},{8,16},{9,4... | collective-permute-start | bytes 258056 | tf_op jit(solution)/shard_map/ppermute | solution.py:257
  62.7 2.1 %collective-permute-start.4 = (bf16[8,5376]{1,0:T(8,128)(2,1)S(1)}, bf16[8,5376]{1,0:T(8,128)(2,1)S(1)}, u32[]{:S(2)}, u32[]{:S(2)}) collective-permute-start(bf16[8,5376]{1,0:T(8,128)(2,1)S(1)} %bitcast.49), channel_id=1, source_target_pairs={{0,24},{1,97},{2,26},{3,99},{4,28},{5,101},{6,30},{7,103},{8,0},{9... | collective-permute-start | bytes 258056 | tf_op jit(solution)/shard_map/ppermute | solution.py:257
  64.9 1.5 %collective-permute-done.2 = bf16[8,5376]{1,0:T(8,128)(2,1)S(1)} collective-permute-done((bf16[8,5376]{1,0:T(8,128)(2,1)S(1)}, bf16[8,5376]{1,0:T(8,128)(2,1)S(1)}, u32[]{:S(2)}, u32[]{:S(2)}) %collective-permute-start.2) | collective-permute-done | bytes 86048 | tf_op jit(solution)/shard_map/ppermute | solution.py:257
  66.4 0.9 %collective-permute-done.3 = bf16[8,5376]{1,0:T(8,128)(2,1)S(1)} collective-permute-done((bf16[8,5376]{1,0:T(8,128)(2,1)S(1)}, bf16[8,5376]{1,0:T(8,128)(2,1)S(1)}, u32[]{:S(2)}, u32[]{:S(2)}) %collective-permute-start.3) | collective-permute-done | bytes 86048 | tf_op jit(solution)/shard_map/ppermute | solution.py:257
  67.4 3.0 %collective-permute-start.5 = (bf16[4,8,5376]{2,1,0:T(8,128)(2,1)S(1)}, bf16[4,8,5376]{2,1,0:T(8,128)(2,1)S(1)}, u32[]{:S(2)}, u32[]{:S(2)}) collective-permute-start(bf16[4,8,5376]{2,1,0:T(8,128)(2,1)S(1)} %pad_maximum_fusion.refs_0_), channel_id=1, source_target_pairs={{0,64},{1,17},{2,66},{3,19},{4,68},{5,21},{6,70},{7,23},{8,72},{9,... | collective-permute-start | bytes 1032200 | tf_op jit(solution)/shard_map/ppermute | solution.py:257
  71.0 2.7 %collective-permute-start.7 = (bf16[4,8,5376]{2,1,0:T(8,128)(2,1)S(1)}, bf16[4,8,5376]{2,1,0:T(8,128)(2,1)S(1)}, u32[]{:S(2)}, u32[]{:S(2)}) collective-permute-start(bf16[4,8,5376]{2,1,0:T(8,128)(2,1)S(1)} %pad_maximum_fusion.refs_0_), channel_id=1, source_target_pairs={{0,96},{1,25},{2,98},{3,27},{4,100},{5,29},{6,102},{7,31},{8,104},... | collective-permute-start | bytes 1032200 | tf_op jit(solution)/shard_map/ppermute | solution.py:257
  73.7 2.0 %shard_map.103 = (f32[1,672,128]{2,1,0:T(8,128)}, f32[1,672,128]{2,1,0:T(8,128)}, f32[1,672,128]{2,1,0:T(8,128)}) custom-call(s32[3,128]{1,0:T(4,128)S(1)} %bitcast.42, f32[8,88,384]{2,1,0:T(8,128)S(1)} %convert_element_type.49.rows_ref, f32[1,672,128]{2,1,0:T(8,128)S(1)} %copy-done), custom_call_target="tpu_custom_call" | custom-call | tf_op jit(solution)/shard_map/pallas_call | solution.py:269
  76.3 3.6 %collective-permute-done.6.refs_2_ = bf16[4,8,5376]{2,1,0:T(8,128)(2,1)S(1)} collective-permute-done((bf16[4,8,5376]{2,1,0:T(8,128)(2,1)S(1)}, bf16[4,8,5376]{2,1,0:T(8,128)(2,1)S(1)}, u32[]{:S(2)}, u32[]{:S(2)}) %collective-permute-start.6) | collective-permute-done | bytes 344096 | tf_op jit(solution)/shard_map/ppermute | solution.py:257
  79.9 1.3 %shard_map.104 = bf16[16,8,5376]{2,1,0:T(8,128)(2,1)} custom-call(bf16[4,8,5376]{2,1,0:T(8,128)(2,1)S(1)} %pad_maximum_fusion.refs_0_, bf16[4,8,5376]{2,1,0:T(8,128)(2,1)S(1)} %collective-permute-done.5.refs_1_, bf16[4,8,5376]{2,1,0:T(8,128)(2,1)S(1)} %collective-permute-done.6.refs_2_, bf16[4,8,5376]{2,1,0:T(8,128)(2,1)S(1)} %collective-permute-done.7.refs_3_), custom_call_target="tpu_custom_call" | custom-call | tf_op jit(solution)/shard_map/pallas_call | solution.py:261
  (72 shorter events, 4.1 us)
Async XLA Ops:
  2.0 9.2 %copy-start.1 = (s32[128,3]{0,1:T(4,128)S(1)}, s32[128,3]{0,1:T(4,128)}, u32[]{:S(2)}) copy-start(s32[128,3]{0,1:T(4,128)} %param.12) | copy-start | bytes 4612
  2.0 9.3 %copy-start.2 = (s32[128,3]{0,1:T(4,128)S(1)}, s32[128,3]{0,1:T(4,128)}, u32[]{:S(2)}) copy-start(s32[128,3]{0,1:T(4,128)} %param.11) | copy-start | bytes 4612
  2.0 9.7 %copy-start.3 = (s32[112]{0:T(128)S(1)}, s32[112]{0:T(128)}, u32[]{:S(2)}) copy-start(s32[112]{0:T(128)} %param.13) | copy-start | bytes 1348
  3.0 20.1 %all-to-all-start = ((f16[32,24,384]{2,1,0:T(8,128)(2,1)}), f16[32,24,384]{2,1,0:T(8,128)(2,1)S(1)}, u32[]{:S(2)}, u32[]{:S(2)}) async-start(f16[32,24,384]{2,1,0:T(8,128)(2,1)} %convert_element_type.45), calls=%async_computation | async-start | bytes 1179648 | tf_op jit(solution)/shard_map/all_to_all | solution.py:171
  25.2 18.6 %all-to-all-start.1 = ((f16[16,48,384]{2,1,0:T(8,128)(2,1)}), f16[16,48,384]{2,1,0:T(8,128)(2,1)S(1)}, u32[]{:S(2)}, u32[]{:S(2)}) async-start(f16[16,48,384]{2,1,0:T(8,128)(2,1)} %bitcast.6), calls=%async_computation.1 | async-start | bytes 1179648 | tf_op jit(solution)/shard_map/all_to_all | solution.py:204
  31.2 11.2 %collective-permute-start = (f16[8,48,128]{2,1,0:T(8,128)(2,1)S(1)}, f16[8,48,128]{2,1,0:T(8,128)(2,1)S(1)}, u32[]{:S(2)}, u32[]{:S(2)}) collective-permute-start(f16[8,48,128]{2,1,0:T(8,128)(2,1)S(1)} %slice_bitcast_fusion.1), channel_id=1, source_target_pairs={{0,120},{8,0},{16,8},{24,16},{32,24},{40,32},{48,40},{56,48},{64,5... | collective-permute-start | bytes 294920 | tf_op jit(solution)/shard_map/ppermute | solution.py:175
  46.0 14.0 %all-to-all-start.2 = ((f16[8,88,384]{2,1,0:T(8,128)(2,1)}), f16[8,88,384]{2,1,0:T(8,128)(2,1)S(1)}, u32[]{:S(2)}, u32[]{:S(2)}) async-start(f16[8,88,384]{2,1,0:T(8,128)(2,1)} %bitcast.9), calls=%async_computation.2 | async-start | bytes 1081344 | tf_op jit(solution)/shard_map/all_to_all | solution.py:218
  49.5 10.5 %collective-permute-start.1 = (f16[8,48,128]{2,1,0:T(8,128)(2,1)S(1)}, f16[8,48,128]{2,1,0:T(8,128)(2,1)S(1)}, u32[]{:S(2)}, u32[]{:S(2)}) collective-permute-start(f16[8,48,128]{2,1,0:T(8,128)(2,1)S(1)} %slice_bitcast_fusion.1), channel_id=1, source_target_pairs={{0,8},{8,16},{16,24},{24,32},{32,40},{40,48},{48,56},{56,64},{64,7... | collective-permute-start | bytes 294920 | tf_op jit(solution)/shard_map/ppermute | solution.py:176
  60.3 6.1 %collective-permute-start.2 = (bf16[8,5376]{1,0:T(8,128)(2,1)S(1)}, bf16[8,5376]{1,0:T(8,128)(2,1)S(1)}, u32[]{:S(2)}, u32[]{:S(2)}) collective-permute-start(bf16[8,5376]{1,0:T(8,128)(2,1)S(1)} %bitcast.47), channel_id=1, source_target_pairs={{0,16},{1,65},{2,18},{3,67},{4,20},{5,69},{6,22},{7,71},{8,24},{9,... | collective-permute-start | bytes 258056 | tf_op jit(solution)/shard_map/ppermute | solution.py:257
  61.6 5.7 %collective-permute-start.3 = (bf16[8,5376]{1,0:T(8,128)(2,1)S(1)}, bf16[8,5376]{1,0:T(8,128)(2,1)S(1)}, u32[]{:S(2)}, u32[]{:S(2)}) collective-permute-start(bf16[8,5376]{1,0:T(8,128)(2,1)S(1)} %bitcast.48), channel_id=1, source_target_pairs={{0,8},{1,33},{2,10},{3,35},{4,12},{5,37},{6,14},{7,39},{8,16},{9,4... | collective-permute-start | bytes 258056 | tf_op jit(solution)/shard_map/ppermute | solution.py:257
  62.7 4.6 %collective-permute-start.4 = (bf16[8,5376]{1,0:T(8,128)(2,1)S(1)}, bf16[8,5376]{1,0:T(8,128)(2,1)S(1)}, u32[]{:S(2)}, u32[]{:S(2)}) collective-permute-start(bf16[8,5376]{1,0:T(8,128)(2,1)S(1)} %bitcast.49), channel_id=1, source_target_pairs={{0,24},{1,97},{2,26},{3,99},{4,28},{5,101},{6,30},{7,103},{8,0},{9... | collective-permute-start | bytes 258056 | tf_op jit(solution)/shard_map/ppermute | solution.py:257
  64.9 8.8 %copy-start = (f32[1,672,128]{2,1,0:T(8,128)S(1)}, f32[1,672,128]{2,1,0:T(8,128)}, u32[]{:S(2)}) copy-start(f32[1,672,128]{2,1,0:T(8,128)} %g_ref.3) | copy-start | bytes 1032196
  67.4 8.9 %collective-permute-start.5 = (bf16[4,8,5376]{2,1,0:T(8,128)(2,1)S(1)}, bf16[4,8,5376]{2,1,0:T(8,128)(2,1)S(1)}, u32[]{:S(2)}, u32[]{:S(2)}) collective-permute-start(bf16[4,8,5376]{2,1,0:T(8,128)(2,1)S(1)} %pad_maximum_fusion.refs_0_), channel_id=1, source_target_pairs={{0,64},{1,17},{2,66},{3,19},{4,68},{5,21},{6,70},{7,23},{8,72},{9,... | collective-permute-start | bytes 1032200 | tf_op jit(solution)/shard_map/ppermute | solution.py:257
  70.4 9.5 %collective-permute-start.6 = (bf16[4,8,5376]{2,1,0:T(8,128)(2,1)S(1)}, bf16[4,8,5376]{2,1,0:T(8,128)(2,1)S(1)}, u32[]{:S(2)}, u32[]{:S(2)}) collective-permute-start(bf16[4,8,5376]{2,1,0:T(8,128)(2,1)S(1)} %pad_maximum_fusion.refs_0_), channel_id=1, source_target_pairs={{0,32},{1,9},{2,34},{3,11},{4,36},{5,13},{6,38},{7,15},{8,40},{9,1... | collective-permute-start | bytes 1032200 | tf_op jit(solution)/shard_map/ppermute | solution.py:257
  71.0 9.0 %collective-permute-start.7 = (bf16[4,8,5376]{2,1,0:T(8,128)(2,1)S(1)}, bf16[4,8,5376]{2,1,0:T(8,128)(2,1)S(1)}, u32[]{:S(2)}, u32[]{:S(2)}) collective-permute-start(bf16[4,8,5376]{2,1,0:T(8,128)(2,1)S(1)} %pad_maximum_fusion.refs_0_), channel_id=1, source_target_pairs={{0,96},{1,25},{2,98},{3,27},{4,100},{5,29},{6,102},{7,31},{8,104},... | collective-permute-start | bytes 1032200 | tf_op jit(solution)/shard_map/ppermute | solution.py:257

commit v7 on v6

--- a/solution.py
+++ b/solution.py
@@ -47,46 +47,45 @@
 
 
 def pack_kernel(
-    old_hbm, new_hbm, w_ref, m_ref, v_ref, g_ref, out_ref, gout_ref, info_ref,
-    scratch, old_ref, new_ref, sems,
+    old_hbm, w_ref, m_ref, v_ref, out_ref, scratch, old_ref, sems
 ):
-    tables = [
-        pltpu.make_async_copy(old_hbm, old_ref, sems.at[4]),
-        pltpu.make_async_copy(new_hbm, new_ref, sems.at[5]),
-    ]
-    for copy in tables:
-        copy.start()
+    table = pltpu.make_async_copy(old_hbm, old_ref, sems.at[3])
+    table.start()
     copies = [
         pltpu.make_async_copy(ref.at[0], scratch.at[s, pl.ds(0, SLOT)], sems.at[s])
-        for s, ref in enumerate((g_ref, w_ref, m_ref, v_ref))
+        for s, ref in enumerate((w_ref, m_ref, v_ref))
     ]
     for copy in copies:
         copy.start()
-    for copy in tables:
-        copy.wait()
+    table.wait()
     dp = lax.axis_index("y") * 4 + lax.axis_index("x")
     tp = lax.axis_index("z") * 2 + lax.axis_index("c")
     old_start = lax.rem(old_ref[1, dp * 8 + tp], SLOT)
+    for s, copy in enumerate(copies):
+        copy.wait()
+        scratch[s, pl.ds(SLOT, QPAD), :] = scratch[s, pl.ds(0, QPAD), :]
+        scale = (SCALE_W, SCALE_M, SCALE_V)[s]
+        for hq in range(4):
+            for t in range(8):
+                offset = wrap(t * ROW_OLD + hq * QUART - old_start)
+                piece = scratch[s, pl.ds(offset, QPAD), :]
+                out_ref[hq * 8 + t, :, pl.ds(s * LANES, LANES)] = piece * scale
+
+
+def grad_kernel(new_ref, g_ref, gout_ref, info_ref, scratch):
+    dp = lax.axis_index("y") * 4 + lax.axis_index("x")
+    tp = lax.axis_index("z") * 2 + lax.axis_index("c")
     new_start = new_ref[1, dp * 8 + tp]
     new_place = lax.rem(new_start - dp * UNIT, SLOT)
     above = lax.rem(dp + 1, 16)
     info_ref[0] = jnp.full((8, LANES), new_ref[1, above * 8 + tp] - above * UNIT, jnp.int32)
     info_ref[1] = jnp.full((8, LANES), new_start - above * UNIT, jnp.int32)
-    for s, copy in enumerate(copies):
-        copy.wait()
-        scratch[s, pl.ds(SLOT, RPAD), :] = scratch[s, pl.ds(0, RPAD), :]
-        if s == 0:
-            for half in range(2):
-                for t in range(8):
-                    offset = wrap(half * UNIT + t * ROW_NEW - new_place)
-                    gout_ref[half, t] = scratch[0, pl.ds(offset, RPAD), :] * SCALE_G
-            continue
-        scale = (SCALE_W, SCALE_M, SCALE_V)[s - 1]
-        for hq in range(4):
-            for t in range(8):
-                offset = wrap(t * ROW_OLD + hq * QUART - old_start)
-                piece = scratch[s, pl.ds(offset, QPAD), :]
-                out_ref[hq * 8 + t, :, pl.ds((s - 1) * LANES, LANES)] = piece * scale
+    scratch[pl.ds(0, SLOT), :] = g_ref[0]
+    scratch[pl.ds(SLOT, RPAD), :] = g_ref[0, pl.ds(0, RPAD), :]
+    for half in range(2):
+        for t in range(8):
+            offset = wrap(half * UNIT + t * ROW_NEW - new_place)
+            gout_ref[half, t] = scratch[pl.ds(offset, RPAD), :] * SCALE_G
 
 
 def owner_kernel(new_ref, rows_ref, g_ref, w_out, m_out, v_out, scratch):
@@ -148,22 +147,28 @@
     vmem = pl.BlockSpec(memory_space=pltpu.VMEM)
     smem = pl.BlockSpec(memory_space=pltpu.SMEM)
     hbm = pl.BlockSpec(memory_space=pltpu.HBM)
-    packed, grad_rows, info = pl.pallas_call(
+    packed = pl.pallas_call(
         pack_kernel,
+        out_shape=pltpu.VMEM((32, QPAD, 3 * LANES), jnp.float32),
+        in_specs=[hbm] * 4,
+        out_specs=vmem,
+        scratch_shapes=[
+            pltpu.VMEM((3, SLOT + RPAD, LANES), jnp.float32),
+            pltpu.SMEM((3, 128), jnp.int32),
+            pltpu.SemaphoreType.DMA((4,)),
+        ],
+    )(old_table.T, old_master, old_avg, old_sq)
+    grad_rows, info = pl.pallas_call(
+        grad_kernel,
         out_shape=(
-            pltpu.VMEM((32, QPAD, 3 * LANES), jnp.float32),
-            pltpu.VMEM((2, 8, RPAD, LANES), jnp.float32),
-            pltpu.VMEM((2, 8, LANES), jnp.int32),
+            jax.ShapeDtypeStruct((2, 8, RPAD, LANES), jnp.float32),
+            jax.ShapeDtypeStruct((2, 8, LANES), jnp.int32),
         ),
-        in_specs=[hbm] * 6,
-        out_specs=(vmem, vmem, vmem),
-        scratch_shapes=[
-            pltpu.VMEM((4, SLOT + RPAD, LANES), jnp.float32),
-            pltpu.SMEM((3, 128), jnp.int32),
-            pltpu.SMEM((3, 128), jnp.int32),
-            pltpu.SemaphoreType.DMA((6,)),
-        ],
-    )(old_table.T, new_table.T, old_master, old_avg, old_sq, grad)
+        in_specs=[smem, vmem],
+        out_specs=(vmem, vmem),
+        scratch_shapes=[pltpu.VMEM((SLOT + RPAD, LANES), jnp.float32)],
+        compiler_params=pltpu.CompilerParams(vmem_limit_bytes=16 * 1024 * 1024),
+    )(new_table.T, grad)
 
     up = [(i, (i + 1) % 16) for i in range(16)]
     down = [(i, (i - 1) % 16) for i in range(16)]

time: 82 us -> 81.8 us (level)
    pallas_call x1 -> x2, Pallas kernels: 1.38 us -> 1.9 us  [the longest x1 1.26 us: on_device(): pl.pallas_call(pack_kernel, out_shape=pltpu.VMEM((32, QPAD, 3 * LANES), j...]
  transfers between devices with their start and end apart: 11 -> 11, of which waited for: 8 -> 8; matrix products, arithmetic and copies ran while one was open for 4% -> 4% of each run, Pallas kernels for 2% -> 3%
where the time goes in v7:
time: 81.8 us; the launch traced here: 81.1 us
  starting transfers between devices  35 us (43%)
  waiting for transfers between devices  30.7 us (38%)
  Pallas kernels  5.18 us (6%)
  matrix products  4.32 us (5%)
  other arithmetic  3.36 us (4%)
  local copies, waits for them, and re-layouts  1.46 us (2%)
  between operations  1 us (1%)
    ppermute x6, starting transfers between devices, turn(): lax.ppermute(value, ('y', 'x', 'z', 'c'), moves(by, first))  10.7 us
    all_to_all x1, waiting for transfers between devices, on_device(): lax.all_to_all(heads.reshape(8, PAIR, 3 * LANES), ('z', 'c'), 0, 0, tiled...  8.97 us
    all_to_all x1, starting transfers between devices, on_device(): lax.all_to_all(packed.astype(f16), ('x', 'z', 'c'), 0, 0, tiled=True)  8.25 us
    all_to_all x1, waiting for transfers between devices, on_device(): lax.all_to_all(packed.astype(f16), ('x', 'z', 'c'), 0, 0, tiled=True)  7.95 us
    ppermute x6, waiting for transfers between devices, turn(): lax.ppermute(value, ('y', 'x', 'z', 'c'), moves(by, first))  6.68 us
    all_to_all x1, starting transfers between devices, on_device(): lax.all_to_all(rows.reshape(16, 2 * QPAD, 3 * LANES), ('y', 'x'), 0, 0, t...  5.77 us
    ppermute x1, waiting for transfers between devices, on_device(): grad_first = lax.ppermute(grad_send[0], ('y', 'x'), down)  5.59 us
    ppermute x1, starting transfers between devices, on_device(): grad_first = lax.ppermute(grad_send[0], ('y', 'x'), down)  5.32 us
  transfers between devices with their start and end apart: 11, of which 8 were waited for; matrix products, arithmetic and copies ran while one was open for 4% of the time, Pallas kernels for 3%

profile of v7, /device:TPU:0, one launch (start us, length us, event | category | flops | bytes accessed | tf_op | source)
XLA Modules:
  0.0 81.1 jit_solution(3859118080149594141)
XLA Ops:
  0.6 1.3 %shard_map.103 = f32[32,24,384]{2,1,0:T(8,128)S(1)} custom-call(s32[3,128]{1,0:T(4,128)} %bitcast.53, f32[1,672,128]{2,1,0:T(8,128)} %w_ref.1, f32[1,672,128]{2,1,0:T(8,128)} %m_ref.1, f32[1,672,128]{2,1,0:T(8,128)} %v_ref.1), custom_call_target="tpu_custom_call" | custom-call | tf_op jit(solution)/shard_map/pallas_call | solution.py:150
  1.9 0.9 %convert_element_type.45 = f16[32,24,384]{2,1,0:T(8,128)(2,1)} convert(f32[32,24,384]{2,1,0:T(8,128)S(1)} %shard_map.103) | non-fusion elementwise | flops 294912 | bytes 1769472 | tf_op jit(solution)/shard_map/convert_element_type | solution.py:176
  2.8 8.2 %all-to-all-start = ((f16[32,24,384]{2,1,0:T(8,128)(2,1)}), f16[32,24,384]{2,1,0:T(8,128)(2,1)S(1)}, u32[]{:S(2)}, u32[]{:S(2)}) async-start(f16[32,24,384]{2,1,0:T(8,128)(2,1)} %convert_element_type.45), calls=%async_computation | async-start | bytes 1179648 | tf_op jit(solution)/shard_map/all_to_all | solution.py:176
  12.8 1.0 %fusion.2 = bf16[768,768]{1,0:T(8,128)(2,1)S(1)} fusion(s32[768]{0:T(1024)S(1)} %add.247, s32[768]{0:T(1024)S(1)} %ge.62, s32[768]{0:T(1024)S(1)} %get-tuple-element.35, s32[768]{0:T(1024)S(1)} %get-tuple-element.36, s32[768]{0:T(1024)S(1)} %reshape.306, pred[768]{0:T(1024)(128)(4,1)S(1)} %fusion.26), kind=kLoop, calls=%fused_computation.3 | loop fusion | flops 4718592 | bytes 1195776 | tf_op jit(solution)/shard_map/convert_element_type | solution.py:206
  14.9 7.9 %all-to-all-done = f16[32,24,384]{2,1,0:T(8,128)(2,1)S(1)} async-done(((f16[32,24,384]{2,1,0:T(8,128)(2,1)}), f16[32,24,384]{2,1,0:T(8,128)(2,1)S(1)}, u32[]{:S(2)}, u32[]{:S(2)}) %all-to-all-start) | async-done | bytes 589856 | tf_op jit(solution)/shard_map/all_to_all | solution.py:176
  22.9 2.2 %convolution_convert_fusion = f16[768,384]{1,0:T(8,128)(2,1)} fusion(bf16[768,768]{1,0:T(8,128)(2,1)S(1)} %fusion.2, f16[768,384]{1,0:T(8,128)(2,1)S(1)} %bitcast.45), kind=kOutput, calls=%fused_computation.6 | convolution fusion | flops 453279744 | bytes 2359296 | tf_op jit(solution)/shard_map/dot_general | solution.py:130
  25.1 5.8 %all-to-all-start.1 = ((f16[16,48,384]{2,1,0:T(8,128)(2,1)}), f16[16,48,384]{2,1,0:T(8,128)(2,1)S(1)}, u32[]{:S(2)}, u32[]{:S(2)}) async-start(f16[16,48,384]{2,1,0:T(8,128)(2,1)} %bitcast.6), calls=%async_computation.1 | async-start | bytes 1179648 | tf_op jit(solution)/shard_map/all_to_all | solution.py:209
  31.1 5.3 %collective-permute-start = (f16[8,48,128]{2,1,0:T(8,128)(2,1)S(1)}, f16[8,48,128]{2,1,0:T(8,128)(2,1)S(1)}, u32[]{:S(2)}, u32[]{:S(2)}) collective-permute-start(f16[8,48,128]{2,1,0:T(8,128)(2,1)S(1)} %slice_bitcast_fusion.1), channel_id=1, source_target_pairs={{0,120},{8,0},{16,8},{24,16},{32,24},{40,32},{48,40},{56,48},{64,5... | collective-permute-start | bytes 294920 | tf_op jit(solution)/shard_map/ppermute | solution.py:180
  36.6 5.6 %collective-permute-done = f16[8,48,128]{2,1,0:T(8,128)(2,1)S(1)} collective-permute-done((f16[8,48,128]{2,1,0:T(8,128)(2,1)S(1)}, f16[8,48,128]{2,1,0:T(8,128)(2,1)S(1)}, u32[]{:S(2)}, u32[]{:S(2)}) %collective-permute-start) | collective-permute-done | bytes 98336 | tf_op jit(solution)/shard_map/ppermute | solution.py:180
  42.2 1.5 %all-to-all-done.1 = f16[16,48,384]{2,1,0:T(8,128)(2,1)S(1)} async-done(((f16[16,48,384]{2,1,0:T(8,128)(2,1)}), f16[16,48,384]{2,1,0:T(8,128)(2,1)S(1)}, u32[]{:S(2)}, u32[]{:S(2)}) %all-to-all-start.1) | async-done | bytes 589856 | tf_op jit(solution)/shard_map/all_to_all | solution.py:209
  43.7 2.1 %convolution_convert_fusion.1 = f16[704,384]{1,0:T(8,128)(2,1)} fusion(bf16[704,768]{1,0:T(8,128)(2,1)S(1)} %fusion.3, f16[768,384]{1,0:T(8,128)(2,1)S(1)} %bitcast.46), kind=kOutput, calls=%fused_computation.7 | convolution fusion | flops 415506432 | bytes 2211840 | tf_op jit(solution)/shard_map/dot_general | solution.py:130
  45.8 3.5 %all-to-all-start.2 = ((f16[8,88,384]{2,1,0:T(8,128)(2,1)}), f16[8,88,384]{2,1,0:T(8,128)(2,1)S(1)}, u32[]{:S(2)}, u32[]{:S(2)}) async-start(f16[8,88,384]{2,1,0:T(8,128)(2,1)} %bitcast.9), calls=%async_computation.2 | async-start | bytes 1081344 | tf_op jit(solution)/shard_map/all_to_all | solution.py:223
  49.4 1.4 %collective-permute-start.1 = (f16[8,48,128]{2,1,0:T(8,128)(2,1)S(1)}, f16[8,48,128]{2,1,0:T(8,128)(2,1)S(1)}, u32[]{:S(2)}, u32[]{:S(2)}) collective-permute-start(f16[8,48,128]{2,1,0:T(8,128)(2,1)S(1)} %slice_bitcast_fusion.1), channel_id=1, source_target_pairs={{0,8},{8,16},{16,24},{24,32},{32,40},{40,48},{48,56},{56,64},{64,7... | collective-permute-start | bytes 294920 | tf_op jit(solution)/shard_map/ppermute | solution.py:181
  50.8 9.0 %all-to-all-done.2 = f16[8,88,384]{2,1,0:T(8,128)(2,1)S(1)} async-done(((f16[8,88,384]{2,1,0:T(8,128)(2,1)}), f16[8,88,384]{2,1,0:T(8,128)(2,1)S(1)}, u32[]{:S(2)}, u32[]{:S(2)}) %all-to-all-start.2) | async-done | bytes 540704 | tf_op jit(solution)/shard_map/all_to_all | solution.py:223
  60.2 1.2 %collective-permute-start.2 = (bf16[8,5376]{1,0:T(8,128)(2,1)S(1)}, bf16[8,5376]{1,0:T(8,128)(2,1)S(1)}, u32[]{:S(2)}, u32[]{:S(2)}) collective-permute-start(bf16[8,5376]{1,0:T(8,128)(2,1)S(1)} %bitcast.47), channel_id=1, source_target_pairs={{0,16},{1,65},{2,18},{3,67},{4,20},{5,69},{6,22},{7,71},{8,24},{9,... | collective-permute-start | bytes 258056 | tf_op jit(solution)/shard_map/ppermute | solution.py:262
  61.5 1.1 %collective-permute-start.3 = (bf16[8,5376]{1,0:T(8,128)(2,1)S(1)}, bf16[8,5376]{1,0:T(8,128)(2,1)S(1)}, u32[]{:S(2)}, u32[]{:S(2)}) collective-permute-start(bf16[8,5376]{1,0:T(8,128)(2,1)S(1)} %bitcast.48), channel_id=1, source_target_pairs={{0,8},{1,33},{2,10},{3,35},{4,12},{5,37},{6,14},{7,39},{8,16},{9,4... | collective-permute-start | bytes 258056 | tf_op jit(solution)/shard_map/ppermute | solution.py:262
  62.6 2.1 %collective-permute-start.4 = (bf16[8,5376]{1,0:T(8,128)(2,1)S(1)}, bf16[8,5376]{1,0:T(8,128)(2,1)S(1)}, u32[]{:S(2)}, u32[]{:S(2)}) collective-permute-start(bf16[8,5376]{1,0:T(8,128)(2,1)S(1)} %bitcast.49), channel_id=1, source_target_pairs={{0,24},{1,97},{2,26},{3,99},{4,28},{5,101},{6,30},{7,103},{8,0},{9... | collective-permute-start | bytes 258056 | tf_op jit(solution)/shard_map/ppermute | solution.py:262
  64.7 1.5 %collective-permute-done.2 = bf16[8,5376]{1,0:T(8,128)(2,1)S(1)} collective-permute-done((bf16[8,5376]{1,0:T(8,128)(2,1)S(1)}, bf16[8,5376]{1,0:T(8,128)(2,1)S(1)}, u32[]{:S(2)}, u32[]{:S(2)}) %collective-permute-start.2) | collective-permute-done | bytes 86048 | tf_op jit(solution)/shard_map/ppermute | solution.py:262
  66.3 0.9 %collective-permute-done.3 = bf16[8,5376]{1,0:T(8,128)(2,1)S(1)} collective-permute-done((bf16[8,5376]{1,0:T(8,128)(2,1)S(1)}, bf16[8,5376]{1,0:T(8,128)(2,1)S(1)}, u32[]{:S(2)}, u32[]{:S(2)}) %collective-permute-start.3) | collective-permute-done | bytes 86048 | tf_op jit(solution)/shard_map/ppermute | solution.py:262
  67.3 3.0 %collective-permute-start.5 = (bf16[4,8,5376]{2,1,0:T(8,128)(2,1)S(1)}, bf16[4,8,5376]{2,1,0:T(8,128)(2,1)S(1)}, u32[]{:S(2)}, u32[]{:S(2)}) collective-permute-start(bf16[4,8,5376]{2,1,0:T(8,128)(2,1)S(1)} %pad_maximum_fusion.refs_0_), channel_id=1, source_target_pairs={{0,64},{1,17},{2,66},{3,19},{4,68},{5,21},{6,70},{7,23},{8,72},{9,... | collective-permute-start | bytes 1032200 | tf_op jit(solution)/shard_map/ppermute | solution.py:262
  70.8 2.7 %collective-permute-start.7 = (bf16[4,8,5376]{2,1,0:T(8,128)(2,1)S(1)}, bf16[4,8,5376]{2,1,0:T(8,128)(2,1)S(1)}, u32[]{:S(2)}, u32[]{:S(2)}) collective-permute-start(bf16[4,8,5376]{2,1,0:T(8,128)(2,1)S(1)} %pad_maximum_fusion.refs_0_), channel_id=1, source_target_pairs={{0,96},{1,25},{2,98},{3,27},{4,100},{5,29},{6,102},{7,31},{8,104},... | collective-permute-start | bytes 1032200 | tf_op jit(solution)/shard_map/ppermute | solution.py:262
  73.6 2.0 %shard_map.104 = (f32[1,672,128]{2,1,0:T(8,128)}, f32[1,672,128]{2,1,0:T(8,128)}, f32[1,672,128]{2,1,0:T(8,128)}) custom-call(s32[3,128]{1,0:T(4,128)S(1)} %bitcast.42, f32[8,88,384]{2,1,0:T(8,128)S(1)} %convert_element_type.49.rows_ref, f32[1,672,128]{2,1,0:T(8,128)S(1)} %copy-done), custom_call_target="tpu_custom_call" | custom-call | tf_op jit(solution)/shard_map/pallas_call | solution.py:274
  76.2 3.6 %collective-permute-done.6.refs_2_ = bf16[4,8,5376]{2,1,0:T(8,128)(2,1)S(1)} collective-permute-done((bf16[4,8,5376]{2,1,0:T(8,128)(2,1)S(1)}, bf16[4,8,5376]{2,1,0:T(8,128)(2,1)S(1)}, u32[]{:S(2)}, u32[]{:S(2)}) %collective-permute-start.6) | collective-permute-done | bytes 344096 | tf_op jit(solution)/shard_map/ppermute | solution.py:262
  79.8 1.3 %shard_map.105 = bf16[16,8,5376]{2,1,0:T(8,128)(2,1)} custom-call(bf16[4,8,5376]{2,1,0:T(8,128)(2,1)S(1)} %pad_maximum_fusion.refs_0_, bf16[4,8,5376]{2,1,0:T(8,128)(2,1)S(1)} %collective-permute-done.5.refs_1_, bf16[4,8,5376]{2,1,0:T(8,128)(2,1)S(1)} %collective-permute-done.6.refs_2_, bf16[4,8,5376]{2,1,0:T(8,128)(2,1)S(1)} %collective-permute-done.7.refs_3_), custom_call_target="tpu_custom_call" | custom-call | tf_op jit(solution)/shard_map/pallas_call | solution.py:266
  (73 shorter events, 4.8 us)
Async XLA Ops:
  1.9 9.3 %copy-start.2 = (s32[128,3]{0,1:T(4,128)S(1)}, s32[128,3]{0,1:T(4,128)}, u32[]{:S(2)}) copy-start(s32[128,3]{0,1:T(4,128)} %param.11) | copy-start | bytes 4612
  1.9 9.7 %copy-start.3 = (s32[112]{0:T(128)S(1)}, s32[112]{0:T(128)}, u32[]{:S(2)}) copy-start(s32[112]{0:T(128)} %param.13) | copy-start | bytes 1348
  1.9 10.0 %copy-start.1 = (s32[128,3]{0,1:T(4,128)S(1)}, s32[128,3]{0,1:T(4,128)}, u32[]{:S(2)}) copy-start(s32[128,3]{0,1:T(4,128)} %param.12) | copy-start | bytes 4612
  2.8 20.1 %all-to-all-start = ((f16[32,24,384]{2,1,0:T(8,128)(2,1)}), f16[32,24,384]{2,1,0:T(8,128)(2,1)S(1)}, u32[]{:S(2)}, u32[]{:S(2)}) async-start(f16[32,24,384]{2,1,0:T(8,128)(2,1)} %convert_element_type.45), calls=%async_computation | async-start | bytes 1179648 | tf_op jit(solution)/shard_map/all_to_all | solution.py:176
  11.1 3.2 %copy-start = (f32[1,672,128]{2,1,0:T(8,128)S(1)}, f32[1,672,128]{2,1,0:T(8,128)}, u32[]{:S(2)}) copy-start(f32[1,672,128]{2,1,0:T(8,128)} %g_ref.3) | copy-start | bytes 1032196
  25.1 18.6 %all-to-all-start.1 = ((f16[16,48,384]{2,1,0:T(8,128)(2,1)}), f16[16,48,384]{2,1,0:T(8,128)(2,1)S(1)}, u32[]{:S(2)}, u32[]{:S(2)}) async-start(f16[16,48,384]{2,1,0:T(8,128)(2,1)} %bitcast.6), calls=%async_computation.1 | async-start | bytes 1179648 | tf_op jit(solution)/shard_map/all_to_all | solution.py:209
  31.1 11.2 %collective-permute-start = (f16[8,48,128]{2,1,0:T(8,128)(2,1)S(1)}, f16[8,48,128]{2,1,0:T(8,128)(2,1)S(1)}, u32[]{:S(2)}, u32[]{:S(2)}) collective-permute-start(f16[8,48,128]{2,1,0:T(8,128)(2,1)S(1)} %slice_bitcast_fusion.1), channel_id=1, source_target_pairs={{0,120},{8,0},{16,8},{24,16},{32,24},{40,32},{48,40},{56,48},{64,5... | collective-permute-start | bytes 294920 | tf_op jit(solution)/shard_map/ppermute | solution.py:180
  45.8 14.0 %all-to-all-start.2 = ((f16[8,88,384]{2,1,0:T(8,128)(2,1)}), f16[8,88,384]{2,1,0:T(8,128)(2,1)S(1)}, u32[]{:S(2)}, u32[]{:S(2)}) async-start(f16[8,88,384]{2,1,0:T(8,128)(2,1)} %bitcast.9), calls=%async_computation.2 | async-start | bytes 1081344 | tf_op jit(solution)/shard_map/all_to_all | solution.py:223
  49.4 10.5 %collective-permute-start.1 = (f16[8,48,128]{2,1,0:T(8,128)(2,1)S(1)}, f16[8,48,128]{2,1,0:T(8,128)(2,1)S(1)}, u32[]{:S(2)}, u32[]{:S(2)}) collective-permute-start(f16[8,48,128]{2,1,0:T(8,128)(2,1)S(1)} %slice_bitcast_fusion.1), channel_id=1, source_target_pairs={{0,8},{8,16},{16,24},{24,32},{32,40},{40,48},{48,56},{56,64},{64,7... | collective-permute-start | bytes 294920 | tf_op jit(solution)/shard_map/ppermute | solution.py:181
  60.2 6.1 %collective-permute-start.2 = (bf16[8,5376]{1,0:T(8,128)(2,1)S(1)}, bf16[8,5376]{1,0:T(8,128)(2,1)S(1)}, u32[]{:S(2)}, u32[]{:S(2)}) collective-permute-start(bf16[8,5376]{1,0:T(8,128)(2,1)S(1)} %bitcast.47), channel_id=1, source_target_pairs={{0,16},{1,65},{2,18},{3,67},{4,20},{5,69},{6,22},{7,71},{8,24},{9,... | collective-permute-start | bytes 258056 | tf_op jit(solution)/shard_map/ppermute | solution.py:262
  61.5 5.7 %collective-permute-start.3 = (bf16[8,5376]{1,0:T(8,128)(2,1)S(1)}, bf16[8,5376]{1,0:T(8,128)(2,1)S(1)}, u32[]{:S(2)}, u32[]{:S(2)}) collective-permute-start(bf16[8,5376]{1,0:T(8,128)(2,1)S(1)} %bitcast.48), channel_id=1, source_target_pairs={{0,8},{1,33},{2,10},{3,35},{4,12},{5,37},{6,14},{7,39},{8,16},{9,4... | collective-permute-start | bytes 258056 | tf_op jit(solution)/shard_map/ppermute | solution.py:262
  62.6 4.6 %collective-permute-start.4 = (bf16[8,5376]{1,0:T(8,128)(2,1)S(1)}, bf16[8,5376]{1,0:T(8,128)(2,1)S(1)}, u32[]{:S(2)}, u32[]{:S(2)}) collective-permute-start(bf16[8,5376]{1,0:T(8,128)(2,1)S(1)} %bitcast.49), channel_id=1, source_target_pairs={{0,24},{1,97},{2,26},{3,99},{4,28},{5,101},{6,30},{7,103},{8,0},{9... | collective-permute-start | bytes 258056 | tf_op jit(solution)/shard_map/ppermute | solution.py:262
  67.3 8.9 %collective-permute-start.5 = (bf16[4,8,5376]{2,1,0:T(8,128)(2,1)S(1)}, bf16[4,8,5376]{2,1,0:T(8,128)(2,1)S(1)}, u32[]{:S(2)}, u32[]{:S(2)}) collective-permute-start(bf16[4,8,5376]{2,1,0:T(8,128)(2,1)S(1)} %pad_maximum_fusion.refs_0_), channel_id=1, source_target_pairs={{0,64},{1,17},{2,66},{3,19},{4,68},{5,21},{6,70},{7,23},{8,72},{9,... | collective-permute-start | bytes 1032200 | tf_op jit(solution)/shard_map/ppermute | solution.py:262
  70.3 9.5 %collective-permute-start.6 = (bf16[4,8,5376]{2,1,0:T(8,128)(2,1)S(1)}, bf16[4,8,5376]{2,1,0:T(8,128)(2,1)S(1)}, u32[]{:S(2)}, u32[]{:S(2)}) collective-permute-start(bf16[4,8,5376]{2,1,0:T(8,128)(2,1)S(1)} %pad_maximum_fusion.refs_0_), channel_id=1, source_target_pairs={{0,32},{1,9},{2,34},{3,11},{4,36},{5,13},{6,38},{7,15},{8,40},{9,1... | collective-permute-start | bytes 1032200 | tf_op jit(solution)/shard_map/ppermute | solution.py:262
  70.8 9.0 %collective-permute-start.7 = (bf16[4,8,5376]{2,1,0:T(8,128)(2,1)S(1)}, bf16[4,8,5376]{2,1,0:T(8,128)(2,1)S(1)}, u32[]{:S(2)}, u32[]{:S(2)}) collective-permute-start(bf16[4,8,5376]{2,1,0:T(8,128)(2,1)S(1)} %pad_maximum_fusion.refs_0_), channel_id=1, source_target_pairs={{0,96},{1,25},{2,98},{3,27},{4,100},{5,29},{6,102},{7,31},{8,104},... | collective-permute-start | bytes 1032200 | tf_op jit(solution)/shard_map/ppermute | solution.py:262

commit v8 on v7

--- a/solution.py
+++ b/solution.py
@@ -16,7 +16,6 @@
 QPAD = 24
 ROW_NEW = 42
 RPAD = 48
-PAIR = 88
 TURNS = (0, 2, 1, 3)
 
 beta_first = 0.9
@@ -88,15 +87,15 @@
             gout_ref[half, t] = scratch[pl.ds(offset, RPAD), :] * SCALE_G
 
 
-def owner_kernel(new_ref, rows_ref, g_ref, w_out, m_out, v_out, scratch):
+def owner_kernel(new_ref, ends_ref, mid_ref, g_ref, w_out, m_out, v_out, scratch):
     dp = lax.axis_index("y") * 4 + lax.axis_index("x")
     tp = lax.axis_index("z") * 2 + lax.axis_index("c")
     new_place = lax.rem(new_ref[1, dp * 8 + tp] - dp * UNIT, SLOT)
     length = new_ref[2, dp * 8 + tp]
-    for half in range(2):
+    for half, ref in enumerate((ends_ref, mid_ref)):
         for t in range(8):
             for s in range(3):
-                piece = rows_ref[t, pl.ds((1 - half) * ROW_NEW, ROW_NEW), pl.ds(s * LANES, LANES)]
+                piece = ref[t, pl.ds(0, ROW_NEW), pl.ds(s * LANES, LANES)]
                 at = half * UNIT + t * ROW_NEW
                 scratch[s, pl.ds(at, ROW_NEW), :] = piece
                 scratch[s, pl.ds(at + SLOT, ROW_NEW), :] = piece
@@ -140,7 +139,8 @@
     y = lax.axis_index("y")
     x = lax.axis_index("x")
     core = lax.axis_index("c")
-    t = lax.axis_index("z") * 2 + core
+    z = lax.axis_index("z")
+    t = z * 2 + core
     dp = y * 4 + x
     f16 = jnp.float16
 
@@ -209,18 +209,19 @@
     second = lax.all_to_all(
         rows.reshape(16, 2 * QPAD, 3 * LANES), ("y", "x"), 0, 0, tiled=True
     )
-    second, grad_first = lax.optimization_barrier((second, grad_first))
-    order = head_order.reshape(8, 1, 1, 14)
-    kind = jnp.arange(2, dtype=jnp.int32).reshape(1, 2, 1, 1)
-    comp = jnp.arange(3, dtype=jnp.int32).reshape(1, 1, 3, 1)
-    origin = ((order // 7) * 2 + kind) * QPAD + (order % 7) * 3 + comp
-    origin = jnp.pad(origin.reshape(8, 2 * ROW_NEW), ((0, 0), (0, PAIR - 2 * ROW_NEW)))
-    origin = origin.reshape(8 * PAIR, 1)
-    col_id = lax.broadcasted_iota(jnp.int32, (8 * PAIR, 32 * QPAD), 1)
+    second, grad_first, grad_last = lax.optimization_barrier((second, grad_first, grad_last))
+    second = second.reshape(32 * QPAD, 3 * LANES)
+    order = head_order.reshape(8, 1, 14)
+    comp = jnp.arange(3, dtype=jnp.int32).reshape(1, 3, 1)
+    origin = (order // 7) * (2 * QPAD) + (order % 7) * 3 + comp
+    origin = jnp.pad(origin.reshape(8, ROW_NEW), ((0, 0), (0, RPAD - ROW_NEW)))
+    origin = origin.reshape(8 * RPAD, 1)
+    col_id = lax.broadcasted_iota(jnp.int32, (8 * RPAD, 32 * QPAD), 1)
     moved = lax.optimization_barrier((origin == col_id).astype(jnp.bfloat16))
-    heads = one_hot_dot(moved, second.reshape(32 * QPAD, 3 * LANES))
-
-    block = lax.all_to_all(heads.reshape(8, PAIR, 3 * LANES), ("z", "c"), 0, 0, tiled=True)
+    moved_ends = lax.optimization_barrier((origin + QPAD == col_id).astype(jnp.bfloat16))
+    heads = one_hot_dot(moved, second).reshape(8, RPAD, 3 * LANES)
+
+    block = lax.all_to_all(heads, ("z", "c"), 0, 0, tiled=True)
 
     own = lax.broadcasted_iota(jnp.int32, (8, RPAD, LANES), 0) * ROW_NEW
     own = own + lax.broadcasted_iota(jnp.int32, (8, RPAD, LANES), 1)
@@ -233,7 +234,7 @@
             grad_last.astype(jnp.float32),
         ),
     ) * (1.0 / SCALE_G)
-    wide = block[:, :RPAD].astype(jnp.float32)
+    wide = block.astype(jnp.float32)
     master, _, _ = adam_update(
         wide[:, :, :LANES] * (1.0 / SCALE_W),
         wide[:, :, LANES : 2 * LANES] * (1.0 / SCALE_M),
@@ -262,7 +263,9 @@
             lax.ppermute(value, ("y", "x", "z", "c"), moves(by, first)) for by in TURNS[1:]
         ]
 
-    held = turn(jnp.stack(turn(mine, True)), False)
+    mine, second = lax.optimization_barrier((mine, second))
+    by_one = jnp.stack(turn(mine, True))
+    held = turn(by_one, False)
     params = pl.pallas_call(
         place_kernel,
         out_shape=jax.ShapeDtypeStruct((16, 8, ROW_NEW * LANES), jnp.bfloat16),
@@ -271,14 +274,27 @@
         compiler_params=pltpu.CompilerParams(vmem_limit_bytes=16 * 1024 * 1024),
     )(*held).reshape(128, ROW_NEW * LANES)
 
+    ends = one_hot_dot(moved_ends, second)
+    even = core == 0
+    ends = ends.reshape(4, 2, RPAD, 3 * LANES)
+    keep = jnp.where(even, ends[:, 0], ends[:, 1])
+    got = lax.ppermute(jnp.where(even, ends[:, 1], ends[:, 0]), "c", [(0, 1), (1, 0)])
+    both = jnp.stack([jnp.where(even, keep, got), jnp.where(even, got, keep)], axis=1)
+    from_z = [lax.dynamic_index_in_dim(both, z, 0, keepdims=False)]
+    for by in (2, 1, 3):
+        leaving = lax.dynamic_index_in_dim(both, (z + by) % 4, 0, keepdims=False)
+        from_z.append(lax.ppermute(leaving, "z", [(i, (i + by) % 4) for i in range(4)]))
+    back = [from_z[3], from_z[1], from_z[2], from_z[0]]
+    ends = lax.dynamic_slice_in_dim(jnp.stack(back + back), 3 - z, 4, 0)
+    ends = ends.reshape(8, RPAD, 3 * LANES)
     outs = pl.pallas_call(
         owner_kernel,
         out_shape=(jax.ShapeDtypeStruct((1, SLOT, LANES), jnp.float32),) * 3,
-        in_specs=[smem, vmem, vmem],
+        in_specs=[smem, vmem, vmem, vmem],
         out_specs=(vmem, vmem, vmem),
         scratch_shapes=[pltpu.VMEM((3, 2 * SLOT, LANES), jnp.float32)],
         compiler_params=pltpu.CompilerParams(vmem_limit_bytes=24 * 1024 * 1024),
-    )(new_table.T, block.astype(jnp.float32), grad)
+    )(new_table.T, ends.astype(jnp.float32), block.astype(jnp.float32), grad)
     return (*outs, params)
 
 

time: 81.8 us -> 82.4 us (level)
  starting transfers between devices: 35 us -> 33.2 us
  matrix products: 4.32 us -> 5.6 us
    ppermute x6, waiting for transfers between devices: 6.68 us -> 1.99 us  [turn(): lax.ppermute(value, ('y', 'x', 'z', 'c'), moves(by, first))]
    ppermute x0 -> x4, waiting for transfers between devices: none -> 4.59 us  [the longest x3 4.59 us: on_device(): lax.ppermute(leaving, 'z', [(i, (i + by) % 4) for i in range(4)])]
    ppermute x6, starting transfers between devices: 10.7 us -> 6.85 us  [turn(): lax.ppermute(value, ('y', 'x', 'z', 'c'), moves(by, first))]
    ppermute x0 -> x4, starting transfers between devices: none -> 3.32 us  [the longest x3 3.23 us: on_device(): lax.ppermute(leaving, 'z', [(i, (i + by) % 4) for i in range(4)])]
    ppermute x1, waiting for transfers between devices: 0.01 us -> 3.28 us  [on_device(): grad_last = lax.ppermute(grad_send[0], ('y', 'x'), up)]
    all_to_all x1, waiting for transfers between devices: 1.51 us -> 0.01 us  [on_device(): lax.all_to_all(rows.reshape(16, 2 * QPAD, 3 * LANES), ('y', 'x'), 0, 0, t...]
    ppermute x1, starting transfers between devices: 1.45 us -> 0.01 us  [on_device(): grad_last = lax.ppermute(grad_send[0], ('y', 'x'), up)]
    dot_general x2 -> x3, matrix products: 4.32 us -> 5.6 us  [one_hot_dot(): jnp.dot(chosen.astype(jnp.float32), source.astype(jnp.float32), precision...]
  transfers between devices with their start and end apart: 11 -> 15, of which waited for: 8 -> 8; matrix products, arithmetic and copies ran while one was open for 4% -> 5% of each run, Pallas kernels for 3% -> 3%
where the time goes in v8:
time: 82.4 us; the launch traced here: 81.5 us
  starting transfers between devices  33.2 us (40%)
  waiting for transfers between devices  31.1 us (38%)
  matrix products  5.6 us (7%)
  Pallas kernels  5.2 us (6%)
  other arithmetic  3.73 us (5%)
  local copies, waits for them, and re-layouts  1.61 us (2%)
  between operations  1.1 us (1%)
    all_to_all x1, starting transfers between devices, on_device(): lax.all_to_all(packed.astype(f16), ('x', 'z', 'c'), 0, 0, tiled=True)  8.49 us
    all_to_all x1, waiting for transfers between devices, on_device(): block = lax.all_to_all(heads, ('z', 'c'), 0, 0, tiled=True)  7.78 us
    all_to_all x1, waiting for transfers between devices, on_device(): lax.all_to_all(packed.astype(f16), ('x', 'z', 'c'), 0, 0, tiled=True)  7.73 us
    ppermute x6, starting transfers between devices, turn(): lax.ppermute(value, ('y', 'x', 'z', 'c'), moves(by, first))  6.85 us
    all_to_all x1, starting transfers between devices, on_device(): lax.all_to_all(rows.reshape(16, 2 * QPAD, 3 * LANES), ('y', 'x'), 0, 0, t...  5.77 us
    ppermute x1, waiting for transfers between devices, on_device(): grad_first = lax.ppermute(grad_send[0], ('y', 'x'), down)  5.75 us
    dot_general x3, matrix products, one_hot_dot(): jnp.dot(chosen.astype(jnp.float32), source.astype(jnp.float32), precision...  5.6 us
    ppermute x1, starting transfers between devices, on_device(): grad_first = lax.ppermute(grad_send[0], ('y', 'x'), down)  5.32 us
  transfers between devices with their start and end apart: 15, of which 8 were waited for; matrix products, arithmetic and copies ran while one was open for 5% of the time, Pallas kernels for 3%

profile of v8, /device:TPU:0, one launch (start us, length us, event | category | flops | bytes accessed | tf_op | source)
XLA Modules:
  0.0 81.5 jit_solution(13958824574095994928)
XLA Ops:
  0.6 1.3 %shard_map.103 = f32[32,24,384]{2,1,0:T(8,128)S(1)} custom-call(s32[3,128]{1,0:T(4,128)} %bitcast.114, f32[1,672,128]{2,1,0:T(8,128)} %w_ref.1, f32[1,672,128]{2,1,0:T(8,128)} %m_ref.1, f32[1,672,128]{2,1,0:T(8,128)} %v_ref.1), custom_call_target="tpu_custom_call" | custom-call | tf_op jit(solution)/shard_map/pallas_call | solution.py:150
  1.9 0.9 %convert_element_type.57 = f16[32,24,384]{2,1,0:T(8,128)(2,1)} convert(f32[32,24,384]{2,1,0:T(8,128)S(1)} %shard_map.103) | non-fusion elementwise | flops 294912 | bytes 1769472 | tf_op jit(solution)/shard_map/convert_element_type | solution.py:176
  2.8 8.5 %all-to-all-start = ((f16[32,24,384]{2,1,0:T(8,128)(2,1)}), f16[32,24,384]{2,1,0:T(8,128)(2,1)}, u32[]{:S(2)}, u32[]{:S(2)}) async-start(f16[32,24,384]{2,1,0:T(8,128)(2,1)} %convert_element_type.57), calls=%async_computation | async-start | bytes 1179648 | tf_op jit(solution)/shard_map/all_to_all | solution.py:176
  13.2 1.0 %fusion.2 = bf16[768,768]{1,0:T(8,128)(2,1)S(1)} fusion(s32[768]{0:T(1024)S(1)} %add.269, s32[768]{0:T(1024)S(1)} %ge.62, s32[768]{0:T(1024)S(1)} %get-tuple-element.46, s32[768]{0:T(1024)S(1)} %get-tuple-element.47, s32[768]{0:T(1024)S(1)} %reshape.314, pred[768]{0:T(1024)(128)(4,1)S(1)} %fusion.38), kind=kLoop, calls=%fused_computation.3 | loop fusion | flops 4718592 | bytes 1195776 | tf_op jit(solution)/shard_map/convert_element_type | solution.py:206
  14.6 0.6 shard_map.102
  15.4 7.7 %all-to-all-done = f16[32,24,384]{2,1,0:T(8,128)(2,1)} async-done(((f16[32,24,384]{2,1,0:T(8,128)(2,1)}), f16[32,24,384]{2,1,0:T(8,128)(2,1)}, u32[]{:S(2)}, u32[]{:S(2)}) %all-to-all-start) | async-done | bytes 589856 | tf_op jit(solution)/shard_map/all_to_all | solution.py:176
  23.1 3.3 %convolution_convert_fusion = f16[768,384]{1,0:T(8,128)(2,1)} fusion(bf16[768,768]{1,0:T(8,128)(2,1)S(1)} %fusion.2, f16[768,384]{1,0:T(8,128)(2,1)} %bitcast.5), kind=kOutput, calls=%fused_computation.4 | convolution fusion | flops 453279744 | bytes 2359296 | tf_op jit(solution)/shard_map/dot_general | solution.py:129
  26.4 5.8 %all-to-all-start.1 = ((f16[16,48,384]{2,1,0:T(8,128)(2,1)}), f16[16,48,384]{2,1,0:T(8,128)(2,1)S(1)}, u32[]{:S(2)}, u32[]{:S(2)}) async-start(f16[16,48,384]{2,1,0:T(8,128)(2,1)} %bitcast.106), calls=%async_computation.1 | async-start | bytes 1179648 | tf_op jit(solution)/shard_map/all_to_all | solution.py:209
  32.3 5.3 %collective-permute-start = (f16[8,48,128]{2,1,0:T(8,128)(2,1)S(1)}, f16[8,48,128]{2,1,0:T(8,128)(2,1)S(1)}, u32[]{:S(2)}, u32[]{:S(2)}) collective-permute-start(f16[8,48,128]{2,1,0:T(8,128)(2,1)S(1)} %slice_bitcast_fusion.3), channel_id=1, source_target_pairs={{0,120},{8,0},{16,8},{24,16},{32,24},{40,32},{48,40},{56,48},{64,5... | collective-permute-start | bytes 294920 | tf_op jit(solution)/shard_map/ppermute | solution.py:180
  37.8 5.8 %collective-permute-done = f16[8,48,128]{2,1,0:T(8,128)(2,1)S(1)} collective-permute-done((f16[8,48,128]{2,1,0:T(8,128)(2,1)S(1)}, f16[8,48,128]{2,1,0:T(8,128)(2,1)S(1)}, u32[]{:S(2)}, u32[]{:S(2)}) %collective-permute-start) | collective-permute-done | bytes 98336 | tf_op jit(solution)/shard_map/ppermute | solution.py:180
  43.5 3.3 %collective-permute-done.1 = f16[8,48,128]{2,1,0:T(8,128)(2,1)S(1)} collective-permute-done((f16[8,48,128]{2,1,0:T(8,128)(2,1)S(1)}, f16[8,48,128]{2,1,0:T(8,128)(2,1)S(1)}, u32[]{:S(2)}, u32[]{:S(2)}) %collective-permute-start.1) | collective-permute-done | bytes 98336 | tf_op jit(solution)/shard_map/ppermute | solution.py:181
  46.8 1.5 %convolution_convert_fusion.2 = f16[384,384]{1,0:T(8,128)(2,1)} fusion(bf16[384,768]{1,0:T(8,128)(2,1)S(1)} %fusion.4, f16[768,384]{1,0:T(8,128)(2,1)S(1)} %bitcast.101), kind=kOutput, calls=%fused_computation.6 | convolution fusion | flops 226639872 | bytes 1474560 | tf_op jit(solution)/shard_map/dot_general | solution.py:129
  48.3 3.4 %all-to-all-start.2 = ((f16[8,48,384]{2,1,0:T(8,128)(2,1)}), f16[8,48,384]{2,1,0:T(8,128)(2,1)S(1)}, u32[]{:S(2)}, u32[]{:S(2)}) async-start(f16[8,48,384]{2,1,0:T(8,128)(2,1)} %bitcast.9), calls=%async_computation.2 | async-start | bytes 589824 | tf_op jit(solution)/shard_map/all_to_all | solution.py:224
  51.8 7.8 %all-to-all-done.2 = f16[8,48,384]{2,1,0:T(8,128)(2,1)S(1)} async-done(((f16[8,48,384]{2,1,0:T(8,128)(2,1)}), f16[8,48,384]{2,1,0:T(8,128)(2,1)S(1)}, u32[]{:S(2)}, u32[]{:S(2)}) %all-to-all-start.2) | async-done | bytes 294944 | tf_op jit(solution)/shard_map/all_to_all | solution.py:224
  59.9 0.8 convolution_convert_fusion.1
  61.6 2.8 %collective-permute-start.8 = (bf16[8,5376]{1,0:T(8,128)(2,1)S(1)}, bf16[8,5376]{1,0:T(8,128)(2,1)S(1)}, u32[]{:S(2)}, u32[]{:S(2)}) collective-permute-start(bf16[8,5376]{1,0:T(8,128)(2,1)S(1)} %bitcast.109), channel_id=1, source_target_pairs={{0,24},{1,97},{2,26},{3,99},{4,28},{5,101},{6,30},{7,103},{8,0},{9... | collective-permute-start | bytes 258056 | tf_op jit(solution)/shard_map/ppermute | solution.py:263
  64.5 1.2 %collective-permute-start.3 = (f16[2,48,384]{2,1,0:T(8,128)(2,1)S(1)}, f16[2,48,384]{2,1,0:T(8,128)(2,1)S(1)}, u32[]{:S(2)}, u32[]{:S(2)}) collective-permute-start(f16[2,48,384]{2,1,0:T(8,128)(2,1)S(1)} %get-tuple-element.34), channel_id=1, source_target_pairs={{0,6},{2,0},{4,2},{6,4},{1,7},{3,1},{5,3},{7,5},{8,14},{10,8},{12,... | collective-permute-start | bytes 221192 | tf_op jit(solution)/shard_map/ppermute | solution.py:286
  65.7 1.4 %collective-permute-done.6 = bf16[8,5376]{1,0:T(8,128)(2,1)S(1)} collective-permute-done((bf16[8,5376]{1,0:T(8,128)(2,1)S(1)}, bf16[8,5376]{1,0:T(8,128)(2,1)S(1)}, u32[]{:S(2)}, u32[]{:S(2)}) %collective-permute-start.6) | collective-permute-done | bytes 86048 | tf_op jit(solution)/shard_map/ppermute | solution.py:263
  68.0 3.1 %collective-permute-start.11 = (bf16[4,8,5376]{2,1,0:T(8,128)(2,1)S(1)}, bf16[4,8,5376]{2,1,0:T(8,128)(2,1)S(1)}, u32[]{:S(2)}, u32[]{:S(2)}) collective-permute-start(bf16[4,8,5376]{2,1,0:T(8,128)(2,1)S(1)} %pad_maximum_fusion.refs_0_), channel_id=1, source_target_pairs={{0,96},{1,25},{2,98},{3,27},{4,100},{5,29},{6,102},{7,31},{8,104},... | collective-permute-start | bytes 1032200 | tf_op jit(solution)/shard_map/ppermute | solution.py:263
  71.7 1.6 %collective-permute-start.5 = (f16[2,48,384]{2,1,0:T(8,128)(2,1)S(1)}, f16[2,48,384]{2,1,0:T(8,128)(2,1)S(1)}, u32[]{:S(2)}, u32[]{:S(2)}) collective-permute-start(f16[2,48,384]{2,1,0:T(8,128)(2,1)S(1)} %get-tuple-element.33), channel_id=1, source_target_pairs={{0,2},{2,4},{4,6},{6,0},{1,3},{3,5},{5,7},{7,1},{8,10},{10,12},{12... | collective-permute-start | bytes 221192 | tf_op jit(solution)/shard_map/ppermute | solution.py:286
  73.3 3.9 %collective-permute-done.4 = f16[2,48,384]{2,1,0:T(8,128)(2,1)S(1)} collective-permute-done((f16[2,48,384]{2,1,0:T(8,128)(2,1)S(1)}, f16[2,48,384]{2,1,0:T(8,128)(2,1)S(1)}, u32[]{:S(2)}, u32[]{:S(2)}) %collective-permute-start.4) | collective-permute-done | bytes 73760 | tf_op jit(solution)/shard_map/ppermute | solution.py:286
  77.2 0.7 collective-permute-done.5
  78.2 2.0 %shard_map.104 = (f32[1,672,128]{2,1,0:T(8,128)}, f32[1,672,128]{2,1,0:T(8,128)}, f32[1,672,128]{2,1,0:T(8,128)}) custom-call(s32[3,128]{1,0:T(4,128)S(1)} %bitcast.100, f32[8,48,384]{2,1,0:T(8,128)S(1)} %bitcast_convert_fusion.ends_ref, f32[8,48,384]{2,1,0:T(8,128)S(1)} %convert_element_type.61.mid_ref, f32[1,672,128]{2,1,0:T(8,128)S(1)} %copy-done), custom_call_target="tpu_custom_call" | custom-call | tf_op jit(solution)/shard_map/pallas_call | solution.py:290
  80.2 1.3 %shard_map.105 = bf16[16,8,5376]{2,1,0:T(8,128)(2,1)} custom-call(bf16[4,8,5376]{2,1,0:T(8,128)(2,1)S(1)} %pad_maximum_fusion.refs_0_, bf16[4,8,5376]{2,1,0:T(8,128)(2,1)S(1)} %collective-permute-done.9.refs_1_, bf16[4,8,5376]{2,1,0:T(8,128)(2,1)S(1)} %collective-permute-done.10.refs_2_, bf16[4,8,5376]{2,1,0:T(8,128)(2,1)S(1)} %collective-permute-done.11.refs_3_), custom_call_target="tpu_custom_call" | custom-call | tf_op jit(solution)/shard_map/pallas_call | solution.py:269
  (93 shorter events, 5.6 us)
Async XLA Ops:
  1.9 9.5 %copy-start.3 = (s32[112]{0:T(128)S(1)}, s32[112]{0:T(128)}, u32[]{:S(2)}) copy-start(s32[112]{0:T(128)} %param.13) | copy-start | bytes 1348
  1.9 9.8 %copy-start.1 = (s32[128,3]{0,1:T(4,128)S(1)}, s32[128,3]{0,1:T(4,128)}, u32[]{:S(2)}) copy-start(s32[128,3]{0,1:T(4,128)} %param.12) | copy-start | bytes 4612
  2.8 9.8 %copy-start.2 = (s32[128,3]{0,1:T(4,128)S(1)}, s32[128,3]{0,1:T(4,128)}, u32[]{:S(2)}) copy-start(s32[128,3]{0,1:T(4,128)} %param.11) | copy-start | bytes 4612
  2.8 11.7 %copy-start = (f32[1,672,128]{2,1,0:T(8,128)S(1)}, f32[1,672,128]{2,1,0:T(8,128)}, u32[]{:S(2)}) copy-start(f32[1,672,128]{2,1,0:T(8,128)} %g_ref.3) | copy-start | bytes 1032196
  2.8 20.3 %all-to-all-start = ((f16[32,24,384]{2,1,0:T(8,128)(2,1)}), f16[32,24,384]{2,1,0:T(8,128)(2,1)}, u32[]{:S(2)}, u32[]{:S(2)}) async-start(f16[32,24,384]{2,1,0:T(8,128)(2,1)} %convert_element_type.57), calls=%async_computation | async-start | bytes 1179648 | tf_op jit(solution)/shard_map/all_to_all | solution.py:176
  26.4 20.4 %all-to-all-start.1 = ((f16[16,48,384]{2,1,0:T(8,128)(2,1)}), f16[16,48,384]{2,1,0:T(8,128)(2,1)S(1)}, u32[]{:S(2)}, u32[]{:S(2)}) async-start(f16[16,48,384]{2,1,0:T(8,128)(2,1)} %bitcast.106), calls=%async_computation.1 | async-start | bytes 1179648 | tf_op jit(solution)/shard_map/all_to_all | solution.py:209
  32.3 11.2 %collective-permute-start = (f16[8,48,128]{2,1,0:T(8,128)(2,1)S(1)}, f16[8,48,128]{2,1,0:T(8,128)(2,1)S(1)}, u32[]{:S(2)}, u32[]{:S(2)}) collective-permute-start(f16[8,48,128]{2,1,0:T(8,128)(2,1)S(1)} %slice_bitcast_fusion.3), channel_id=1, source_target_pairs={{0,120},{8,0},{16,8},{24,16},{32,24},{40,32},{48,40},{56,48},{64,5... | collective-permute-start | bytes 294920 | tf_op jit(solution)/shard_map/ppermute | solution.py:180
  37.6 9.2 %collective-permute-start.1 = (f16[8,48,128]{2,1,0:T(8,128)(2,1)S(1)}, f16[8,48,128]{2,1,0:T(8,128)(2,1)S(1)}, u32[]{:S(2)}, u32[]{:S(2)}) collective-permute-start(f16[8,48,128]{2,1,0:T(8,128)(2,1)S(1)} %slice_bitcast_fusion.3), channel_id=1, source_target_pairs={{0,8},{8,16},{16,24},{24,32},{32,40},{40,48},{48,56},{56,64},{64,7... | collective-permute-start | bytes 294920 | tf_op jit(solution)/shard_map/ppermute | solution.py:181
  48.3 11.2 %all-to-all-start.2 = ((f16[8,48,384]{2,1,0:T(8,128)(2,1)}), f16[8,48,384]{2,1,0:T(8,128)(2,1)S(1)}, u32[]{:S(2)}, u32[]{:S(2)}) async-start(f16[8,48,384]{2,1,0:T(8,128)(2,1)} %bitcast.9), calls=%async_computation.2 | async-start | bytes 589824 | tf_op jit(solution)/shard_map/all_to_all | solution.py:224
  60.8 3.5 %collective-permute-start.2 = (f16[4,48,384]{2,1,0:T(8,128)(2,1)S(1)}, f16[4,48,384]{2,1,0:T(8,128)(2,1)S(1)}, u32[]{:S(2)}, u32[]{:S(2)}) collective-permute-start(f16[4,48,384]{2,1,0:T(8,128)(2,1)S(1)} %select_bitcast_fusion), channel_id=1, source_target_pairs={{0,1},{1,0},{2,3},{3,2},{4,5},{5,4},{6,7},{7,6},{8,9},{9,8},{10,11... | collective-permute-start | bytes 442376 | tf_op jit(solution)/shard_map/ppermute | solution.py:281
  60.9 6.2 %collective-permute-start.6 = (bf16[8,5376]{1,0:T(8,128)(2,1)S(1)}, bf16[8,5376]{1,0:T(8,128)(2,1)S(1)}, u32[]{:S(2)}, u32[]{:S(2)}) collective-permute-start(bf16[8,5376]{1,0:T(8,128)(2,1)S(1)} %bitcast.107), channel_id=1, source_target_pairs={{0,16},{1,65},{2,18},{3,67},{4,20},{5,69},{6,22},{7,71},{8,24},{9,... | collective-permute-start | bytes 258056 | tf_op jit(solution)/shard_map/ppermute | solution.py:263
  61.0 6.7 %collective-permute-start.7 = (bf16[8,5376]{1,0:T(8,128)(2,1)S(1)}, bf16[8,5376]{1,0:T(8,128)(2,1)S(1)}, u32[]{:S(2)}, u32[]{:S(2)}) collective-permute-start(bf16[8,5376]{1,0:T(8,128)(2,1)S(1)} %bitcast.108), channel_id=1, source_target_pairs={{0,8},{1,33},{2,10},{3,35},{4,12},{5,37},{6,14},{7,39},{8,16},{9,4... | collective-permute-start | bytes 258056 | tf_op jit(solution)/shard_map/ppermute | solution.py:263
  61.6 6.2 %collective-permute-start.8 = (bf16[8,5376]{1,0:T(8,128)(2,1)S(1)}, bf16[8,5376]{1,0:T(8,128)(2,1)S(1)}, u32[]{:S(2)}, u32[]{:S(2)}) collective-permute-start(bf16[8,5376]{1,0:T(8,128)(2,1)S(1)} %bitcast.109), channel_id=1, source_target_pairs={{0,24},{1,97},{2,26},{3,99},{4,28},{5,101},{6,30},{7,103},{8,0},{9... | collective-permute-start | bytes 258056 | tf_op jit(solution)/shard_map/ppermute | solution.py:263
  64.5 7.2 %collective-permute-start.3 = (f16[2,48,384]{2,1,0:T(8,128)(2,1)S(1)}, f16[2,48,384]{2,1,0:T(8,128)(2,1)S(1)}, u32[]{:S(2)}, u32[]{:S(2)}) collective-permute-start(f16[2,48,384]{2,1,0:T(8,128)(2,1)S(1)} %get-tuple-element.34), channel_id=1, source_target_pairs={{0,6},{2,0},{4,2},{6,4},{1,7},{3,1},{5,3},{7,5},{8,14},{10,8},{12,... | collective-permute-start | bytes 221192 | tf_op jit(solution)/shard_map/ppermute | solution.py:286
  67.8 12.5 %collective-permute-start.10 = (bf16[4,8,5376]{2,1,0:T(8,128)(2,1)S(1)}, bf16[4,8,5376]{2,1,0:T(8,128)(2,1)S(1)}, u32[]{:S(2)}, u32[]{:S(2)}) collective-permute-start(bf16[4,8,5376]{2,1,0:T(8,128)(2,1)S(1)} %pad_maximum_fusion.refs_0_), channel_id=1, source_target_pairs={{0,32},{1,9},{2,34},{3,11},{4,36},{5,13},{6,38},{7,15},{8,40},{9,1... | collective-permute-start | bytes 1032200 | tf_op jit(solution)/shard_map/ppermute | solution.py:263
  68.0 12.2 %collective-permute-start.11 = (bf16[4,8,5376]{2,1,0:T(8,128)(2,1)S(1)}, bf16[4,8,5376]{2,1,0:T(8,128)(2,1)S(1)}, u32[]{:S(2)}, u32[]{:S(2)}) collective-permute-start(bf16[4,8,5376]{2,1,0:T(8,128)(2,1)S(1)} %pad_maximum_fusion.refs_0_), channel_id=1, source_target_pairs={{0,96},{1,25},{2,98},{3,27},{4,100},{5,29},{6,102},{7,31},{8,104},... | collective-permute-start | bytes 1032200 | tf_op jit(solution)/shard_map/ppermute | solution.py:263
  71.1 9.2 %collective-permute-start.9 = (bf16[4,8,5376]{2,1,0:T(8,128)(2,1)S(1)}, bf16[4,8,5376]{2,1,0:T(8,128)(2,1)S(1)}, u32[]{:S(2)}, u32[]{:S(2)}) collective-permute-start(bf16[4,8,5376]{2,1,0:T(8,128)(2,1)S(1)} %pad_maximum_fusion.refs_0_), channel_id=1, source_target_pairs={{0,64},{1,17},{2,66},{3,19},{4,68},{5,21},{6,70},{7,23},{8,72},{9,... | collective-permute-start | bytes 1032200 | tf_op jit(solution)/shard_map/ppermute | solution.py:263
  71.2 5.9 %collective-permute-start.4 = (f16[2,48,384]{2,1,0:T(8,128)(2,1)S(1)}, f16[2,48,384]{2,1,0:T(8,128)(2,1)S(1)}, u32[]{:S(2)}, u32[]{:S(2)}) collective-permute-start(f16[2,48,384]{2,1,0:T(8,128)(2,1)S(1)} %get-tuple-element.35), channel_id=1, source_target_pairs={{0,4},{2,6},{4,0},{6,2},{1,5},{3,7},{5,1},{7,3},{8,12},{10,14},{12... | collective-permute-start | bytes 221192 | tf_op jit(solution)/shard_map/ppermute | solution.py:286
  71.7 6.2 %collective-permute-start.5 = (f16[2,48,384]{2,1,0:T(8,128)(2,1)S(1)}, f16[2,48,384]{2,1,0:T(8,128)(2,1)S(1)}, u32[]{:S(2)}, u32[]{:S(2)}) collective-permute-start(f16[2,48,384]{2,1,0:T(8,128)(2,1)S(1)} %get-tuple-element.33), channel_id=1, source_target_pairs={{0,2},{2,4},{4,6},{6,0},{1,3},{3,5},{5,7},{7,1},{8,10},{10,12},{12... | collective-permute-start | bytes 221192 | tf_op jit(solution)/shard_map/ppermute | solution.py:286
